TPU v7x, 32 devices: a whole 2x2x4 slice. The times are simulated.
32 devices in a mesh: tok: 8 (over z, x), mdl: 4 (over y, core).
Axes of the slice: x: 2, y: 2, z: 4, core: 2. Of those that a mesh axis runs over, the one named last changes fastest.
Arguments:
- tok_grad: bfloat16 [16384, 2048], P('tok', 'mdl'), may hold values from -0.119628906 to 0.119628906
- occurrence: int32 [16384], P('tok'), may hold values from 0 to 1023
- owned: int32 [1024], replicated, may hold values from 0 to 1023, each once
- token_ids: int32 [1024, 8], P('tok'), may hold values from 0 to 31999, as said below
- embeds: bfloat16 [1024, 8, 2048], P('tok', None, 'mdl'), may hold values from -6 to 6
- gain: float32 [2048], replicated, may hold values from 0.5 to 1.5
- w_query: bfloat16 [2048, 2048], P(None, 'mdl'), may hold values from -0.125 to 0.125
- w_key: bfloat16 [2048, 2048], P(None, 'mdl'), may hold values from -0.125 to 0.125
- w_value: bfloat16 [2048, 2048], P(None, 'mdl'), may hold values from -0.125 to 0.125
- w_out: bfloat16 [2048, 2048], P('mdl'), may hold values from -0.125 to 0.125
Outputs:
- embed_grad: bfloat16 [1024, 8, 2048], P('tok', None, 'mdl')
- query_grad: float32 [2048, 2048], P('tok', 'mdl')
- key_grad: float32 [2048, 2048], P('tok', 'mdl')
- value_grad: float32 [2048, 2048], P('tok', 'mdl')
- out_grad: float32 [2048, 2048], P('mdl', 'tok')
Inputs may be any that keep to these rules, and one draw needn't show every extreme that they name: `token_ids`: in each row the nonzero ids come first, then zeros; every row has at least one nonzero id, and some row is full and some has one token.
All inputs are finite; a program needn't handle non-finite values.
Results may differ from a plain program's by a relative error of at most 0.01.
Values may be sent and summed in bfloat16 or wider, within the bound.
No kernel may reach another device: no remote copies, remote signals or barrier semaphores. Data moves between devices by JAX's collectives and lax.ppermute only.
A program may use at most 128 MiB of HBM per device.

v0:
```python
import jax
import jax.numpy as jnp
from jax import lax
from jax.sharding import PartitionSpec as P

HEAD = 128


def tdot(left, right):
    return lax.dot_general(
        left, right, (((0,), (0,)), ((), ())), preferred_element_type=jnp.float32
    )


def rdot(left, right):
    return lax.dot_general(
        left, right, (((1,), (1,)), ((), ())), preferred_element_type=jnp.float32
    )


def on_device(tok_grad, occurrence, owned, token_ids, embeds, gain, w_query, w_key, w_value, w_out):
    f32 = jnp.float32
    bf16 = jnp.bfloat16
    n_tok = lax.axis_size("tok")
    fgrams = owned.shape[0]
    f_dev = fgrams // n_tok
    width = gain.shape[0]
    cols = w_key.shape[1]
    local_heads = cols // HEAD
    flen = token_ids.shape[1]
    scale = 1.0 / HEAD**0.5
    rank = jnp.zeros((fgrams,), jnp.int32).at[owned].set(jnp.arange(fgrams, dtype=jnp.int32))
    target = rank[occurrence]
    onehot = (target[None, :] == jnp.arange(fgrams, dtype=jnp.int32)[:, None]).astype(bf16)
    partial_sums = jnp.dot(onehot, tok_grad, preferred_element_type=f32)
    blocks = partial_sums.reshape(n_tok, f_dev, tok_grad.shape[1])
    arrived = lax.all_to_all(blocks, "tok", split_axis=0, concat_axis=0, tiled=True)
    fgram_sum = jnp.sum(arrived, axis=0)
    fgram_grad = fgram_sum.astype(bf16)
    full_grad = lax.all_gather(fgram_grad, "mdl", axis=1, tiled=True)
    whole_embeds = lax.all_gather(embeds, "mdl", axis=2, tiled=True)
    length = jnp.sum((token_ids != 0).astype(jnp.int32), axis=1)
    positions = jnp.arange(flen, dtype=jnp.int32)
    lastmask = positions[None, :] == (length - 1)[:, None]
    keymask = (positions[None, :] < length[:, None]).astype(f32)
    xfull = whole_embeds.astype(f32)
    recip = lax.rsqrt(jnp.mean(xfull * xfull, axis=-1) + 1e-06)
    normed = (xfull * recip[..., None] * gain).astype(bf16)
    normed_last = jnp.sum(jnp.where(lastmask[..., None], normed.astype(f32), 0.0), axis=1).astype(
        bf16
    )
    rows = normed.reshape(f_dev * flen, width)
    keys = (
        jnp.dot(rows, w_key, preferred_element_type=f32)
        .astype(bf16)
        .reshape(f_dev, flen, local_heads, HEAD)
    )
    values = (
        jnp.dot(rows, w_value, preferred_element_type=f32)
        .astype(bf16)
        .reshape(f_dev, flen, local_heads, HEAD)
    )
    query = (
        jnp.dot(normed_last, w_query, preferred_element_type=f32)
        .astype(bf16)
        .reshape(f_dev, local_heads, HEAD)
    )
    keys32 = keys.astype(f32)
    values32 = values.astype(f32)
    query32 = query.astype(f32)
    scores = jnp.einsum("fhd,fjhd->fhj", query, keys, preferred_element_type=f32) * scale
    expo = jnp.exp(scores) * keymask[:, None, :]
    probs = expo / jnp.sum(expo, axis=-1, keepdims=True)
    probs_b = probs.astype(bf16)
    attended = (
        jnp.einsum("fhj,fjhd->fhd", probs_b, values, preferred_element_type=f32)
        .astype(bf16)
        .reshape(f_dev, cols)
    )
    d_att = rdot(full_grad, w_out).reshape(f_dev, local_heads, HEAD)
    d_prob = jnp.einsum("fhd,fjhd->fhj", d_att, values32)
    d_score = probs * (d_prob - jnp.sum(probs * d_prob, axis=-1, keepdims=True)) * scale
    d_query = jnp.einsum("fhj,fjhd->fhd", d_score, keys32).astype(bf16).reshape(f_dev, cols)
    d_key = jnp.einsum("fhj,fhd->fjhd", d_score, query32).astype(bf16).reshape(f_dev * flen, cols)
    d_value = (
        jnp.einsum("fhj,fhd->fjhd", probs_b.astype(f32), d_att)
        .astype(bf16)
        .reshape(f_dev * flen, cols)
    )
    d_normed = (rdot(d_key, w_key) + rdot(d_value, w_value)).reshape(f_dev, flen, width)
    from_query = rdot(d_query, w_query)
    d_normed = d_normed + jnp.where(lastmask[..., None], from_query[:, None, :], 0.0)
    feat_start = lax.axis_index("mdl") * embeds.shape[2]
    summed = lax.psum(d_normed, "mdl")
    scaled = summed * gain
    product = jnp.mean(xfull * scaled, axis=-1)
    result_full = recip[..., None] * scaled - xfull * (recip**3 * product)[..., None]
    result = lax.dynamic_slice_in_dim(result_full, feat_start, embeds.shape[2], 2)
    result = result + jnp.where(lastmask[..., None], fgram_grad.astype(f32)[:, None, :], 0.0)
    embed_grad = result.astype(bf16)
    query_part = tdot(normed_last, d_query)
    key_part = tdot(rows, d_key)
    value_part = tdot(rows, d_value)
    out_part = tdot(attended, full_grad)
    query_grad, key_grad, value_grad = (
        lax.psum_scatter(query_part, "tok", scatter_dimension=0, tiled=True),
        lax.psum_scatter(key_part, "tok", scatter_dimension=0, tiled=True),
        lax.psum_scatter(value_part, "tok", scatter_dimension=0, tiled=True),
    )
    out_grad = lax.psum_scatter(out_part, "tok", scatter_dimension=1, tiled=True)
    return (embed_grad, query_grad, key_grad, value_grad, out_grad)


def solution(mesh):
    return jax.shard_map(
        on_device,
        mesh=mesh,
        in_specs=(
            P("tok", "mdl"),
            P("tok"),
            P(),
            P("tok", None),
            P("tok", None, "mdl"),
            P(),
            P(None, "mdl"),
            P(None, "mdl"),
            P(None, "mdl"),
            P("mdl", None),
        ),
        out_specs=(
            P("tok", None, "mdl"),
            P("tok", "mdl"),
            P("tok", "mdl"),
            P("tok", "mdl"),
            P("mdl", "tok"),
        ),
        check_vma=False,
    )
```

profile of v0, /device:TPU:0, one launch (start us, length us, event | category | flops | bytes accessed | tf_op | source)
XLA Modules:
  0.0 656.2 jit_solution(7342512595303779714)
XLA Ops:
  7.2 0.7 all-gather.2.cloned.1.call-update
  7.9 0.7 compare_select_fusion.1
  8.6 4.3 scatter_custom_fusion
  12.9 0.7 fusion.64
  13.6 8.6 %gather_fusion = s32[2048]{0:T(1024)S(1)} fusion(s32[1024]{0:T(1024)S(1)} %scatter_custom_fusion, s32[2048]{0:T(1024)S(1)} %fusion.64), kind=kCustom, calls=%fused_computation | custom fusion | bytes 24576 | tf_op jit(solution)/shard_map/gather | solution.py:33
  22.2 5.2 fusion.2
  27.5 7.4 %all-to-all-start = ((f32[8,128,512]{2,1,0:T(8,128)}), f32[8,128,512]{2,1,0:T(8,128)}, u32[]{:S(2)}, u32[]{:S(2)}) async-start(f32[8,128,512]{2,1,0:T(8,128)} %bitcast.80), calls=%async_computation | async-start | bytes 4194304 | tf_op jit(solution)/shard_map/all_to_all | solution.py:37
  35.1 48.1 %all-to-all-done = f32[8,128,512]{2,1,0:T(8,128)} async-done(((f32[8,128,512]{2,1,0:T(8,128)}), f32[8,128,512]{2,1,0:T(8,128)}, u32[]{:S(2)}, u32[]{:S(2)}) %all-to-all-start) | async-done | bytes 2097184 | tf_op jit(solution)/shard_map/all_to_all | solution.py:37
  83.2 1.8 reduce_sum.67
  85.0 7.2 %all_gather.7 = bf16[128,2048]{1,0:T(8,128)(2,1)S(1)} all-gather(bf16[128,512]{1,0:T(8,128)(2,1)S(1)} %reduce_sum.67), channel_id=1, replica_groups=mesh['tok'=8,'mdl'=4] {'mdl'}, dimensions={1}, use_global_device_ids=true | all-gather | bytes 655360 | tf_op jit(solution)/shard_map/all_gather | solution.py:40
  92.2 2.4 fusion.70
  94.7 0.8 reshape.110
  95.5 0.8 reshape.137
  96.3 3.1 multiply_reduce_fusion.1
  99.5 0.5 copy-done.17
  100.0 5.2 select_reduce_fusion
  105.2 0.5 convolution_convert_fusion
  105.7 0.7 reshape.106
  106.4 0.8 reshape.144
  107.2 0.9 convert.6
  108.1 4.7 fusion.24
  112.9 0.7 fusion.69
  113.6 0.2 fusion.27
  113.8 0.7 convert_bitcast_fusion
  114.6 0.6 copy-done.2
  115.1 2.4 fusion.21
  117.6 0.7 fusion.71
  118.2 0.2 fusion.30
  118.5 0.7 fusion.72
  119.2 0.4 copy-done.4
  119.6 0.8 fusion.57
  120.4 2.4 fusion.33
  122.9 5.3 bitcast_add_fusion
  128.2 0.3 reduce-scatter.5.cloned.1.call-start
  128.5 2.6 fusion.46
  131.2 0.7 fusion.49
  132.0 2.8 fusion.53
  134.9 6.8 %fusion.5 = f32[2048,512]{1,0:T(8,128)} fusion(f32[128,4,8]{2,1,0:T(4,128)S(1)} %copy-done.11, f32[128,4,128]{2,1,0:T(4,128)S(1)} %copy-done.13, bf16[128,8,2048]{2,1,0:T(8,128)(2,1)} %all-gather.2.cloned.1.call-done, f32[2048]{0:T(1024)S(1)} %copy-done.21, f32[128,8]{1,0:T(8,128)S(1)} %copy.18), kind=kOutput, calls=%fused_computation.13 | convolution fusion | flops 2156920832 | bytes 8679424 | tf_op jit(solution)/shard_map/dot_general | solution.py:10
  141.8 0.9 copy-done.7
  142.7 6.8 %fusion.3 = f32[2048,512]{1,0:T(8,128)} fusion(f32[128,4,8]{2,1,0:T(4,128)S(1)} %copy-done.9, f32[128,4,128]{2,1,0:T(4,128)S(1)} %copy-done.7, bf16[128,8,2048]{2,1,0:T(8,128)(2,1)} %all-gather.2.cloned.1.call-done, f32[2048]{0:T(1024)S(1)} %copy-done.21, f32[128,8]{1,0:T(8,128)S(1)} %copy.18), kind=kOutput, calls=%fused_computation.11 | convolution fusion | flops 2156920832 | bytes 8679424 | tf_op jit(solution)/shard_map/dot_general | solution.py:10
  149.6 6.5 convert_element_type.74
  156.2 123.9 %all-reduce.2.cloned.1.call-done = f32[128,8,2048]{2,1,0:T(8,128)} async-done(((f32[128,8,2048]{2,1,0:T(8,128)}), f32[128,8,2048]{2,1,0:T(8,128)}) %all-reduce.2.cloned.1.call-update) | async-done | bytes 8388624 | tf_op jit(solution)/shard_map/psum | solution.py:94
  280.1 9.1 %multiply_reduce_fusion = (f32[128,8]{1,0:T(8,128)S(1)}, f32[128,8,2048]{2,1,0:T(8,128)}) fusion(bf16[128,8,2048]{2,1,0:T(8,128)(2,1)} %all-gather.2.cloned.1.call-done, f32[128,8,2048]{2,1,0:T(8,128)} %all-reduce.2.cloned.1.call-done, f32[2048]{0:T(1024)S(1)} %copy-done.21), kind=kLoop, calls=%fused_computation.5 | loop fusion | flops 8387584 | bytes 20983808 | tf_op jit(solution)/shard_map/reduce_sum | solution.py:96
  289.4 3.3 fusion.14
  292.7 79.8 %reduce-scatter.5.cloned.1.call-done = f32[256,512]{1,0:T(8,128)} async-done(((f32[2048,512]{1,0:T(8,128)}), f32[256,512]{1,0:T(8,128)}) %reduce-scatter.5.cloned.1.call-update) | async-done | bytes 524304 | tf_op jit(solution)/shard_map/reduce_scatter | solution.py:106
  372.5 92.8 %reduce-scatter.11.cloned.1.call-done = f32[512,256]{1,0:T(8,128)} async-done(((f32[512,2048]{1,0:T(8,128)}), f32[512,256]{1,0:T(8,128)}) %reduce-scatter.11.cloned.1.call-update) | async-done | bytes 524304 | tf_op jit(solution)/shard_map/reduce_scatter | solution.py:110
  465.3 91.9 %reduce-scatter.7.cloned.1.call-done = f32[256,512]{1,0:T(8,128)} async-done(((f32[2048,512]{1,0:T(8,128)}), f32[256,512]{1,0:T(8,128)}) %reduce-scatter.7.cloned.1.call-update) | async-done | bytes 524304 | tf_op jit(solution)/shard_map/reduce_scatter | solution.py:107
  557.2 92.2 %reduce-scatter.9.cloned.1.call-done = f32[256,512]{1,0:T(8,128)} async-done(((f32[2048,512]{1,0:T(8,128)}), f32[256,512]{1,0:T(8,128)}) %reduce-scatter.9.cloned.1.call-update) | async-done | bytes 524304 | tf_op jit(solution)/shard_map/reduce_scatter | solution.py:108
  (71 shorter events, 1.1 us)
Async XLA Ops:
  7.2 100.9 %copy-start = (bf16[2048,512]{1,0:T(8,128)(2,1)S(1)}, bf16[2048,512]{1,0:T(8,128)(2,1)}, u32[]{:S(2)}) copy-start(bf16[2048,512]{1,0:T(8,128)(2,1)} %param.17) | copy-start | bytes 6291460
  7.2 89.1 %all-gather.2.cloned.1.call-start = ((), (), s32[]{:S(2)}) async-start(), calls=%async_computation.5 | async-start | bytes 5242880 | tf_op jit(solution)/shard_map/all_gather | solution.py:41
  27.5 7.4 %copy-start.22 = (s32[128,8]{0,1:T(8,128)S(1)}, s32[128,8]{0,1:T(8,128)}, u32[]{:S(2)}) copy-start(s32[128,8]{0,1:T(8,128)} %param.13) | copy-start | bytes 12292
  27.5 55.7 %all-to-all-start = ((f32[8,128,512]{2,1,0:T(8,128)}), f32[8,128,512]{2,1,0:T(8,128)}, u32[]{:S(2)}, u32[]{:S(2)}) async-start(f32[8,128,512]{2,1,0:T(8,128)} %bitcast.80), calls=%async_computation | async-start | bytes 4194304 | tf_op jit(solution)/shard_map/all_to_all | solution.py:37
  34.8 245.2 %all-reduce.2.cloned.1.call-start = ((), (), s32[]{:S(2)}) async-start(), calls=%async_computation.6 | async-start | bytes 16777216 | tf_op jit(solution)/shard_map/psum | solution.py:94
  92.2 7.8 %copy-start.19 = (f32[2048]{0:T(1024)S(1)}, f32[2048]{0:T(1024)}, u32[]{:S(2)}) copy-start(f32[2048]{0:T(1024)} %param.15) | copy-start | bytes 24580
  99.4 0.6 copy-start.17
  100.0 5.2 copy-start.3
  108.1 12.3 %copy-start.12 = (f32[128,4,128]{2,1,0:T(4,128)}, f32[128,4,128]{2,1,0:T(4,128)S(1)}, u32[]{:S(2)}) copy-start(f32[128,4,128]{2,1,0:T(4,128)S(1)} %convert.6) | copy-start | bytes 786436
  108.1 4.8 copy-start.14
  108.1 6.4 copy-start.5
  112.9 2.2 copy-start.2
  112.9 2.2 copy-start.20
  115.1 7.7 %copy-start.8 = (f32[128,4,8]{2,1,0:T(4,128)}, f32[128,4,8]{2,1,0:T(4,128)S(1)}, u32[]{:S(2)}) copy-start(f32[128,4,8]{2,1,0:T(4,128)S(1)} %get-tuple-element.8) | copy-start | bytes 49156
  115.1 2.4 copy-start.15
  117.5 2.9 copy-start.23
  117.5 2.1 copy-start.4
  118.5 4.4 copy-start.10
  120.4 2.4 copy-start.6
  128.2 3.0 copy-start.16
  128.2 3.0 copy-start.24
  128.2 244.3 %reduce-scatter.5.cloned.1.call-start = ((), (), s32[]{:S(2)}) async-start(), calls=%async_computation.7 | async-start | bytes 4718592 | tf_op jit(solution)/shard_map/reduce_scatter | solution.py:106
  131.1 334.2 %reduce-scatter.11.cloned.1.call-start = ((), (), s32[]{:S(2)}) async-start(), calls=%async_computation.10 | async-start | bytes 4718592 | tf_op jit(solution)/shard_map/reduce_scatter | solution.py:110
  132.0 2.9 copy-start.11
  132.0 2.9 copy-start.13
  132.0 2.9 copy-start.21
  134.8 422.4 %reduce-scatter.7.cloned.1.call-start = ((), (), s32[]{:S(2)}) async-start(), calls=%async_computation.8 | async-start | bytes 4718592 | tf_op jit(solution)/shard_map/reduce_scatter | solution.py:107
  141.7 1.0 copy-start.7
  141.7 1.0 copy-start.9
  141.7 507.7 %reduce-scatter.9.cloned.1.call-start = ((), (), s32[]{:S(2)}) async-start(), calls=%async_computation.9 | async-start | bytes 4718592 | tf_op jit(solution)/shard_map/reduce_scatter | solution.py:108
  156.2 133.1 %copy-start.18 = (f32[128,8]{0,1:T(8,128)S(1)}, f32[128,8]{0,1:T(8,128)}, u32[]{:S(2)}) copy-start(f32[128,8]{0,1:T(8,128)} %copy-done.17) | copy-start | bytes 12292
  280.1 369.3 %copy-start.1 = (bf16[2048,512]{1,0:T(8,128)(2,1)S(1)}, bf16[2048,512]{1,0:T(8,128)(2,1)}, u32[]{:S(2)}) copy-start(bf16[2048,512]{1,0:T(8,128)(2,1)} %param.17) | copy-start | bytes 6291460
Sparse Core Ops, SparseCore 0:
  9.6 37.1 all-gather.1
  128.3 151.7 all-reduce.1
  284.3 88.1 reduce-scatter.4
  377.0 88.2 reduce-scatter.10
  469.3 87.7 reduce-scatter.6
  561.7 87.6 reduce-scatter.8
where the time goes:
time: 657 us; the launch traced here: 656 us
  waiting for transfers between devices  529 us (81%)
  matrix products  45.6 us (7%)
  other arithmetic  32.9 us (5%)
  local copies, waits for them, and re-layouts  18.8 us (3%)
  between operations  14.5 us (2%)
  starting transfers between devices  7.85 us (1%)
  blocking collectives  7.2 us (1%)
    psum x1, waiting for transfers between devices, on_device(): summed = lax.psum(d_normed, 'mdl')  124 us
    reduce_scatter x1, waiting for transfers between devices, on_device(): lax.psum_scatter(out_part, 'tok', scatter_dimension=1, tiled=True)  92.8 us
    reduce_scatter x1, waiting for transfers between devices, on_device(): lax.psum_scatter(value_part, 'tok', scatter_dimension=0, tiled=True)  92.2 us
    reduce_scatter x1, waiting for transfers between devices, on_device(): lax.psum_scatter(key_part, 'tok', scatter_dimension=0, tiled=True)  91.9 us
    reduce_scatter x1, waiting for transfers between devices, on_device(): lax.psum_scatter(query_part, 'tok', scatter_dimension=0, tiled=True)  79.8 us
    all_to_all x1, waiting for transfers between devices, on_device(): lax.all_to_all(blocks, 'tok', split_axis=0, concat_axis=0, tiled=True)  48.1 us
    dot_general x4, matrix products, tdot(): lax.dot_general(left, right, (((0,), (0,)), ((), ())), preferred_element_...  19.1 us
  transfers between devices with their start and end apart: 7, of which 6 were waited for; matrix products, arithmetic and copies ran while one was open for 10% of the time, Pallas kernels for 0%

commit v1 on v0

v1 whole, which is shorter than its diff:
```python
import functools

import jax
import jax.numpy as jnp
from jax import lax
from jax.experimental import pallas as pl
from jax.experimental.pallas import tpu as pltpu
from jax.sharding import PartitionSpec as P

HEAD = 128
BF = jnp.bfloat16
F32 = jnp.float32
VMEM = pl.BlockSpec(memory_space=pltpu.VMEM)
SMEM = pl.BlockSpec(memory_space=pltpu.SMEM)
LIMIT = 56 * 2**20


def dot(left, right):
    return jnp.dot(left, right, preferred_element_type=F32)


def tdot(left, right):
    return lax.dot_general(left, right, (((0,), (0,)), ((), ())), preferred_element_type=F32)


def rdot(left, right):
    return lax.dot_general(left, right, (((1,), (1,)), ((), ())), preferred_element_type=F32)


def call(body, ins, outs, scratch=(), smem=1, flops=0):
    return pl.pallas_call(
        body,
        in_specs=[SMEM] * smem + [VMEM] * (len(ins) - smem),
        out_specs=[VMEM] * len(outs),
        out_shape=[jax.ShapeDtypeStruct(s, t) for s, t in outs],
        scratch_shapes=list(scratch),
        compiler_params=pltpu.CompilerParams(vmem_limit_bytes=LIMIT),
    )(*ins)


def sums_kernel(idx, owned, occ, grads, out):
    onehot = jnp.where(owned[...] == occ[...], 1.0, 0.0).astype(BF)
    out[...] = dot(onehot, grads[...]).astype(out.dtype)


def partial_sums(idx, owned, occ, grads, n_out, f_dev, other, dtype):
    tokens, cols = grads.shape

    def owner(k, idx):
        z, x = idx[1], idx[2]
        side = 1 - x if other else x
        return lax.rem(z + k, n_out) * 2 + side

    return pl.pallas_call(
        sums_kernel,
        grid_spec=pltpu.PrefetchScalarGridSpec(
            num_scalar_prefetch=1,
            grid=(n_out,),
            in_specs=[
                pl.BlockSpec((f_dev, 1), lambda k, idx: (owner(k, idx), 0)),
                pl.BlockSpec((1, tokens), lambda k, idx: (0, 0)),
                pl.BlockSpec((tokens, cols), lambda k, idx: (0, 0)),
            ],
            out_specs=pl.BlockSpec((f_dev, cols), lambda k, idx: (k, 0)),
        ),
        out_shape=jax.ShapeDtypeStruct((n_out * f_dev, cols), dtype),
        compiler_params=pltpu.CompilerParams(vmem_limit_bytes=LIMIT),
    )(idx, owned, occ, grads)


def norm_kernel(near, idx, x0, x1, x2, x3, gain, normed, recip, *sends):
    m, z, x = idx[0], idx[1], idx[2]
    blocks = (x0, x1, x2, x3)
    rows, cols = x0.shape
    width = 4 * cols
    tile = 128

    def step(i, carry):
        at = pl.ds(pl.multiple_of(i * tile, tile), tile)
        total = jnp.zeros((tile, 1), F32)
        for block in blocks:
            part = block[at, :].astype(F32)
            total = total + jnp.sum(part * part, axis=1, keepdims=True)
        r = lax.rsqrt(total * (1.0 / width) + 1e-06)
        recip[at, :] = r
        for k, block in enumerate(blocks):
            lanes = pl.ds(pl.multiple_of((m ^ k) * cols, cols), cols)
            normed[at, lanes] = (block[at, :].astype(F32) * r * gain[:, lanes]).astype(BF)
        return carry

    lax.fori_loop(0, rows // tile, step, 0)
    if near:
        quarter = rows // 2
        feats = cols // 2
        at = pl.ds(pl.multiple_of((m & 1) * quarter, quarter), quarter)
        for kz, send in enumerate(sends):
            for kx in range(2):
                block = lax.rem(z + kz, 4) * 2 + (x ^ kx)
                send[kx] = normed[at, pl.ds(pl.multiple_of(block * feats, feats), feats)]


def diagonal(f_quarter, flen):
    rows = lax.broadcasted_iota(jnp.int32, (f_quarter, f_quarter * flen), 0)
    lanes = lax.broadcasted_iota(jnp.int32, (f_quarter, f_quarter * flen), 1)
    return rows == lanes // flen


def fold(which, lanes, flen):
    rows = lax.broadcasted_iota(jnp.int32, (lanes, 128), 0)
    to = lax.broadcasted_iota(jnp.int32, (lanes, 128), 1)
    return jnp.where(to == lax.rem(rows, flen) + which * flen, 1.0, 0.0).astype(BF)


def forward_kernel(flen, idx, near, far, w_query, w_key, w_value, kmask, lmask,
                   early, probs, raw, upro, last, mixed):
    m = idx[0]
    half = 2 * (m >> 1)
    cols = w_key.shape[1]
    heads = cols // HEAD
    rows = near.shape[0] // 2
    fq = rows // flen
    scale = 1.0 / HEAD**0.5
    diag = diagonal(fq, flen)

    def quarter(i):
        return (near, far)[i // 2].at[pl.ds((i % 2) * rows, rows), :]

    for i in range(4):
        select = jnp.where(diag, lmask[i ^ half], 0.0).astype(BF)
        last[pl.ds(i * fq, fq), :] = dot(select, quarter(i)[...]).astype(BF)
    query = dot(last[...], w_query[...]).astype(BF)
    for h in range(heads):
        at = slice(h * HEAD, (h + 1) * HEAD)
        up = rdot(query[:, at], w_key[:, at]).astype(BF)
        for i in range(4):
            upro[i, pl.ds(h * fq, fq), :] = up[i * fq:(i + 1) * fq, :]
    for i in range(4):
        a = i ^ half
        to = pl.ds(pl.multiple_of(a * fq, fq), fq)
        normed = quarter(i)[...]
        score = rdot(upro[i], normed)
        mask = jnp.concatenate([jnp.where(diag, kmask[a], 0.0)] * heads, axis=0) > 0.0
        expo = jnp.where(mask, jnp.exp(score * scale), 0.0)
        prob = expo / jnp.sum(expo, axis=1, keepdims=True)
        raw[i] = score
        probs[i] = prob
        prob_b = prob.astype(BF)
        mix = dot(prob_b, normed).astype(BF)
        select = jnp.where(diag, lmask[a], 0.0).astype(BF)
        coef = dot(select, fold(2 * heads, rows, flen))
        for h in range(heads):
            mixed[h, pl.ds(i * fq, fq), :] = mix[h * fq:(h + 1) * fq, :]
            coef = coef + dot(prob_b[h * fq:(h + 1) * fq, :], fold(h, rows, flen))
        early[to, 0:cols] = query[i * fq:(i + 1) * fq, :]
        early[to, 2 * cols:2 * cols + 128] = coef.astype(BF)
    for h in range(heads):
        at = slice(h * HEAD, (h + 1) * HEAD)
        attended = dot(mixed[h], w_value[:, at]).astype(BF)
        for i in range(4):
            to = pl.ds(pl.multiple_of((i ^ half) * fq, fq), fq)
            early[to, cols + h * HEAD:cols + (h + 1) * HEAD] = attended[i * fq:(i + 1) * fq, :]


def backward_kernel(flen, idx, near, far, w_query, w_key, w_value, w_out, lmask,
                    g0, g1, g2, g3, early, probs, raw, upro,
                    late, product, d0, d1, d2, d3, tpro, vpro, mixed, dscore):
    m = idx[0]
    half = 2 * (m >> 1)
    cols = w_key.shape[1]
    heads = cols // HEAD
    rows = near.shape[0] // 2
    fq = rows // flen
    scale = 1.0 / HEAD**0.5
    diag = diagonal(fq, flen)

    def quarter(i):
        return (near, far)[i // 2].at[pl.ds((i % 2) * rows, rows), :]

    def here(i):
        return pl.ds(pl.multiple_of((i ^ half) * fq, fq), fq)

    d_att = jnp.zeros((4 * fq, cols), F32)
    for k, block in enumerate((g0, g1, g2, g3)):
        lanes = pl.ds(pl.multiple_of((m ^ k) * cols, cols), cols)
        grads = jnp.concatenate([block[here(i), :] for i in range(4)], axis=0)
        d_att = d_att + rdot(grads, w_out[:, lanes])
    d_att = d_att.astype(BF)
    for i in range(4):
        late[here(i), 0:cols] = d_att[i * fq:(i + 1) * fq, :]
    for h in range(heads):
        at = slice(h * HEAD, (h + 1) * HEAD)
        up = rdot(d_att[:, at], w_value[:, at]).astype(BF)
        for i in range(4):
            tpro[i, pl.ds(h * fq, fq), :] = up[i * fq:(i + 1) * fq, :]
    prods = []
    for i in range(4):
        normed = quarter(i)[...]
        d_prob = rdot(tpro[i], normed)
        prob = probs[i]
        d_score = prob * (d_prob - jnp.sum(prob * d_prob, axis=1, keepdims=True)) * scale
        score_b = d_score.astype(BF)
        prob_b = prob.astype(BF)
        dscore[i] = score_b
        prods.append(jnp.sum(d_score * raw[i] + prob_b.astype(F32) * d_prob, axis=0, keepdims=True))
        mix = dot(score_b, normed).astype(BF)
        coef = jnp.zeros((fq, 128), F32)
        for h in range(heads):
            mixed[h, pl.ds(i * fq, fq), :] = mix[h * fq:(h + 1) * fq, :]
            coef = coef + dot(score_b[h * fq:(h + 1) * fq, :], fold(heads + h, rows, flen))
        late[here(i), 2 * cols:2 * cols + 128] = coef.astype(BF)
    parts = []
    for h in range(heads):
        at = slice(h * HEAD, (h + 1) * HEAD)
        parts.append(dot(mixed[h], w_key[:, at]))
    d_query = jnp.concatenate(parts, axis=1).astype(BF)
    vpro[...] = rdot(d_query, w_query[...]).astype(BF)
    for i in range(4):
        dq = d_query[i * fq:(i + 1) * fq, :]
        late[here(i), cols:2 * cols] = dq
        query = early[here(i), 0:cols]
        inner = jnp.sum(query.astype(F32) * dq.astype(F32), axis=1, keepdims=True)
        select = jnp.where(diag, lmask[i ^ half], 0.0)
        product[pl.ds(i ^ half, 1), :] = prods[i] + jnp.sum(select * inner, axis=0, keepdims=True)
        to = pl.ds(pl.multiple_of((i ^ half) * rows, rows), rows)
        prob_b = probs[i].astype(BF)
        select = select.astype(BF)
        for k, out in enumerate((d0, d1, d2, d3)):
            lanes = pl.ds(pl.multiple_of((m ^ k) * cols, cols), cols)
            total = tdot(dscore[i], upro[i, :, lanes]) + tdot(prob_b, tpro[i, :, lanes])
            total = total + tdot(select, vpro[pl.ds(i * fq, fq), lanes])
            out[to, :] = total.astype(BF)


def weights_kernel(flen, n_src, idx, b0, b1, b2, b3, f0, f1, f2, f3, *refs):
    early, late = refs[:n_src], refs[n_src:2 * n_src]
    query_grad, key_grad, value_grad, out_grad = refs[2 * n_src:2 * n_src + 4]
    z_all, q_all, a_all, da_all, dq_all = refs[2 * n_src + 4:]
    m = idx[0]
    rows, feats = b0.shape[1:]
    fq = rows // flen
    cols = key_grad.shape[1]
    heads = cols // HEAD
    parts = 2 * heads + 1
    diag = jnp.where(diagonal(fq, flen), 1.0, 0.0)
    spread = jnp.concatenate([fold(p, rows, flen).T for p in range(parts)], axis=1)
    for out in (query_grad, key_grad, value_grad, out_grad):
        out[...] = jnp.zeros_like(out)
    for k, (normed, grads) in enumerate(zip((b0, b1, b2, b3), (f0, f1, f2, f3))):
        at = pl.ds(pl.multiple_of((m ^ k) * fq, fq), fq)
        for s in range(n_src):
            to = pl.ds(s * fq, fq)
            coef = early[s][at, 2 * cols:2 * cols + 128] + late[s][at, 2 * cols:2 * cols + 128]
            wide = dot(coef, spread)
            left = jnp.concatenate(
                [(wide[:, p * rows:(p + 1) * rows] * diag).astype(BF) for p in range(parts)], axis=0
            )
            mix = dot(left, normed[s]).astype(BF)
            for p in range(parts):
                z_all[p, to, :] = mix[p * fq:(p + 1) * fq, :]
            q_all[to, :] = early[s][at, 0:cols]
            a_all[to, :] = early[s][at, cols:2 * cols]
            da_all[to, :] = late[s][at, 0:cols]
            dq_all[to, :] = late[s][at, cols:2 * cols]
        for h in range(heads):
            lanes = slice(h * HEAD, (h + 1) * HEAD)
            key_grad[:, lanes] += tdot(z_all[heads + h], q_all[:, lanes])
            value_grad[:, lanes] += tdot(z_all[h], da_all[:, lanes])
        query_grad[...] += tdot(z_all[2 * heads], dq_all[...])
        out_grad[...] += tdot(a_all[...], grads[...].reshape(n_src * fq, feats))


def on_device(tok_grad, occurrence, owned, token_ids, embeds, gain, w_query, w_key, w_value, w_out):
    n_tok = lax.axis_size("tok")
    n_out = n_tok // 2
    f_dev, flen = token_ids.shape
    width = gain.shape[0]
    cols = w_key.shape[1]
    rows = f_dev * flen
    feats = width // n_tok
    fq = f_dev // 4
    quarter = fq * flen
    m = lax.axis_index("mdl")
    t = lax.axis_index("tok")
    z, x = t // 2, t % 2
    idx = jnp.stack([m, z, x, t]).astype(jnp.int32)

    def flip(array, bit):
        return lax.ppermute(array, "mdl", [(i, i ^ bit) for i in range(4)])

    def swap(array):
        return lax.ppermute(array, "tok", [(i, i ^ 1) for i in range(n_tok)])

    def shift(array, k):
        pairs = [(i, (i + 2 * k) % n_tok) for i in range(n_tok)]
        return lax.ppermute(array, "tok", pairs)

    owned_col = owned.reshape(-1, 1)
    occ_row = occurrence.reshape(1, -1)
    give = partial_sums(idx, owned_col, occ_row, tok_grad, n_out, f_dev, True, BF)
    took = swap(give)
    keep = partial_sums(idx, owned_col, occ_row, tok_grad, n_out, f_dev, False, F32)

    flat = embeds.reshape(rows, cols)
    pair = m >> 1
    mine = lax.dynamic_slice_in_dim(flat, pair * (rows // 2), rows // 2, 0)
    others = lax.dynamic_slice_in_dim(flat, (1 - pair) * (rows // 2), rows // 2, 0)
    near2 = flip(others, 2)
    far2 = flip(mine, 2)
    near1, near3 = flip(mine, 1), flip(near2, 1)
    far1, far3 = flip(others, 1), flip(far2, 1)
    gain_row = gain.reshape(1, width)
    near, near_r, *sends = call(
        functools.partial(norm_kernel, True),
        (idx, mine, near1, near2, near3, gain_row),
        [((rows // 2, width), BF), ((rows // 2, 1), F32)] + [((2, quarter, feats), BF)] * n_out,
    )

    both = keep + took.astype(F32)
    both = both.reshape(n_out, f_dev, cols)
    total = both[0]
    for k in range(1, n_out):
        total = total + shift(both[k].astype(BF), k).astype(F32)
    grad0 = total.astype(BF)
    grad2 = flip(grad0, 2)
    grad1, grad3 = flip(grad0, 1), flip(grad2, 1)

    def route(pieces):
        came = [pieces[0]] + [shift(pieces[k], k) for k in range(1, n_out)]
        direct = jnp.stack([c[0] for c in came])
        crossed = swap(jnp.stack([c[1] for c in came]))
        whole = jnp.concatenate([direct, crossed])
        from2 = flip(whole, 2)
        return whole, flip(whole, 1), from2, flip(from2, 1)

    normed_all = route(sends)

    far, far_r = call(
        functools.partial(norm_kernel, False),
        (idx, others, far1, far2, far3, gain_row),
        [((rows // 2, width), BF), ((rows // 2, 1), F32)],
    )

    length = jnp.sum((token_ids != 0).astype(jnp.int32), axis=1)
    positions = jnp.arange(flen, dtype=jnp.int32)
    lastmask = (positions[None, :] == (length - 1)[:, None]).astype(F32)
    keymask = (positions[None, :] < length[:, None]).astype(F32)
    lmask = lastmask.reshape(4, 1, quarter)
    kmask = keymask.reshape(4, 1, quarter)

    heads = cols // HEAD
    early, probs, raw, upro = call(
        functools.partial(forward_kernel, flen),
        (idx, near, far, w_query, w_key, w_value, kmask, lmask),
        [
            ((f_dev, 2 * cols + 128), BF),
            ((4, heads * fq, quarter), F32),
            ((4, heads * fq, quarter), F32),
            ((4, heads * fq, width), BF),
        ],
        [pltpu.VMEM((f_dev, width), BF), pltpu.VMEM((heads, f_dev, width), BF)],
    )

    def gather(item):
        direct = [item] + [shift(item, k) for k in range(1, n_out)]
        return direct + [swap(d) for d in direct]

    early_all = gather(early)

    late, product, d0, d1, d2, d3 = call(
        functools.partial(backward_kernel, flen),
        (idx, near, far, w_query, w_key, w_value, w_out, lmask,
         grad0, grad1, grad2, grad3, early, probs, raw, upro),
        [((f_dev, 2 * cols + 128), BF), ((4, quarter), F32)] + [((rows, cols), BF)] * 4,
        [
            pltpu.VMEM((4, heads * fq, width), BF),
            pltpu.VMEM((f_dev, width), BF),
            pltpu.VMEM((heads, f_dev, width), BF),
            pltpu.VMEM((4, heads * fq, quarter), BF),
        ],
    )
    late_all = gather(late)

    grad_full = jnp.stack([grad0, grad1, grad2, grad3])
    grad_quarter = lax.dynamic_slice_in_dim(grad_full, m * fq, fq, 1)
    pieces = []
    for k in range(n_out):
        block = lax.dynamic_index_in_dim(grad_quarter, m ^ lax.rem(z + k, n_out), 0, False)
        block = block.reshape(fq, 2, feats)
        first = lax.dynamic_index_in_dim(block, x, 1, False)
        second = lax.dynamic_index_in_dim(block, 1 - x, 1, False)
        pieces.append(jnp.stack([first, second]))
    grads_all = route(pieces)

    query_grad, key_grad, value_grad, out_grad = call(
        functools.partial(weights_kernel, flen, n_tok),
        (idx, *normed_all, *grads_all, *early_all, *late_all),
        [((feats, cols), F32)] * 3 + [((cols, feats), F32)],
        [
            pltpu.VMEM((2 * heads + 1, n_tok * fq, feats), BF),
            pltpu.VMEM((n_tok * fq, cols), BF),
            pltpu.VMEM((n_tok * fq, cols), BF),
            pltpu.VMEM((n_tok * fq, cols), BF),
            pltpu.VMEM((n_tok * fq, cols), BF),
        ],
    )

    product = product + flip(product, 1)
    product = product + flip(product, 2)
    own = d0.astype(F32) + flip(d1, 1).astype(F32)
    across = d2.astype(F32) + flip(d3, 1).astype(F32)
    summed = own + flip(across.astype(BF), 2).astype(F32)
    recip = jnp.where(
        pair == 0, jnp.concatenate([near_r, far_r]), jnp.concatenate([far_r, near_r])
    ).reshape(f_dev, flen, 1)
    gain_mine = lax.dynamic_slice_in_dim(gain, m * cols, cols, 0)
    scaled = summed.reshape(f_dev, flen, cols) * gain_mine
    weight = recip * recip * (product.reshape(f_dev, flen, 1) * (1.0 / width))
    result = recip * scaled - embeds.astype(F32) * weight
    result = result + jnp.where(lastmask[..., None] > 0, grad0.astype(F32)[:, None, :], 0.0)
    return (result.astype(BF), query_grad, key_grad, value_grad, out_grad)


def general(tok_grad, occurrence, owned, token_ids, embeds, gain, w_query, w_key, w_value, w_out):
    f32 = F32
    bf16 = BF
    n_tok = lax.axis_size("tok")
    fgrams = owned.shape[0]
    f_dev = fgrams // n_tok
    width = gain.shape[0]
    cols = w_key.shape[1]
    local_heads = cols // HEAD
    flen = token_ids.shape[1]
    scale = 1.0 / HEAD**0.5
    onehot = (owned[:, None] == occurrence[None, :]).astype(bf16)
    partial_sum = jnp.dot(onehot, tok_grad, preferred_element_type=f32)
    blocks = partial_sum.reshape(n_tok, f_dev, tok_grad.shape[1])
    arrived = lax.all_to_all(blocks, "tok", split_axis=0, concat_axis=0, tiled=True)
    fgram_sum = jnp.sum(arrived, axis=0)
    fgram_grad = fgram_sum.astype(bf16)
    full_grad = lax.all_gather(fgram_grad, "mdl", axis=1, tiled=True)
    whole_embeds = lax.all_gather(embeds, "mdl", axis=2, tiled=True)
    length = jnp.sum((token_ids != 0).astype(jnp.int32), axis=1)
    positions = jnp.arange(flen, dtype=jnp.int32)
    lastmask = positions[None, :] == (length - 1)[:, None]
    keymask = (positions[None, :] < length[:, None]).astype(f32)
    xfull = whole_embeds.astype(f32)
    recip = lax.rsqrt(jnp.mean(xfull * xfull, axis=-1) + 1e-06)
    normed = (xfull * recip[..., None] * gain).astype(bf16)
    normed_last = jnp.sum(jnp.where(lastmask[..., None], normed.astype(f32), 0.0), axis=1).astype(bf16)
    rows = normed.reshape(f_dev * flen, width)
    keys = dot(rows, w_key).astype(bf16).reshape(f_dev, flen, local_heads, HEAD)
    values = dot(rows, w_value).astype(bf16).reshape(f_dev, flen, local_heads, HEAD)
    query = dot(normed_last, w_query).astype(bf16).reshape(f_dev, local_heads, HEAD)
    keys32 = keys.astype(f32)
    values32 = values.astype(f32)
    query32 = query.astype(f32)
    scores = jnp.einsum("fhd,fjhd->fhj", query, keys, preferred_element_type=f32) * scale
    expo = jnp.exp(scores) * keymask[:, None, :]
    probs = expo / jnp.sum(expo, axis=-1, keepdims=True)
    probs_b = probs.astype(bf16)
    attended = jnp.einsum("fhj,fjhd->fhd", probs_b, values, preferred_element_type=f32)
    attended = attended.astype(bf16).reshape(f_dev, cols)
    d_att = rdot(full_grad, w_out).reshape(f_dev, local_heads, HEAD)
    d_prob = jnp.einsum("fhd,fjhd->fhj", d_att, values32)
    d_score = probs * (d_prob - jnp.sum(probs * d_prob, axis=-1, keepdims=True)) * scale
    d_query = jnp.einsum("fhj,fjhd->fhd", d_score, keys32).astype(bf16).reshape(f_dev, cols)
    d_key = jnp.einsum("fhj,fhd->fjhd", d_score, query32).astype(bf16).reshape(f_dev * flen, cols)
    d_value = jnp.einsum("fhj,fhd->fjhd", probs_b.astype(f32), d_att)
    d_value = d_value.astype(bf16).reshape(f_dev * flen, cols)
    d_normed = (rdot(d_key, w_key) + rdot(d_value, w_value)).reshape(f_dev, flen, width)
    from_query = rdot(d_query, w_query)
    d_normed = d_normed + jnp.where(lastmask[..., None], from_query[:, None, :], 0.0)
    feat_start = lax.axis_index("mdl") * embeds.shape[2]
    summed = lax.psum(d_normed, "mdl")
    scaled = summed * gain
    product = jnp.mean(xfull * scaled, axis=-1)
    result = recip[..., None] * scaled - xfull * (recip**3 * product)[..., None]
    result = lax.dynamic_slice_in_dim(result, feat_start, embeds.shape[2], 2)
    result = result + jnp.where(lastmask[..., None], fgram_grad.astype(f32)[:, None, :], 0.0)
    query_grad, key_grad, value_grad = (
        lax.psum_scatter(part, "tok", scatter_dimension=0, tiled=True)
        for part in (tdot(normed_last, d_query), tdot(rows, d_key), tdot(rows, d_value))
    )
    out_grad = lax.psum_scatter(tdot(attended, full_grad), "tok", scatter_dimension=1, tiled=True)
    return (result.astype(bf16), query_grad, key_grad, value_grad, out_grad)


def chosen(*args):
    fits = lax.axis_size("tok") == 8 and lax.axis_size("mdl") == 4
    return (on_device if fits else general)(*args)


def solution(mesh):
    return jax.shard_map(
        chosen,
        mesh=mesh,
        in_specs=(
            P("tok", "mdl"),
            P("tok"),
            P(),
            P("tok", None),
            P("tok", None, "mdl"),
            P(),
            P(None, "mdl"),
            P(None, "mdl"),
            P(None, "mdl"),
            P("mdl", None),
        ),
        out_specs=(
            P("tok", None, "mdl"),
            P("tok", "mdl"),
            P("tok", "mdl"),
            P("tok", "mdl"),
            P("mdl", "tok"),
        ),
        check_vma=False,
    )
```

time: 657 us -> 261 us (0.40)
  waiting for transfers between devices: 529 us -> 117 us
  Pallas kernels: 0 us -> 62 us
  starting transfers between devices: 7.85 us -> 57.8 us
  matrix products: 45.6 us -> 0 us
  other arithmetic: 32.9 us -> 8.81 us
  between operations: 14.5 us -> 1.43 us
  local copies, waits for them, and re-layouts: 18.8 us -> 8.96 us
  blocking collectives: 7.2 us -> 0 us
    reduce_scatter x4 -> x0, waiting for transfers between devices: 357 us -> none  [the longest x1 92.8 us: on_device(): lax.psum_scatter(out_part, 'tok', scatter_dimension=1, tiled=True)]
    psum x1 -> x0, waiting for transfers between devices: 124 us -> none  [on_device(): summed = lax.psum(d_normed, 'mdl')]
    ppermute x0 -> x46, waiting for transfers between devices: none -> 117 us  [the longest x15 51.7 us: shift(): return lax.ppermute(array, 'tok', pairs)]
    pallas_call x0 -> x7, Pallas kernels: none -> 62 us  [the longest x5 51 us: call(): pl.pallas_call(body, in_specs=[SMEM] * smem + [VMEM] * (len(ins) - smem),...]
    ppermute x0 -> x46, starting transfers between devices: none -> 57.8 us  [the longest x15 29.9 us: shift(): return lax.ppermute(array, 'tok', pairs)]
    all_to_all x1 -> x0, waiting for transfers between devices: 48.1 us -> none  [on_device(): lax.all_to_all(blocks, 'tok', split_axis=0, concat_axis=0, tiled=True)]
    dot_general x16 -> x0, matrix products: 45.6 us -> none  [the longest x4 19.1 us: tdot(): lax.dot_general(left, right, (((0,), (0,)), ((), ())), preferred_element_...]
    reduce_sum x4 -> x0, other arithmetic: 19.2 us -> none  [the longest x1 9.11 us: on_device(): product = jnp.mean(xfull * scaled, axis=-1)]
  transfers between devices with their start and end apart: 7 -> 46, of which waited for: 6 -> 19; matrix products, arithmetic and copies ran while one was open for 10% -> 5% of each run, Pallas kernels for 0% -> 17%
where the time goes in v1:
time: 261 us; the launch traced here: 256 us
  waiting for transfers between devices  117 us (45%)
  Pallas kernels  62 us (24%)
  starting transfers between devices  57.8 us (22%)
  local copies, waits for them, and re-layouts  8.96 us (3%)
  other arithmetic  8.81 us (3%)
    ppermute x15, waiting for transfers between devices, shift(): return lax.ppermute(array, 'tok', pairs)  51.7 us
    pallas_call x5, Pallas kernels, call(): pl.pallas_call(body, in_specs=[SMEM] * smem + [VMEM] * (len(ins) - smem),...  51 us
    ppermute x11, waiting for transfers between devices, swap(): return lax.ppermute(array, 'tok', [(i, i ^ 1) for i in range(n_tok)])  46.5 us
    ppermute x15, starting transfers between devices, shift(): return lax.ppermute(array, 'tok', pairs)  29.9 us
    ppermute x20, waiting for transfers between devices, flip(): return lax.ppermute(array, 'mdl', [(i, i ^ bit) for i in range(4)])  19.1 us
    ppermute x11, starting transfers between devices, swap(): return lax.ppermute(array, 'tok', [(i, i ^ 1) for i in range(n_tok)])  15.2 us
    ppermute x20, starting transfers between devices, flip(): return lax.ppermute(array, 'mdl', [(i, i ^ bit) for i in range(4)])  12.7 us
    pallas_call x2, Pallas kernels, partial_sums(): pl.pallas_call(sums_kernel, grid_spec=pltpu.PrefetchScalarGridSpec(num_sc...  11 us
  transfers between devices with their start and end apart: 46, of which 19 were waited for; matrix products, arithmetic and copies ran while one was open for 5% of the time, Pallas kernels for 17%

profile of v1, /device:TPU:0, one launch (start us, length us, event | category | flops | bytes accessed | tf_op | source)
XLA Modules:
  0.0 256.3 jit_solution(7572333695776276931)
XLA Ops:
  0.6 1.7 copy.37.owned
  2.9 5.5 %shard_map.140 = bf16[512,512]{1,0:T(8,128)(2,1)} custom-call(s32[4]{0:T(128)} %pad_add_fusion.idx, s32[1024,1]{1,0:T(8,128)} %copy.37.owned, s32[1,2048]{1,0:T(1,128)} %bitcast.59, bf16[2048,512]{1,0:T(8,128)(2,1)} %grads.3), custom_call_target="tpu_custom_call" | custom-call | tf_op jit(solution)/shard_map/pallas_call | solution.py:54
  8.4 2.9 %collective-permute-start.6 = (bf16[512,512]{1,0:T(8,128)(2,1)}, bf16[512,512]{1,0:T(8,128)(2,1)S(1)}, u32[]{:S(2)}, u32[]{:S(2)}) collective-permute-start(bf16[512,512]{1,0:T(8,128)(2,1)} %shard_map.140), channel_id=1, source_target_pairs={{0,4},{4,0},{8,12},{12,8},{16,20},{20,16},{24,28},{28,24},{1,5},{5... | collective-permute-start | bytes 1572872 | tf_op jit(solution)/shard_map/ppermute | solution.py:291
  11.3 5.5 %shard_map.139 = f32[512,512]{1,0:T(8,128)} custom-call(s32[4]{0:T(128)} %pad_add_fusion.idx, s32[1024,1]{1,0:T(8,128)} %copy.37.owned, s32[1,2048]{1,0:T(1,128)} %bitcast.60, bf16[2048,512]{1,0:T(8,128)(2,1)} %grads.3), custom_call_target="tpu_custom_call" | custom-call | tf_op jit(solution)/shard_map/pallas_call | solution.py:54
  16.9 6.6 %collective-permute-done.6 = bf16[512,512]{1,0:T(8,128)(2,1)S(1)} collective-permute-done((bf16[512,512]{1,0:T(8,128)(2,1)}, bf16[512,512]{1,0:T(8,128)(2,1)S(1)}, u32[]{:S(2)}, u32[]{:S(2)}) %collective-permute-start.6) | collective-permute-done | bytes 524320 | tf_op jit(solution)/shard_map/ppermute | solution.py:291
  25.6 3.9 %collective-permute-start.9 = (bf16[128,512]{1,0:T(8,128)(2,1)}, bf16[128,512]{1,0:T(8,128)(2,1)}, u32[]{:S(2)}, u32[]{:S(2)}) collective-permute-start(bf16[128,512]{1,0:T(8,128)(2,1)} %get-tuple-element.60), channel_id=1, source_target_pairs={{0,24},{4,28},{8,0},{12,4},{16,8},{20,12},{24,16},{28,20},{1,25},{... | collective-permute-start | bytes 393224 | tf_op jit(solution)/shard_map/ppermute | solution.py:295
  30.6 1.6 collective-permute-start.4
  33.7 1.5 collective-permute-start.1
  35.2 5.3 %collective-permute-done.8 = bf16[128,512]{1,0:T(8,128)(2,1)} collective-permute-done((bf16[128,512]{1,0:T(8,128)(2,1)S(1)}, bf16[128,512]{1,0:T(8,128)(2,1)}, u32[]{:S(2)}, u32[]{:S(2)}) %collective-permute-start.8) | collective-permute-done | bytes 131104 | tf_op jit(solution)/shard_map/ppermute | solution.py:295
  41.7 1.6 collective-permute-start.11
  43.6 15.4 %collective-permute-done.11.g2 = bf16[128,512]{1,0:T(8,128)(2,1)S(1)} collective-permute-done((bf16[128,512]{1,0:T(8,128)(2,1)S(1)}, bf16[128,512]{1,0:T(8,128)(2,1)S(1)}, u32[]{:S(2)}, u32[]{:S(2)}) %collective-permute-start.11) | collective-permute-done | bytes 131104 | tf_op jit(solution)/shard_map/ppermute | solution.py:288
  61.3 2.5 collective-permute-start.25
  63.9 3.2 %collective-permute-done.25 = bf16[2,32,256]{2,1,0:T(8,128)(2,1)S(1)} collective-permute-done((bf16[2,32,256]{2,1,0:T(8,128)(2,1)S(1)}, bf16[2,32,256]{2,1,0:T(8,128)(2,1)S(1)}, u32[]{:S(2)}, u32[]{:S(2)}) %collective-permute-start.25) | collective-permute-done | bytes 32800 | tf_op jit(solution)/shard_map/ppermute | solution.py:295
  67.2 2.9 %collective-permute-start.27 = (bf16[2,32,256]{2,1,0:T(8,128)(2,1)S(1)}, bf16[2,32,256]{2,1,0:T(8,128)(2,1)S(1)}, u32[]{:S(2)}, u32[]{:S(2)}) collective-permute-start(bf16[2,32,256]{2,1,0:T(8,128)(2,1)S(1)} %pad_maximum_fusion.5), channel_id=1, source_target_pairs={{0,24},{4,28},{8,0},{12,4},{16,8},{20,12},{24,16},{28,20},{1,25},{... | collective-permute-start | bytes 98312 | tf_op jit(solution)/shard_map/ppermute | solution.py:295
  70.1 4.7 %shard_map.137 = (bf16[512,2048]{1,0:T(8,128)(2,1)}, f32[512,1]{1,0:T(8,128)}, bf16[2,256,256]{2,1,0:T(8,128)(2,1)}, bf16[2,256,256]{2,1,0:T(8,128)(2,1)}, bf16[...) custom-call(s32[4]{0:T(128)} %pad_add_fusion.idx, bf16[512,512]{1,0:T(8,128)(2,1)} %copy-done.2, ...), custom_call_target="tpu_custom_call" | custom-call | tf_op jit(solution)/shard_map/pallas_call | solution.py:31
  74.9 4.3 %shard_map.138 = (bf16[512,2048]{1,0:T(8,128)(2,1)}, f32[512,1]{1,0:T(8,128)}) custom-call(s32[4]{0:T(128)} %pad_add_fusion.idx, bf16[512,512]{1,0:T(8,128)(2,1)} %copy-done.1, bf16[512,512]{1,0:T(8,128)(2,1)} %collective-permute-done.3.x1, bf16[512,512]{1,0:T(8,128)(2,1)} %collective-permute-done.4.x2, bf16[512,512]{1,0:T(8,128)(2,1)} %collective-permute-done.5.x3, ...), custom_call_target="tpu_custom_call" | custom-call | tf_op jit(solution)/shard_map/pallas_call | solution.py:31
  79.2 11.7 %shard_map.141 = (bf16[128,1152]{1,0:T(8,128)(2,1)}, f32[4,128,256]{2,1,0:T(8,128)}, f32[4,128,256]{2,1,0:T(8,128)}, bf16[4,128,2048]{2,1,0:T(8,128)(2,1)}) custom-call(s32[4]{0:T(128)} %pad_add_fusion.idx, bf16[512,2048]{1,0:T(8,128)(2,1)} %get-tuple-element.29.near, bf16[512,2048]{1,0:T(8,128)(2,1)} %get-tuple-element.30.far, bf16[2048,512]{1,0:T(8,128)(2,1)} %w_query.3, ...), custom_call_target="tpu_custom_call" | custom-call | tf_op jit(solution)/shard_map/pallas_call | solution.py:31
  90.9 18.0 %shard_map.142 = (bf16[128,1152]{1,0:T(8,128)(2,1)}, f32[4,256]{1,0:T(4,128)}, bf16[1024,512]{1,0:T(8,128)(2,1)}, bf16[1024,512]{1,0:T(8,128)(2,1)}, bf16[1024,5...) custom-call(s32[4]{0:T(128)} %pad_add_fusion.idx, bf16[512,2048]{1,0:T(8,128)(2,1)} %get-tuple-element.29.near, ...), custom_call_target="tpu_custom_call" | custom-call | tf_op jit(solution)/shard_map/pallas_call | solution.py:31
  109.1 3.8 %collective-permute-start.20 = (bf16[2,256,256]{2,1,0:T(8,128)(2,1)S(1)}, bf16[2,256,256]{2,1,0:T(8,128)(2,1)S(1)}, u32[]{:S(2)}, u32[]{:S(2)}) collective-permute-start(bf16[2,256,256]{2,1,0:T(8,128)(2,1)S(1)} %copy-done.28), channel_id=1, source_target_pairs={{0,24},{4,28},{8,0},{12,4},{16,8},{20,12},{24,16},{28,20},{1,25},{... | collective-permute-start | bytes 786440 | tf_op jit(solution)/shard_map/ppermute | solution.py:295
  113.0 16.1 %collective-permute-done.19 = bf16[2,256,256]{2,1,0:T(8,128)(2,1)S(1)} collective-permute-done((bf16[2,256,256]{2,1,0:T(8,128)(2,1)S(1)}, bf16[2,256,256]{2,1,0:T(8,128)(2,1)S(1)}, u32[]{:S(2)}, u32[]{:S(2)}) %collective-permute-start.19) | collective-permute-done | bytes 262176 | tf_op jit(solution)/shard_map/ppermute | solution.py:295
  129.3 1.5 collective-permute-start.21
  131.5 12.9 %collective-permute-done.28 = bf16[4,32,256]{2,1,0:T(8,128)(2,1)S(1)} collective-permute-done((bf16[4,32,256]{2,1,0:T(8,128)(2,1)S(1)}, bf16[4,32,256]{2,1,0:T(8,128)(2,1)S(1)}, u32[]{:S(2)}, u32[]{:S(2)}) %collective-permute-start.28) | collective-permute-done | bytes 65568 | tf_op jit(solution)/shard_map/ppermute | solution.py:291
  144.4 1.6 collective-permute-start.30
  146.0 1.6 collective-permute-start.32
  149.5 1.5 collective-permute-start.17
  151.0 2.0 collective-permute-done.17
  153.1 1.5 collective-permute-start.23
  154.6 2.0 collective-permute-start.33
  156.6 2.6 collective-permute-start.34
  159.1 1.5 collective-permute-start.35
  160.6 9.5 %collective-permute-done.33.refs_2_ = bf16[128,1152]{1,0:T(8,128)(2,1)} collective-permute-done((bf16[128,1152]{1,0:T(8,128)(2,1)S(1)}, bf16[128,1152]{1,0:T(8,128)(2,1)}, u32[]{:S(2)}, u32[]{:S(2)}) %collective-permute-start.33) | collective-permute-done | bytes 294944 | tf_op jit(solution)/shard_map/ppermute | solution.py:295
  170.1 5.9 %collective-permute-start.39 = (bf16[128,1152]{1,0:T(8,128)(2,1)S(1)}, bf16[128,1152]{1,0:T(8,128)(2,1)S(1)}, u32[]{:S(2)}, u32[]{:S(2)}) collective-permute-start(bf16[128,1152]{1,0:T(8,128)(2,1)S(1)} %copy-done.11), channel_id=1, source_target_pairs={{0,8},{4,12},{8,16},{12,20},{16,24},{20,28},{24,0},{28,4},{1,9},{5... | collective-permute-start | bytes 884744 | tf_op jit(solution)/shard_map/ppermute | solution.py:295
  176.0 3.5 %collective-permute-start.40 = (bf16[128,1152]{1,0:T(8,128)(2,1)S(1)}, bf16[128,1152]{1,0:T(8,128)(2,1)S(1)}, u32[]{:S(2)}, u32[]{:S(2)}) collective-permute-start(bf16[128,1152]{1,0:T(8,128)(2,1)S(1)} %copy-done.11), channel_id=1, source_target_pairs={{0,16},{4,20},{8,24},{12,28},{16,0},{20,4},{24,8},{28,12},{1,17},{... | collective-permute-start | bytes 884744 | tf_op jit(solution)/shard_map/ppermute | solution.py:295
  179.5 1.5 collective-permute-start.42
  182.3 4.5 %collective-permute-done.39.refs_9_ = bf16[128,1152]{1,0:T(8,128)(2,1)S(1)} collective-permute-done((bf16[128,1152]{1,0:T(8,128)(2,1)S(1)}, bf16[128,1152]{1,0:T(8,128)(2,1)S(1)}, u32[]{:S(2)}, u32[]{:S(2)}) %collective-permute-start.39) | collective-permute-done | bytes 294944 | tf_op jit(solution)/shard_map/ppermute | solution.py:295
  186.9 11.9 %collective-permute-done.40.refs_10_ = bf16[128,1152]{1,0:T(8,128)(2,1)S(1)} collective-permute-done((bf16[128,1152]{1,0:T(8,128)(2,1)S(1)}, bf16[128,1152]{1,0:T(8,128)(2,1)S(1)}, u32[]{:S(2)}, u32[]{:S(2)}) %collective-permute-start.40) | collective-permute-done | bytes 294944 | tf_op jit(solution)/shard_map/ppermute | solution.py:295
  198.8 1.5 collective-permute-start.15
  200.3 1.5 collective-permute-start.36
  203.9 6.7 %collective-permute-done.36.refs_5_ = bf16[128,1152]{1,0:T(8,128)(2,1)} collective-permute-done((bf16[128,1152]{1,0:T(8,128)(2,1)}, bf16[128,1152]{1,0:T(8,128)(2,1)}, u32[]{:S(2)}, u32[]{:S(2)}) %collective-permute-start.36) | collective-permute-done | bytes 294944 | tf_op jit(solution)/shard_map/ppermute | solution.py:291
  213.5 2.0 collective-permute-done.37.refs_6_
  215.5 1.5 collective-permute-start.38
  218.4 5.1 %collective-permute-done.38.refs_7_ = bf16[128,1152]{1,0:T(8,128)(2,1)} collective-permute-done((bf16[128,1152]{1,0:T(8,128)(2,1)}, bf16[128,1152]{1,0:T(8,128)(2,1)}, u32[]{:S(2)}, u32[]{:S(2)}) %collective-permute-start.38) | collective-permute-done | bytes 294944 | tf_op jit(solution)/shard_map/ppermute | solution.py:291
  225.5 1.5 collective-permute-start.45
  227.0 2.9 %fusion.3 = bf16[128,8,512]{2,1,0:T(8,128)(2,1)} fusion(bf16[128,8,512]{2,1,0:T(8,128)(2,1)S(1)} %copy-done, bf16[1024,512]{1,0:T(8,128)(2,1)} %collective-permute-done.15, bf16[1024,512]{1,0:T(8,128)(2,1)} %collective-permute-done.13, bf16[1024,512]{1,0:T(8,128)(2,1)S(1)} %copy-done.6, f32[128,512]{1,0:T(8,128)S(1)} %get-tuple-element.49, ...), kind=kLoop, calls=%fused_computation.4 | loop fusion | flops 6815744 | bytes 5516288 | tf_op jit(solution)/shard_map/convert_element_type | solution.py:420
  229.9 3.7 %collective-permute-done.43.refs_13_ = bf16[128,1152]{1,0:T(8,128)(2,1)S(1)} collective-permute-done((bf16[128,1152]{1,0:T(8,128)(2,1)}, bf16[128,1152]{1,0:T(8,128)(2,1)S(1)}, u32[]{:S(2)}, u32[]{:S(2)}) %collective-permute-start.43) | collective-permute-done | bytes 294944 | tf_op jit(solution)/shard_map/ppermute | solution.py:291
  233.6 6.3 %collective-permute-done.44.refs_14_ = bf16[128,1152]{1,0:T(8,128)(2,1)S(1)} collective-permute-done((bf16[128,1152]{1,0:T(8,128)(2,1)}, bf16[128,1152]{1,0:T(8,128)(2,1)S(1)}, u32[]{:S(2)}, u32[]{:S(2)}) %collective-permute-start.44) | collective-permute-done | bytes 294944 | tf_op jit(solution)/shard_map/ppermute | solution.py:291
  239.9 3.2 %collective-permute-done.45.refs_15_ = bf16[128,1152]{1,0:T(8,128)(2,1)S(1)} collective-permute-done((bf16[128,1152]{1,0:T(8,128)(2,1)}, bf16[128,1152]{1,0:T(8,128)(2,1)S(1)}, u32[]{:S(2)}, u32[]{:S(2)}) %collective-permute-start.45) | collective-permute-done | bytes 294944 | tf_op jit(solution)/shard_map/ppermute | solution.py:291
  243.8 12.3 %shard_map.143 = (f32[256,512]{1,0:T(8,128)}, f32[256,512]{1,0:T(8,128)}, f32[256,512]{1,0:T(8,128)}, f32[512,256]{1,0:T(8,128)}) custom-call(s32[4]{0:T(128)} %pad_add_fusion.idx, bf16[8,256,256]{2,1,0:T(8,128)(2,1)} %copy-done.3, bf16[8,256,256]{2,1,0:T(8,128)(2,1)} %collective-permute-done.22.b1, bf16[8,256,256]{2,1,0:T(8,128)(2,1)} %collective-permute-done.23.b2, ...), custom_call_target="tpu_custom_call" | custom-call | tf_op jit(solution)/shard_map/pallas_call | solution.py:31
  (171 shorter events, 22.2 us)
Async XLA Ops:
  8.4 15.1 %collective-permute-start.6 = (bf16[512,512]{1,0:T(8,128)(2,1)}, bf16[512,512]{1,0:T(8,128)(2,1)S(1)}, u32[]{:S(2)}, u32[]{:S(2)}) collective-permute-start(bf16[512,512]{1,0:T(8,128)(2,1)} %shard_map.140), channel_id=1, source_target_pairs={{0,4},{4,0},{8,12},{12,8},{16,20},{20,16},{24,28},{28,24},{1,5},{5... | collective-permute-start | bytes 1572872 | tf_op jit(solution)/shard_map/ppermute | solution.py:291
  25.6 8.1 %collective-permute-start.9 = (bf16[128,512]{1,0:T(8,128)(2,1)}, bf16[128,512]{1,0:T(8,128)(2,1)}, u32[]{:S(2)}, u32[]{:S(2)}) collective-permute-start(bf16[128,512]{1,0:T(8,128)(2,1)} %get-tuple-element.60), channel_id=1, source_target_pairs={{0,24},{4,28},{8,0},{12,4},{16,8},{20,12},{24,16},{28,20},{1,25},{... | collective-permute-start | bytes 393224 | tf_op jit(solution)/shard_map/ppermute | solution.py:295
  29.5 11.1 %collective-permute-start.8 = (bf16[128,512]{1,0:T(8,128)(2,1)S(1)}, bf16[128,512]{1,0:T(8,128)(2,1)}, u32[]{:S(2)}, u32[]{:S(2)}) collective-permute-start(bf16[128,512]{1,0:T(8,128)(2,1)S(1)} %get-tuple-element.61), channel_id=1, source_target_pairs={{0,16},{4,20},{8,24},{12,28},{16,0},{20,4},{24,8},{28,12},{1,17},{... | collective-permute-start | bytes 393224 | tf_op jit(solution)/shard_map/ppermute | solution.py:295
  29.5 11.1 %collective-permute-start.7 = (bf16[128,512]{1,0:T(8,128)(2,1)S(1)}, bf16[128,512]{1,0:T(8,128)(2,1)}, u32[]{:S(2)}, u32[]{:S(2)}) collective-permute-start(bf16[128,512]{1,0:T(8,128)(2,1)S(1)} %get-tuple-element.59), channel_id=1, source_target_pairs={{0,8},{4,12},{8,16},{12,20},{16,24},{20,28},{24,0},{28,4},{1,9},{5... | collective-permute-start | bytes 393224 | tf_op jit(solution)/shard_map/ppermute | solution.py:295
  30.6 36.6 %collective-permute-start = (bf16[512,512]{1,0:T(8,128)(2,1)S(1)}, bf16[512,512]{1,0:T(8,128)(2,1)}, u32[]{:S(2)}, u32[]{:S(2)}) collective-permute-start(bf16[512,512]{1,0:T(8,128)(2,1)S(1)} %get-tuple-element.54.x0), channel_id=1, source_target_pairs={{0,1},{1,0},{2,3},{3,2},{4,5},{5,4},{6,7},{7,6},{8,9},{9,8},{10,11... | collective-permute-start | bytes 1572872 | tf_op jit(solution)/shard_map/ppermute | solution.py:288
  30.6 29.5 %collective-permute-start.4 = (bf16[512,512]{1,0:T(8,128)(2,1)S(1)}, bf16[512,512]{1,0:T(8,128)(2,1)}, u32[]{:S(2)}, u32[]{:S(2)}) collective-permute-start(bf16[512,512]{1,0:T(8,128)(2,1)S(1)} %get-tuple-element.54.x0), channel_id=1, source_target_pairs={{0,2},{1,3},{2,0},{3,1},{4,6},{5,7},{6,4},{7,5},{8,10},{9,11},{10,... | collective-permute-start | bytes 1572872 | tf_op jit(solution)/shard_map/ppermute | solution.py:288
  33.7 25.9 %collective-permute-start.1 = (bf16[512,512]{1,0:T(8,128)(2,1)S(1)}, bf16[512,512]{1,0:T(8,128)(2,1)}, u32[]{:S(2)}, u32[]{:S(2)}) collective-permute-start(bf16[512,512]{1,0:T(8,128)(2,1)S(1)} %get-tuple-element.53.x0), channel_id=1, source_target_pairs={{0,2},{1,3},{2,0},{3,1},{4,6},{5,7},{6,4},{7,5},{8,10},{9,11},{10,... | collective-permute-start | bytes 1572872 | tf_op jit(solution)/shard_map/ppermute | solution.py:288
  41.7 17.3 %collective-permute-start.11 = (bf16[128,512]{1,0:T(8,128)(2,1)S(1)}, bf16[128,512]{1,0:T(8,128)(2,1)S(1)}, u32[]{:S(2)}, u32[]{:S(2)}) collective-permute-start(bf16[128,512]{1,0:T(8,128)(2,1)S(1)} %get-tuple-element.50.g0), channel_id=1, source_target_pairs={{0,2},{1,3},{2,0},{3,1},{4,6},{5,7},{6,4},{7,5},{8,10},{9,11},{10,... | collective-permute-start | bytes 393224 | tf_op jit(solution)/shard_map/ppermute | solution.py:288
  43.5 16.7 %collective-permute-start.10 = (bf16[128,512]{1,0:T(8,128)(2,1)S(1)}, bf16[128,512]{1,0:T(8,128)(2,1)S(1)}, u32[]{:S(2)}, u32[]{:S(2)}) collective-permute-start(bf16[128,512]{1,0:T(8,128)(2,1)S(1)} %get-tuple-element.50.g0), channel_id=1, source_target_pairs={{0,1},{1,0},{2,3},{3,2},{4,5},{5,4},{6,7},{7,6},{8,9},{9,8},{10,11... | collective-permute-start | bytes 393224 | tf_op jit(solution)/shard_map/ppermute | solution.py:288
  59.0 1.6 collective-permute-start.12
  59.7 15.2 %collective-permute-start.3 = (bf16[512,512]{1,0:T(8,128)(2,1)S(1)}, bf16[512,512]{1,0:T(8,128)(2,1)}, u32[]{:S(2)}, u32[]{:S(2)}) collective-permute-start(bf16[512,512]{1,0:T(8,128)(2,1)S(1)} %get-tuple-element.53.x0), channel_id=1, source_target_pairs={{0,1},{1,0},{2,3},{3,2},{4,5},{5,4},{6,7},{7,6},{8,9},{9,8},{10,11... | collective-permute-start | bytes 1572872 | tf_op jit(solution)/shard_map/ppermute | solution.py:288
  60.1 10.0 %collective-permute-start.2 = (bf16[512,512]{1,0:T(8,128)(2,1)}, bf16[512,512]{1,0:T(8,128)(2,1)}, u32[]{:S(2)}, u32[]{:S(2)}) collective-permute-start(bf16[512,512]{1,0:T(8,128)(2,1)} %collective-permute-done.1.x2), channel_id=1, source_target_pairs={{0,1},{1,0},{2,3},{3,2},{4,5},{5,4},{6,7},{7,6},{8,9},{9,8},{10,11... | collective-permute-start | bytes 1572872 | tf_op jit(solution)/shard_map/ppermute | solution.py:288
  60.2 14.7 %collective-permute-start.5 = (bf16[512,512]{1,0:T(8,128)(2,1)}, bf16[512,512]{1,0:T(8,128)(2,1)}, u32[]{:S(2)}, u32[]{:S(2)}) collective-permute-start(bf16[512,512]{1,0:T(8,128)(2,1)} %collective-permute-done.4.x2), channel_id=1, source_target_pairs={{0,1},{1,0},{2,3},{3,2},{4,5},{5,4},{6,7},{7,6},{8,9},{9,8},{10,11... | collective-permute-start | bytes 1572872 | tf_op jit(solution)/shard_map/ppermute | solution.py:288
  61.3 5.8 %collective-permute-start.25 = (bf16[2,32,256]{2,1,0:T(8,128)(2,1)S(1)}, bf16[2,32,256]{2,1,0:T(8,128)(2,1)S(1)}, u32[]{:S(2)}, u32[]{:S(2)}) collective-permute-start(bf16[2,32,256]{2,1,0:T(8,128)(2,1)S(1)} %pad_maximum_fusion.3), channel_id=1, source_target_pairs={{0,8},{4,12},{8,16},{12,20},{16,24},{20,28},{24,0},{28,4},{1,9},{5... | collective-permute-start | bytes 98312 | tf_op jit(solution)/shard_map/ppermute | solution.py:295
  67.0 7.8 %collective-permute-start.26 = (bf16[2,32,256]{2,1,0:T(8,128)(2,1)S(1)}, bf16[2,32,256]{2,1,0:T(8,128)(2,1)S(1)}, u32[]{:S(2)}, u32[]{:S(2)}) collective-permute-start(bf16[2,32,256]{2,1,0:T(8,128)(2,1)S(1)} %pad_maximum_fusion.4), channel_id=1, source_target_pairs={{0,16},{4,20},{8,24},{12,28},{16,0},{20,4},{24,8},{28,12},{1,17},{... | collective-permute-start | bytes 98312 | tf_op jit(solution)/shard_map/ppermute | solution.py:295
  67.2 63.6 %collective-permute-start.27 = (bf16[2,32,256]{2,1,0:T(8,128)(2,1)S(1)}, bf16[2,32,256]{2,1,0:T(8,128)(2,1)S(1)}, u32[]{:S(2)}, u32[]{:S(2)}) collective-permute-start(bf16[2,32,256]{2,1,0:T(8,128)(2,1)S(1)} %pad_maximum_fusion.5), channel_id=1, source_target_pairs={{0,24},{4,28},{8,0},{12,4},{16,8},{20,12},{24,16},{28,20},{1,25},{... | collective-permute-start | bytes 98312 | tf_op jit(solution)/shard_map/ppermute | solution.py:295
  74.8 38.2 %collective-permute-start.18 = (bf16[2,256,256]{2,1,0:T(8,128)(2,1)}, bf16[2,256,256]{2,1,0:T(8,128)(2,1)S(1)}, u32[]{:S(2)}, u32[]{:S(2)}) collective-permute-start(bf16[2,256,256]{2,1,0:T(8,128)(2,1)} %get-tuple-element.41), channel_id=1, source_target_pairs={{0,8},{4,12},{8,16},{12,20},{16,24},{20,28},{24,0},{28,4},{1,9},{5... | collective-permute-start | bytes 786440 | tf_op jit(solution)/shard_map/ppermute | solution.py:295
  109.0 70.5 %collective-permute-start.14 = (bf16[1024,512]{1,0:T(8,128)(2,1)}, bf16[1024,512]{1,0:T(8,128)(2,1)S(1)}, u32[]{:S(2)}, u32[]{:S(2)}) collective-permute-start(bf16[1024,512]{1,0:T(8,128)(2,1)} %get-tuple-element.38), channel_id=1, source_target_pairs={{0,1},{1,0},{2,3},{3,2},{4,5},{5,4},{6,7},{7,6},{8,9},{9,8},{10,11... | collective-permute-start | bytes 3145736 | tf_op jit(solution)/shard_map/ppermute | solution.py:288
  109.1 20.1 %collective-permute-start.20 = (bf16[2,256,256]{2,1,0:T(8,128)(2,1)S(1)}, bf16[2,256,256]{2,1,0:T(8,128)(2,1)S(1)}, u32[]{:S(2)}, u32[]{:S(2)}) collective-permute-start(bf16[2,256,256]{2,1,0:T(8,128)(2,1)S(1)} %copy-done.28), channel_id=1, source_target_pairs={{0,24},{4,28},{8,0},{12,4},{16,8},{20,12},{24,16},{28,20},{1,25},{... | collective-permute-start | bytes 786440 | tf_op jit(solution)/shard_map/ppermute | solution.py:295
  112.9 16.2 %collective-permute-start.19 = (bf16[2,256,256]{2,1,0:T(8,128)(2,1)S(1)}, bf16[2,256,256]{2,1,0:T(8,128)(2,1)S(1)}, u32[]{:S(2)}, u32[]{:S(2)}) collective-permute-start(bf16[2,256,256]{2,1,0:T(8,128)(2,1)S(1)} %copy-done.29), channel_id=1, source_target_pairs={{0,16},{4,20},{8,24},{12,28},{16,0},{20,4},{24,8},{28,12},{1,17},{... | collective-permute-start | bytes 786440 | tf_op jit(solution)/shard_map/ppermute | solution.py:295
  129.3 21.7 %collective-permute-start.21 = (bf16[4,256,256]{2,1,0:T(8,128)(2,1)S(1)}, bf16[4,256,256]{2,1,0:T(8,128)(2,1)S(1)}, u32[]{:S(2)}, u32[]{:S(2)}) collective-permute-start(bf16[4,256,256]{2,1,0:T(8,128)(2,1)S(1)} %pad_maximum_fusion), channel_id=1, source_target_pairs={{0,4},{4,0},{8,12},{12,8},{16,20},{20,16},{24,28},{28,24},{1,5},{5... | collective-permute-start | bytes 1572872 | tf_op jit(solution)/shard_map/ppermute | solution.py:291
  130.8 13.6 %collective-permute-start.28 = (bf16[4,32,256]{2,1,0:T(8,128)(2,1)S(1)}, bf16[4,32,256]{2,1,0:T(8,128)(2,1)S(1)}, u32[]{:S(2)}, u32[]{:S(2)}) collective-permute-start(bf16[4,32,256]{2,1,0:T(8,128)(2,1)S(1)} %pad_maximum_fusion.2), channel_id=1, source_target_pairs={{0,4},{4,0},{8,12},{12,8},{16,20},{20,16},{24,28},{28,24},{1,5},{5... | collective-permute-start | bytes 196616 | tf_op jit(solution)/shard_map/ppermute | solution.py:291
  144.4 5.0 %collective-permute-start.30 = (bf16[8,32,256]{2,1,0:T(8,128)(2,1)S(1)}, bf16[8,32,256]{2,1,0:T(8,128)(2,1)S(1)}, u32[]{:S(2)}, u32[]{:S(2)}) collective-permute-start(bf16[8,32,256]{2,1,0:T(8,128)(2,1)S(1)} %constant_dynamic-update-slice_fusion.1.f0), channel_id=1, source_target_pairs={{0,2},{1,3},{2,0},{3,1},{4,6},{5,7},{6,4},{7,5},{8,10},{9,11},{10,... | collective-permute-start | bytes 393224 | tf_op jit(solution)/shard_map/ppermute | solution.py:288
  146.0 13.1 %collective-permute-start.32 = (bf16[128,1152]{1,0:T(8,128)(2,1)S(1)}, bf16[128,1152]{1,0:T(8,128)(2,1)}, u32[]{:S(2)}, u32[]{:S(2)}) collective-permute-start(bf16[128,1152]{1,0:T(8,128)(2,1)S(1)} %copy-done.5), channel_id=1, source_target_pairs={{0,8},{4,12},{8,16},{12,20},{16,24},{20,28},{24,0},{28,4},{1,9},{5... | collective-permute-start | bytes 884744 | tf_op jit(solution)/shard_map/ppermute | solution.py:295
  147.7 1.2 collective-permute-start.16
  148.8 5.8 %collective-permute-start.29 = (bf16[8,32,256]{2,1,0:T(8,128)(2,1)S(1)}, bf16[8,32,256]{2,1,0:T(8,128)(2,1)S(1)}, u32[]{:S(2)}, u32[]{:S(2)}) collective-permute-start(bf16[8,32,256]{2,1,0:T(8,128)(2,1)S(1)} %constant_dynamic-update-slice_fusion.1.f0), channel_id=1, source_target_pairs={{0,1},{1,0},{2,3},{3,2},{4,5},{5,4},{6,7},{7,6},{8,9},{9,8},{10,11... | collective-permute-start | bytes 393224 | tf_op jit(solution)/shard_map/ppermute | solution.py:288
  149.5 3.6 %collective-permute-start.17 = (f32[4,256]{1,0:T(4,128)S(1)}, f32[4,256]{1,0:T(4,128)S(1)}, u32[]{:S(2)}, u32[]{:S(2)}) collective-permute-start(f32[4,256]{1,0:T(4,128)S(1)} %add.112), channel_id=1, source_target_pairs={{0,2},{1,3},{2,0},{3,1},{4,6},{5,7},{6,4},{7,5},{8,10},{9,11},{10,... | collective-permute-start | bytes 12296 | tf_op jit(solution)/shard_map/ppermute | solution.py:288
  151.0 5.6 %collective-permute-start.31 = (bf16[8,32,256]{2,1,0:T(8,128)(2,1)S(1)}, bf16[8,32,256]{2,1,0:T(8,128)(2,1)S(1)}, u32[]{:S(2)}, u32[]{:S(2)}) collective-permute-start(bf16[8,32,256]{2,1,0:T(8,128)(2,1)S(1)} %collective-permute-done.30.f2), channel_id=1, source_target_pairs={{0,1},{1,0},{2,3},{3,2},{4,5},{5,4},{6,7},{7,6},{8,9},{9,8},{10,11... | collective-permute-start | bytes 393224 | tf_op jit(solution)/shard_map/ppermute | solution.py:288
  151.0 78.9 %copy-start.3 = (bf16[8,256,256]{2,1,0:T(8,128)(2,1)}, bf16[8,256,256]{2,1,0:T(8,128)(2,1)S(1)}, u32[]{:S(2)}) copy-start(bf16[8,256,256]{2,1,0:T(8,128)(2,1)S(1)} %constant_dynamic-update-slice_fusion.b0) | copy-start | bytes 3145732
  151.0 76.0 %copy-start.6 = (bf16[1024,512]{1,0:T(8,128)(2,1)S(1)}, bf16[1024,512]{1,0:T(8,128)(2,1)}, u32[]{:S(2)}) copy-start(bf16[1024,512]{1,0:T(8,128)(2,1)} %get-tuple-element.35) | copy-start | bytes 3145732
  153.1 57.5 %collective-permute-start.23 = (bf16[8,256,256]{2,1,0:T(8,128)(2,1)S(1)}, bf16[8,256,256]{2,1,0:T(8,128)(2,1)}, u32[]{:S(2)}, u32[]{:S(2)}) collective-permute-start(bf16[8,256,256]{2,1,0:T(8,128)(2,1)S(1)} %constant_dynamic-update-slice_fusion.b0), channel_id=1, source_target_pairs={{0,2},{1,3},{2,0},{3,1},{4,6},{5,7},{6,4},{7,5},{8,10},{9,11},{10,... | collective-permute-start | bytes 3145736 | tf_op jit(solution)/shard_map/ppermute | solution.py:288
  154.6 15.5 %collective-permute-start.33 = (bf16[128,1152]{1,0:T(8,128)(2,1)S(1)}, bf16[128,1152]{1,0:T(8,128)(2,1)}, u32[]{:S(2)}, u32[]{:S(2)}) collective-permute-start(bf16[128,1152]{1,0:T(8,128)(2,1)S(1)} %copy-done.5), channel_id=1, source_target_pairs={{0,16},{4,20},{8,24},{12,28},{16,0},{20,4},{24,8},{28,12},{1,17},{... | collective-permute-start | bytes 884744 | tf_op jit(solution)/shard_map/ppermute | solution.py:295
  156.6 19.4 %collective-permute-start.34 = (bf16[128,1152]{1,0:T(8,128)(2,1)S(1)}, bf16[128,1152]{1,0:T(8,128)(2,1)S(1)}, u32[]{:S(2)}, u32[]{:S(2)}) collective-permute-start(bf16[128,1152]{1,0:T(8,128)(2,1)S(1)} %copy-done.5), channel_id=1, source_target_pairs={{0,24},{4,28},{8,0},{12,4},{16,8},{20,12},{24,16},{28,20},{1,25},{... | collective-permute-start | bytes 884744 | tf_op jit(solution)/shard_map/ppermute | solution.py:295
  159.1 20.3 %collective-permute-start.35 = (bf16[128,1152]{1,0:T(8,128)(2,1)S(1)}, bf16[128,1152]{1,0:T(8,128)(2,1)S(1)}, u32[]{:S(2)}, u32[]{:S(2)}) collective-permute-start(bf16[128,1152]{1,0:T(8,128)(2,1)S(1)} %copy-done.5), channel_id=1, source_target_pairs={{0,4},{4,0},{8,12},{12,8},{16,20},{20,16},{24,28},{28,24},{1,5},{5... | collective-permute-start | bytes 884744 | tf_op jit(solution)/shard_map/ppermute | solution.py:291
  170.1 16.8 %collective-permute-start.39 = (bf16[128,1152]{1,0:T(8,128)(2,1)S(1)}, bf16[128,1152]{1,0:T(8,128)(2,1)S(1)}, u32[]{:S(2)}, u32[]{:S(2)}) collective-permute-start(bf16[128,1152]{1,0:T(8,128)(2,1)S(1)} %copy-done.11), channel_id=1, source_target_pairs={{0,8},{4,12},{8,16},{12,20},{16,24},{20,28},{24,0},{28,4},{1,9},{5... | collective-permute-start | bytes 884744 | tf_op jit(solution)/shard_map/ppermute | solution.py:295
  176.0 22.8 %collective-permute-start.40 = (bf16[128,1152]{1,0:T(8,128)(2,1)S(1)}, bf16[128,1152]{1,0:T(8,128)(2,1)S(1)}, u32[]{:S(2)}, u32[]{:S(2)}) collective-permute-start(bf16[128,1152]{1,0:T(8,128)(2,1)S(1)} %copy-done.11), channel_id=1, source_target_pairs={{0,16},{4,20},{8,24},{12,28},{16,0},{20,4},{24,8},{28,12},{1,17},{... | collective-permute-start | bytes 884744 | tf_op jit(solution)/shard_map/ppermute | solution.py:295
  179.5 20.9 %collective-permute-start.41 = (bf16[128,1152]{1,0:T(8,128)(2,1)S(1)}, bf16[128,1152]{1,0:T(8,128)(2,1)S(1)}, u32[]{:S(2)}, u32[]{:S(2)}) collective-permute-start(bf16[128,1152]{1,0:T(8,128)(2,1)S(1)} %copy-done.11), channel_id=1, source_target_pairs={{0,24},{4,28},{8,0},{12,4},{16,8},{20,12},{24,16},{28,20},{1,25},{... | collective-permute-start | bytes 884744 | tf_op jit(solution)/shard_map/ppermute | solution.py:295
  179.5 22.3 %collective-permute-start.42 = (bf16[128,1152]{1,0:T(8,128)(2,1)S(1)}, bf16[128,1152]{1,0:T(8,128)(2,1)S(1)}, u32[]{:S(2)}, u32[]{:S(2)}) collective-permute-start(bf16[128,1152]{1,0:T(8,128)(2,1)S(1)} %copy-done.11), channel_id=1, source_target_pairs={{0,4},{4,0},{8,12},{12,8},{16,20},{20,16},{24,28},{28,24},{1,5},{5... | collective-permute-start | bytes 884744 | tf_op jit(solution)/shard_map/ppermute | solution.py:291
  186.8 38.1 %collective-permute-start.13 = (bf16[1024,512]{1,0:T(8,128)(2,1)}, bf16[1024,512]{1,0:T(8,128)(2,1)}, u32[]{:S(2)}, u32[]{:S(2)}) collective-permute-start(bf16[1024,512]{1,0:T(8,128)(2,1)} %get-tuple-element.36), channel_id=1, source_target_pairs={{0,1},{1,0},{2,3},{3,2},{4,5},{5,4},{6,7},{7,6},{8,9},{9,8},{10,11... | collective-permute-start | bytes 3145736 | tf_op jit(solution)/shard_map/ppermute | solution.py:288
  198.8 26.7 %collective-permute-start.15 = (bf16[1024,512]{1,0:T(8,128)(2,1)}, bf16[1024,512]{1,0:T(8,128)(2,1)}, u32[]{:S(2)}, u32[]{:S(2)}) collective-permute-start(bf16[1024,512]{1,0:T(8,128)(2,1)} %add_convert_fusion), channel_id=1, source_target_pairs={{0,2},{1,3},{2,0},{3,1},{4,6},{5,7},{6,4},{7,5},{8,10},{9,11},{10,... | collective-permute-start | bytes 3145736 | tf_op jit(solution)/shard_map/ppermute | solution.py:288
  200.3 10.2 %collective-permute-start.36 = (bf16[128,1152]{1,0:T(8,128)(2,1)}, bf16[128,1152]{1,0:T(8,128)(2,1)}, u32[]{:S(2)}, u32[]{:S(2)}) collective-permute-start(bf16[128,1152]{1,0:T(8,128)(2,1)} %collective-permute-done.32.refs_1_), channel_id=1, source_target_pairs={{0,4},{4,0},{8,12},{12,8},{16,20},{20,16},{24,28},{28,24},{1,5},{5... | collective-permute-start | bytes 884744 | tf_op jit(solution)/shard_map/ppermute | solution.py:291
  201.8 13.7 %collective-permute-start.37 = (bf16[128,1152]{1,0:T(8,128)(2,1)}, bf16[128,1152]{1,0:T(8,128)(2,1)}, u32[]{:S(2)}, u32[]{:S(2)}) collective-permute-start(bf16[128,1152]{1,0:T(8,128)(2,1)} %collective-permute-done.33.refs_2_), channel_id=1, source_target_pairs={{0,4},{4,0},{8,12},{12,8},{16,20},{20,16},{24,28},{28,24},{1,5},{5... | collective-permute-start | bytes 884744 | tf_op jit(solution)/shard_map/ppermute | solution.py:291
  210.6 32.5 %collective-permute-start.22 = (bf16[8,256,256]{2,1,0:T(8,128)(2,1)S(1)}, bf16[8,256,256]{2,1,0:T(8,128)(2,1)}, u32[]{:S(2)}, u32[]{:S(2)}) collective-permute-start(bf16[8,256,256]{2,1,0:T(8,128)(2,1)S(1)} %constant_dynamic-update-slice_fusion.b0), channel_id=1, source_target_pairs={{0,1},{1,0},{2,3},{3,2},{4,5},{5,4},{6,7},{7,6},{8,9},{9,8},{10,11... | collective-permute-start | bytes 3145736 | tf_op jit(solution)/shard_map/ppermute | solution.py:288
  210.6 32.5 %collective-permute-start.24 = (bf16[8,256,256]{2,1,0:T(8,128)(2,1)}, bf16[8,256,256]{2,1,0:T(8,128)(2,1)}, u32[]{:S(2)}, u32[]{:S(2)}) collective-permute-start(bf16[8,256,256]{2,1,0:T(8,128)(2,1)} %collective-permute-done.23.b2), channel_id=1, source_target_pairs={{0,1},{1,0},{2,3},{3,2},{4,5},{5,4},{6,7},{7,6},{8,9},{9,8},{10,11... | collective-permute-start | bytes 3145736 | tf_op jit(solution)/shard_map/ppermute | solution.py:288
  215.5 8.0 %collective-permute-start.38 = (bf16[128,1152]{1,0:T(8,128)(2,1)}, bf16[128,1152]{1,0:T(8,128)(2,1)}, u32[]{:S(2)}, u32[]{:S(2)}) collective-permute-start(bf16[128,1152]{1,0:T(8,128)(2,1)} %copy-done.12), channel_id=1, source_target_pairs={{0,4},{4,0},{8,12},{12,8},{16,20},{20,16},{24,28},{28,24},{1,5},{5... | collective-permute-start | bytes 884744 | tf_op jit(solution)/shard_map/ppermute | solution.py:291
  223.5 10.2 %collective-permute-start.43 = (bf16[128,1152]{1,0:T(8,128)(2,1)}, bf16[128,1152]{1,0:T(8,128)(2,1)S(1)}, u32[]{:S(2)}, u32[]{:S(2)}) collective-permute-start(bf16[128,1152]{1,0:T(8,128)(2,1)} %copy-done.14), channel_id=1, source_target_pairs={{0,4},{4,0},{8,12},{12,8},{16,20},{20,16},{24,28},{28,24},{1,5},{5... | collective-permute-start | bytes 884744 | tf_op jit(solution)/shard_map/ppermute | solution.py:291
  225.0 14.9 %collective-permute-start.44 = (bf16[128,1152]{1,0:T(8,128)(2,1)}, bf16[128,1152]{1,0:T(8,128)(2,1)S(1)}, u32[]{:S(2)}, u32[]{:S(2)}) collective-permute-start(bf16[128,1152]{1,0:T(8,128)(2,1)} %copy-done.15), channel_id=1, source_target_pairs={{0,4},{4,0},{8,12},{12,8},{16,20},{20,16},{24,28},{28,24},{1,5},{5... | collective-permute-start | bytes 884744 | tf_op jit(solution)/shard_map/ppermute | solution.py:291
  225.5 17.6 %collective-permute-start.45 = (bf16[128,1152]{1,0:T(8,128)(2,1)}, bf16[128,1152]{1,0:T(8,128)(2,1)S(1)}, u32[]{:S(2)}, u32[]{:S(2)}) collective-permute-start(bf16[128,1152]{1,0:T(8,128)(2,1)} %copy-done.16), channel_id=1, source_target_pairs={{0,4},{4,0},{8,12},{12,8},{16,20},{20,16},{24,28},{28,24},{1,5},{5... | collective-permute-start | bytes 884744 | tf_op jit(solution)/shard_map/ppermute | solution.py:291
  (28 other events, 634.0 us)

commit v2 on v0

v2 whole, which is shorter than its diff:
```python
import functools

import jax
import jax.numpy as jnp
from jax import lax
from jax.experimental import pallas as pl
from jax.experimental.pallas import tpu as pltpu
from jax.sharding import PartitionSpec as P

HEAD = 128
BF = jnp.bfloat16
F32 = jnp.float32
VMEM = pl.BlockSpec(memory_space=pltpu.VMEM)
SMEM = pl.BlockSpec(memory_space=pltpu.SMEM)
LIMIT = 56 * 2**20
SCALE = 1.15e9


def dot(left, right):
    return jnp.dot(left, right, preferred_element_type=F32)


def tdot(left, right):
    return lax.dot_general(left, right, (((0,), (0,)), ((), ())), preferred_element_type=F32)


def rdot(left, right):
    return lax.dot_general(left, right, (((1,), (1,)), ((), ())), preferred_element_type=F32)


class Later:
    def __init__(self, copy, ref):
        self.copy, self.ref = copy, ref

    def get(self):
        if self.copy is not None:
            self.copy.wait()
            self.copy = None
        return self.ref


def get(ref):
    return ref.get() if isinstance(ref, Later) else ref


def call(body, ins, outs, micros, scratch=(), later=()):
    n_in, n_out, n_later = len(ins), len(outs), len(later)

    def kernel(*refs):
        given = list(refs[:n_in])
        rest = refs[n_in + n_out:]
        for j, i in enumerate(later):
            copy = pltpu.make_async_copy(given[i], rest[j], rest[n_later].at[j])
            copy.start()
            given[i] = Later(copy, rest[j])
        body(*given, *refs[n_in:n_in + n_out], *rest[n_later + (n_later > 0):])
        for j, i in enumerate(later):
            given[i].get()

    specs = [VMEM] * n_in
    specs[0] = SMEM
    for i in later:
        specs[i] = pl.BlockSpec(memory_space=pl.ANY)
    buffers = [pltpu.VMEM(ins[i].shape, ins[i].dtype) for i in later]
    if later:
        buffers.append(pltpu.SemaphoreType.DMA((n_later,)))
    return pl.pallas_call(
        kernel,
        in_specs=specs,
        out_specs=[VMEM] * len(outs),
        out_shape=[jax.ShapeDtypeStruct(s, t) for s, t in outs],
        scratch_shapes=[*buffers, *scratch],
        compiler_params=pltpu.CompilerParams(vmem_limit_bytes=LIMIT),
        cost_estimate=pl.CostEstimate(
            flops=int(micros * SCALE), bytes_accessed=0, transcendentals=0
        ),
    )(*ins)


def sums_kernel(n_out, other, idx, owned, occ, grads, out):
    z, x = idx[1], idx[2]
    f_dev = out.shape[0] // n_out
    side = 1 - x if other else x
    at = [pl.ds(pl.multiple_of(((z ^ k) * 2 + side) * f_dev, f_dev), f_dev) for k in range(n_out)]
    owners = jnp.concatenate([owned[a, :] for a in at], axis=0)
    onehot = jnp.where(owners == occ[...], 1.0, 0.0).astype(BF)
    out[...] = dot(onehot, get(grads)[...]).astype(out.dtype)


def norm_kernel(idx, x0, x1, x2, x3, gain, normed, recip, *sends):
    m, z, step = idx[0], idx[1], pl.program_id(0)
    tile, cols = x0.shape
    width = 4 * cols
    blocks = [block[...].astype(F32) for block in (x0, x1, x2, x3)]
    total = sum(jnp.sum(block * block, axis=1, keepdims=True) for block in blocks)
    r = lax.rsqrt(total * (1.0 / width) + 1e-06)
    recip[...] = r
    for k, block in enumerate(blocks):
        lanes = pl.ds(pl.multiple_of((m ^ k) * cols, cols), cols)
        normed[:, lanes] = (block * r * gain[:, lanes]).astype(BF)
    per = sends[0].shape[0] // tile

    @pl.when(step // per == m)
    def _():
        at = pl.ds(pl.multiple_of(lax.rem(step, per) * tile, tile), tile)
        for k, send in enumerate(sends):
            send[at, :] = normed[:, pl.ds(pl.multiple_of((z ^ k) * cols, cols), cols)]


def normalize(idx, blocks, gain, n_out):
    rows, cols = blocks[0].shape
    width = 4 * cols
    tile = 128
    quarter = rows // 4
    return pl.pallas_call(
        norm_kernel,
        grid_spec=pltpu.PrefetchScalarGridSpec(
            num_scalar_prefetch=1,
            grid=(rows // tile,),
            in_specs=[pl.BlockSpec((tile, cols), lambda i, idx: (i, 0))] * 4
            + [pl.BlockSpec((1, width), lambda i, idx: (0, 0))],
            out_specs=[
                pl.BlockSpec((tile, width), lambda i, idx: (i, 0)),
                pl.BlockSpec((tile, 1), lambda i, idx: (i, 0)),
            ]
            + [pl.BlockSpec((quarter, cols), lambda i, idx: (0, 0))] * n_out,
        ),
        out_shape=[
            jax.ShapeDtypeStruct((rows, width), BF),
            jax.ShapeDtypeStruct((rows, 1), F32),
        ]
        + [jax.ShapeDtypeStruct((quarter, cols), BF)] * n_out,
        compiler_params=pltpu.CompilerParams(vmem_limit_bytes=LIMIT),
        cost_estimate=pl.CostEstimate(flops=int(5 * SCALE), bytes_accessed=0, transcendentals=0),
    )(idx, *blocks, gain)


def diagonal(f_quarter, flen):
    rows = lax.broadcasted_iota(jnp.int32, (f_quarter, f_quarter * flen), 0)
    lanes = lax.broadcasted_iota(jnp.int32, (f_quarter, f_quarter * flen), 1)
    return rows == lanes // flen


def fold(which, lanes, flen):
    rows = lax.broadcasted_iota(jnp.int32, (lanes, 128), 0)
    to = lax.broadcasted_iota(jnp.int32, (lanes, 128), 1)
    return jnp.where(to == lax.rem(rows, flen) + which * flen, 1.0, 0.0).astype(BF)


def forward_kernel(flen, idx, normed, w_query, w_key, w_value, kmask, lmask,
                   early, probs, raw, upro, last, mixed):
    cols = w_query.ref.shape[1]
    heads = cols // HEAD
    normed = get(normed)
    rows = normed.shape[0] // 4
    fq = rows // flen
    scale = 1.0 / HEAD**0.5
    diag = diagonal(fq, flen)
    some = [slice(i * fq, (i + 1) * fq) for i in range(4)]

    for i in range(4):
        select = jnp.where(diag, lmask[i], 0.0).astype(BF)
        last[some[i], :] = dot(select, normed[i * rows:(i + 1) * rows, :]).astype(BF)
    query = dot(last[...], get(w_query)[...]).astype(BF)
    early[:, 0:cols] = query
    w_key = get(w_key)
    for h in range(heads):
        at = slice(h * HEAD, (h + 1) * HEAD)
        up = rdot(query[:, at], w_key[:, at]).astype(BF)
        for i in range(4):
            upro[i, some[h], :] = up[some[i], :]
    for i in range(4):
        part = normed[i * rows:(i + 1) * rows, :]
        score = rdot(upro[i], part)
        mask = jnp.concatenate([jnp.where(diag, kmask[i], 0.0)] * heads, axis=0) > 0.0
        expo = jnp.where(mask, jnp.exp(score * scale), 0.0)
        prob = expo / jnp.sum(expo, axis=1, keepdims=True)
        raw[i] = score
        probs[i] = prob
        prob_b = prob.astype(BF)
        mix = dot(prob_b, part).astype(BF)
        select = jnp.where(diag, lmask[i], 0.0).astype(BF)
        coef = dot(select, fold(2 * heads, rows, flen))
        for h in range(heads):
            mixed[h, some[i], :] = mix[some[h], :]
            coef = coef + dot(prob_b[some[h], :], fold(h, rows, flen))
        early[some[i], 2 * cols:2 * cols + 128] = coef.astype(BF)
    w_value = get(w_value)
    for h in range(heads):
        at = slice(h * HEAD, (h + 1) * HEAD)
        early[:, cols + h * HEAD:cols + (h + 1) * HEAD] = dot(mixed[h], w_value[:, at]).astype(BF)


def scores_kernel(flen, idx, normed, w_key, w_value, w_out, lmask, g0, g1, g2, g3, early, probs, raw,
                  late, product, tpro, dscore, probs_b, mixed):
    m = idx[0]
    cols = w_key.ref.shape[1]
    heads = cols // HEAD
    rows = normed.ref.shape[0] // 4
    fq = rows // flen
    scale = 1.0 / HEAD**0.5
    diag = diagonal(fq, flen)
    some = [slice(i * fq, (i + 1) * fq) for i in range(4)]

    d_att = jnp.zeros((4 * fq, cols), F32)
    w_out = get(w_out)
    for k, block in enumerate((g0, g1, g2, g3)):
        lanes = pl.ds(pl.multiple_of((m ^ k) * cols, cols), cols)
        d_att = d_att + rdot(block[...], w_out[:, lanes])
    d_att = d_att.astype(BF)
    late[:, 0:cols] = d_att
    w_value = get(w_value)
    for h in range(heads):
        at = slice(h * HEAD, (h + 1) * HEAD)
        up = rdot(d_att[:, at], w_value[:, at]).astype(BF)
        for i in range(4):
            tpro[i, some[h], :] = up[some[i], :]
    prods = []
    normed = get(normed)
    for i in range(4):
        part = normed[i * rows:(i + 1) * rows, :]
        d_prob = rdot(tpro[i], part)
        prob = get(probs)[i]
        d_score = prob * (d_prob - jnp.sum(prob * d_prob, axis=1, keepdims=True)) * scale
        score_b = d_score.astype(BF)
        prob_b = prob.astype(BF)
        dscore[i] = score_b
        probs_b[i] = prob_b
        inner = d_score * get(raw)[i] + prob_b.astype(F32) * d_prob
        prods.append(jnp.sum(inner, axis=0, keepdims=True))
        mix = dot(score_b, part).astype(BF)
        coef = jnp.zeros((fq, 128), F32)
        for h in range(heads):
            mixed[h, some[i], :] = mix[some[h], :]
            coef = coef + dot(score_b[some[h], :], fold(heads + h, rows, flen))
        late[some[i], 2 * cols:2 * cols + 128] = coef.astype(BF)
    parts = []
    w_key = get(w_key)
    for h in range(heads):
        at = slice(h * HEAD, (h + 1) * HEAD)
        parts.append(dot(mixed[h], w_key[:, at]))
    d_query = jnp.concatenate(parts, axis=1).astype(BF)
    late[:, cols:2 * cols] = d_query
    inner = early[:, 0:cols].astype(F32) * d_query.astype(F32)
    inner = jnp.sum(inner, axis=1, keepdims=True)
    for i in range(4):
        select = jnp.where(diag, lmask[i], 0.0)
        product[i:i + 1, :] = prods[i] + jnp.sum(select * inner[some[i], :], axis=0, keepdims=True)


def normed_kernel(flen, idx, w_query, lmask, late, upro, tpro, dscore, probs_b, d0, d1, d2, d3, vpro):
    m = idx[0]
    rows = dscore.shape[2]
    fq = rows // flen
    cols = d0.shape[1]
    diag = diagonal(fq, flen)
    vpro[...] = rdot(late[:, cols:2 * cols], get(w_query)[...]).astype(BF)
    upro, tpro = get(upro), get(tpro)
    for i in range(4):
        select = jnp.where(diag, lmask[i], 0.0).astype(BF)
        left = jnp.concatenate([dscore[i], probs_b[i], select], axis=0)
        for k, out in enumerate((d0, d1, d2, d3)):
            lanes = pl.ds(pl.multiple_of((m ^ k) * cols, cols), cols)
            right = jnp.concatenate(
                [upro[i, :, lanes], tpro[i, :, lanes], vpro[i * fq:(i + 1) * fq, lanes]], axis=0
            )
            out[i * rows:(i + 1) * rows, :] = tdot(left, right).astype(BF)


def out_kernel(idx, g0, g1, g2, g3, e0, e1, e2, e3, mine, other, att):
    m, z, x = idx[0], idx[1], idx[2]
    cols = mine.shape[0]
    half = mine.shape[1]
    for s, early in enumerate((e0, e1, e2, e3)):
        att[s] = get(early)[:, cols:2 * cols]
    for k, grads in enumerate((g0, g1, g2, g3)):
        left = att[(z ^ m) ^ k]
        own = tdot(left, grads[:, pl.ds(pl.multiple_of(x * half, half), half)])
        far = tdot(left, grads[:, pl.ds(pl.multiple_of((1 - x) * half, half), half)])
        mine[...] = own if k == 0 else mine[...] + own
        total = far if k == 0 else total + far
    other[...] = total.astype(BF)


def mix_rows(coef, normed, parts, flen):
    rows = normed.shape[0]
    fq = rows // flen
    diag = jnp.where(diagonal(fq, flen), 1.0, 0.0)
    spread = jnp.concatenate([fold(p, rows, flen).T for p in parts], axis=1)
    wide = dot(coef, spread)
    left = [(wide[:, j * rows:(j + 1) * rows] * diag).astype(BF) for j in range(len(parts))]
    return dot(jnp.concatenate(left, axis=0), normed).astype(BF)


def value_kernel(flen, heads, idx, b0, b1, b2, b3, *refs):
    early, late = refs[:4], refs[4:8]
    mine, other, z_all, d_all = refs[8:]
    m, x = idx[0], idx[2]
    rows = b0.ref.shape[1]
    fq = rows // flen
    cols = mine.shape[1]
    half = mine.shape[0]
    for k, normed in enumerate((b0, b1, b2, b3)):
        at = pl.ds(pl.multiple_of((m ^ k) * fq, fq), fq)
        for s in range(4):
            to = slice((k * 4 + s) * fq, (k * 4 + s + 1) * fq)
            coef = get(early[s])[at, 2 * cols:2 * cols + 128]
            mix = mix_rows(coef, get(normed)[s], range(heads), flen)
            for p in range(heads):
                z_all[p, to, :] = mix[p * fq:(p + 1) * fq, :]
            d_all[to, :] = get(late[s])[at, 0:cols]
    for h in range(heads):
        lanes = slice(h * HEAD, (h + 1) * HEAD)
        own = pl.ds(pl.multiple_of(x * half, half), half)
        far = pl.ds(pl.multiple_of((1 - x) * half, half), half)
        mine[:, lanes] = tdot(z_all[h, :, own], d_all[:, lanes])
        other[:, lanes] = tdot(z_all[h, :, far], d_all[:, lanes]).astype(BF)


def key_kernel(flen, heads, idx, b0, b1, b2, b3, *refs):
    early, late = refs[:4], refs[4:8]
    key_mine, query_mine, other, z_all, q_all, d_all = refs[8:]
    m, x = idx[0], idx[2]
    rows = b0.ref.shape[1]
    fq = rows // flen
    cols = key_mine.shape[1]
    half = key_mine.shape[0]
    for k, normed in enumerate((b0, b1, b2, b3)):
        at = pl.ds(pl.multiple_of((m ^ k) * fq, fq), fq)
        for s in range(4):
            to = slice((k * 4 + s) * fq, (k * 4 + s + 1) * fq)
            first, second = get(early[s]), get(late[s])
            coef = first[at, 2 * cols:2 * cols + 128] + second[at, 2 * cols:2 * cols + 128]
            mix = mix_rows(coef, get(normed)[s], range(heads, 2 * heads + 1), flen)
            for p in range(heads + 1):
                z_all[p, to, :] = mix[p * fq:(p + 1) * fq, :]
            q_all[to, :] = first[at, 0:cols]
            d_all[to, :] = second[at, cols:2 * cols]
    own = pl.ds(pl.multiple_of(x * half, half), half)
    far = pl.ds(pl.multiple_of((1 - x) * half, half), half)
    for h in range(heads):
        lanes = slice(h * HEAD, (h + 1) * HEAD)
        key_mine[:, lanes] = tdot(z_all[h, :, own], q_all[:, lanes])
        other[0, :, lanes] = tdot(z_all[h, :, far], q_all[:, lanes]).astype(BF)
    query_mine[...] = tdot(z_all[heads, :, own], d_all[...])
    other[1] = tdot(z_all[heads, :, far], d_all[...]).astype(BF)


def on_device(tok_grad, occurrence, owned, token_ids, embeds, gain, w_query, w_key, w_value, w_out):
    n_tok = lax.axis_size("tok")
    n_out = n_tok // 2
    f_dev, flen = token_ids.shape
    width = gain.shape[0]
    cols = w_key.shape[1]
    rows = f_dev * flen
    feats = width // n_tok
    fq = f_dev // 4
    quarter = fq * flen
    heads = cols // HEAD
    m = lax.axis_index("mdl")
    t = lax.axis_index("tok")
    z, x = t // 2, t % 2
    idx = jnp.stack([m, z, x, t]).astype(jnp.int32)

    def flip(array, bit):
        return lax.ppermute(array, "mdl", [(i, i ^ bit) for i in range(4)])

    def swap(array):
        return lax.ppermute(array, "tok", [(i, i ^ 1) for i in range(n_tok)])

    def cross(array, k):
        return lax.ppermute(array, "tok", [(i, i ^ (2 * k)) for i in range(n_tok)])

    flat = embeds.reshape(rows, cols)
    flat2 = flip(flat, 2)

    owned_col = owned.reshape(-1, 1)
    occ_row = occurrence.reshape(1, -1)

    def sums(other, dtype):
        return call(
            functools.partial(sums_kernel, n_out, other),
            (idx, owned_col, occ_row, tok_grad),
            [((n_out * f_dev, cols), dtype)],
            4,
            later=(3,),
        )[0]

    took = swap(sums(True, BF))
    keep = sums(False, F32)
    flat1 = flip(flat, 1)
    both = (keep + took.astype(F32)).reshape(n_out, f_dev, cols)
    total = both[0]
    for k in range(1, n_out):
        total = total + cross(both[k].astype(BF), k).astype(F32)
    flat3 = flip(flat2, 1)
    gain_row = gain.reshape(1, width)
    normed, recip, *sends = normalize(idx, (flat, flat1, flat2, flat3), gain_row, n_out)
    grad0 = total.astype(BF)
    grad2 = flip(grad0, 2)
    grad1, grad3 = flip(grad0, 1), flip(grad2, 1)

    def share(whole):
        from2 = flip(whole, 2)
        return whole, flip(whole, 1), from2, flip(from2, 1)

    length = jnp.sum((token_ids != 0).astype(jnp.int32), axis=1)
    positions = jnp.arange(flen, dtype=jnp.int32)
    lastmask = (positions[None, :] == (length - 1)[:, None]).astype(F32)
    keymask = (positions[None, :] < length[:, None]).astype(F32)
    lmask = lastmask.reshape(4, 1, quarter)
    kmask = keymask.reshape(4, 1, quarter)

    normed_all = share(jnp.stack([sends[0]] + [cross(sends[k], k) for k in range(1, n_out)]))

    item = ((f_dev, 2 * cols + 128), BF)
    square = (4, heads * fq, quarter)
    tall = ((4, heads * fq, width), BF)
    early, probs, raw, upro = call(
        functools.partial(forward_kernel, flen),
        (idx, normed, w_query, w_key, w_value, kmask, lmask),
        [item, (square, F32), (square, F32), tall],
        11,
        [pltpu.VMEM((f_dev, width), BF), pltpu.VMEM((heads, f_dev, width), BF)],
        later=(1, 2, 3, 4),
    )

    def gather(own):
        one, two = cross(own, 1), cross(own, 2)
        return [own, one, two, cross(two, 1)]

    early_all = gather(early)

    pairs = []
    for a in range(n_out):
        for b in range(2):
            for c in range(4):
                pairs.append(((a * 2 + b) * 4 + c, (c * 2 + b) * 4 + a))
    grads_all = share(lax.ppermute(grad0, ("tok", "mdl"), pairs))

    late, product, tpro, dscore, probs_b = call(
        functools.partial(scores_kernel, flen),
        (idx, normed, w_key, w_value, w_out, lmask, grad0, grad1, grad2, grad3, early, probs, raw),
        [item, ((4, quarter), F32), tall, (square, BF), (square, BF)],
        10,
        [pltpu.VMEM((heads, f_dev, width), BF)],
        later=(4, 3, 1, 11, 12, 2),
    )
    late_all = gather(late)
    d0, d1, d2, d3 = call(
        functools.partial(normed_kernel, flen),
        (idx, w_query, lmask, late, upro, tpro, dscore, probs_b),
        [((rows, cols), BF)] * 4,
        8,
        [pltpu.VMEM((f_dev, width), BF)],
        later=(1, 4, 5),
    )

    out_mine, out_other = call(
        out_kernel,
        (idx, *grads_all, *early_all),
        [((cols, feats), F32), ((cols, feats), BF)],
        3,
        [pltpu.VMEM((4, f_dev, cols), BF)],
        later=(5, 6, 7, 8),
    )
    out_grad = out_mine + swap(out_other).astype(F32)
    f_all = n_out * f_dev
    value_mine, value_other = call(
        functools.partial(value_kernel, flen, heads),
        (idx, *normed_all, *early_all, *late_all),
        [((feats, cols), F32), ((feats, cols), BF)],
        5,
        [pltpu.VMEM((heads, f_all, 2 * feats), BF), pltpu.VMEM((f_all, cols), BF)],
        later=(5, 6, 7, 8, 9, 10, 11, 12, 1, 2, 3, 4),
    )
    value_grad = value_mine + swap(value_other).astype(F32)
    key_mine, query_mine, both_other = call(
        functools.partial(key_kernel, flen, heads),
        (idx, *normed_all, *early_all, *late_all),
        [((feats, cols), F32), ((feats, cols), F32), ((2, feats, cols), BF)],
        6,
        [
            pltpu.VMEM((heads + 1, f_all, 2 * feats), BF),
            pltpu.VMEM((f_all, cols), BF),
            pltpu.VMEM((f_all, cols), BF),
        ],
        later=(5, 6, 7, 8, 9, 10, 11, 12, 1, 2, 3, 4),
    )
    crossed = swap(both_other)
    key_grad = key_mine + crossed[0].astype(F32)
    query_grad = query_mine + crossed[1].astype(F32)

    product = product + flip(product, 1)
    product = product + flip(product, 2)
    own = d0.astype(F32) + flip(d1, 1).astype(F32)
    across = d2.astype(F32) + flip(d3, 1).astype(F32)
    summed = own + flip(across.astype(BF), 2).astype(F32)
    gain_mine = lax.dynamic_slice_in_dim(gain, m * cols, cols, 0)
    scaled = summed.reshape(f_dev, flen, cols) * gain_mine
    recip = recip.reshape(f_dev, flen, 1)
    weight = recip * recip * (product.reshape(f_dev, flen, 1) * (1.0 / width))
    result = recip * scaled - embeds.astype(F32) * weight
    result = result + jnp.where(lastmask[..., None] > 0, grad0.astype(F32)[:, None, :], 0.0)
    return (result.astype(BF), query_grad, key_grad, value_grad, out_grad)


def general(tok_grad, occurrence, owned, token_ids, embeds, gain, w_query, w_key, w_value, w_out):
    f32 = F32
    bf16 = BF
    n_tok = lax.axis_size("tok")
    fgrams = owned.shape[0]
    f_dev = fgrams // n_tok
    width = gain.shape[0]
    cols = w_key.shape[1]
    local_heads = cols // HEAD
    flen = token_ids.shape[1]
    scale = 1.0 / HEAD**0.5
    onehot = (owned[:, None] == occurrence[None, :]).astype(bf16)
    partial_sum = jnp.dot(onehot, tok_grad, preferred_element_type=f32)
    blocks = partial_sum.reshape(n_tok, f_dev, tok_grad.shape[1])
    arrived = lax.all_to_all(blocks, "tok", split_axis=0, concat_axis=0, tiled=True)
    fgram_sum = jnp.sum(arrived, axis=0)
    fgram_grad = fgram_sum.astype(bf16)
    full_grad = lax.all_gather(fgram_grad, "mdl", axis=1, tiled=True)
    whole_embeds = lax.all_gather(embeds, "mdl", axis=2, tiled=True)
    length = jnp.sum((token_ids != 0).astype(jnp.int32), axis=1)
    positions = jnp.arange(flen, dtype=jnp.int32)
    lastmask = positions[None, :] == (length - 1)[:, None]
    keymask = (positions[None, :] < length[:, None]).astype(f32)
    xfull = whole_embeds.astype(f32)
    recip = lax.rsqrt(jnp.mean(xfull * xfull, axis=-1) + 1e-06)
    normed = (xfull * recip[..., None] * gain).astype(bf16)
    normed_last = jnp.sum(jnp.where(lastmask[..., None], normed.astype(f32), 0.0), axis=1).astype(bf16)
    rows = normed.reshape(f_dev * flen, width)
    keys = dot(rows, w_key).astype(bf16).reshape(f_dev, flen, local_heads, HEAD)
    values = dot(rows, w_value).astype(bf16).reshape(f_dev, flen, local_heads, HEAD)
    query = dot(normed_last, w_query).astype(bf16).reshape(f_dev, local_heads, HEAD)
    keys32 = keys.astype(f32)
    values32 = values.astype(f32)
    query32 = query.astype(f32)
    scores = jnp.einsum("fhd,fjhd->fhj", query, keys, preferred_element_type=f32) * scale
    expo = jnp.exp(scores) * keymask[:, None, :]
    probs = expo / jnp.sum(expo, axis=-1, keepdims=True)
    probs_b = probs.astype(bf16)
    attended = jnp.einsum("fhj,fjhd->fhd", probs_b, values, preferred_element_type=f32)
    attended = attended.astype(bf16).reshape(f_dev, cols)
    d_att = rdot(full_grad, w_out).reshape(f_dev, local_heads, HEAD)
    d_prob = jnp.einsum("fhd,fjhd->fhj", d_att, values32)
    d_score = probs * (d_prob - jnp.sum(probs * d_prob, axis=-1, keepdims=True)) * scale
    d_query = jnp.einsum("fhj,fjhd->fhd", d_score, keys32).astype(bf16).reshape(f_dev, cols)
    d_key = jnp.einsum("fhj,fhd->fjhd", d_score, query32).astype(bf16).reshape(f_dev * flen, cols)
    d_value = jnp.einsum("fhj,fhd->fjhd", probs_b.astype(f32), d_att)
    d_value = d_value.astype(bf16).reshape(f_dev * flen, cols)
    d_normed = (rdot(d_key, w_key) + rdot(d_value, w_value)).reshape(f_dev, flen, width)
    from_query = rdot(d_query, w_query)
    d_normed = d_normed + jnp.where(lastmask[..., None], from_query[:, None, :], 0.0)
    feat_start = lax.axis_index("mdl") * embeds.shape[2]
    summed = lax.psum(d_normed, "mdl")
    scaled = summed * gain
    product = jnp.mean(xfull * scaled, axis=-1)
    result = recip[..., None] * scaled - xfull * (recip**3 * product)[..., None]
    result = lax.dynamic_slice_in_dim(result, feat_start, embeds.shape[2], 2)
    result = result + jnp.where(lastmask[..., None], fgram_grad.astype(f32)[:, None, :], 0.0)
    query_grad, key_grad, value_grad = (
        lax.psum_scatter(part, "tok", scatter_dimension=0, tiled=True)
        for part in (tdot(normed_last, d_query), tdot(rows, d_key), tdot(rows, d_value))
    )
    out_grad = lax.psum_scatter(tdot(attended, full_grad), "tok", scatter_dimension=1, tiled=True)
    return (result.astype(bf16), query_grad, key_grad, value_grad, out_grad)


def chosen(*args):
    fits = lax.axis_size("tok") == 8 and lax.axis_size("mdl") == 4
    return (on_device if fits else general)(*args)


def solution(mesh):
    return jax.shard_map(
        chosen,
        mesh=mesh,
        in_specs=(
            P("tok", "mdl"),
            P("tok"),
            P(),
            P("tok", None),
            P("tok", None, "mdl"),
            P(),
            P(None, "mdl"),
            P(None, "mdl"),
            P(None, "mdl"),
            P("mdl", None),
        ),
        out_specs=(
            P("tok", None, "mdl"),
            P("tok", "mdl"),
            P("tok", "mdl"),
            P("tok", "mdl"),
            P("mdl", "tok"),
        ),
        check_vma=False,
    )
```

time: 657 us -> 185 us (0.28)
  waiting for transfers between devices: 529 us -> 53.8 us
  Pallas kernels: 0 us -> 70.1 us
  matrix products: 45.6 us -> 0 us
  starting transfers between devices: 7.85 us -> 42.3 us
  other arithmetic: 32.9 us -> 10.5 us
  between operations: 14.5 us -> 1.13 us
  local copies, waits for them, and re-layouts: 18.8 us -> 6.03 us
  blocking collectives: 7.2 us -> 0 us
    reduce_scatter x4 -> x0, waiting for transfers between devices: 357 us -> none  [the longest x1 92.8 us: on_device(): lax.psum_scatter(out_part, 'tok', scatter_dimension=1, tiled=True)]
    psum x1 -> x0, waiting for transfers between devices: 124 us -> none  [on_device(): summed = lax.psum(d_normed, 'mdl')]
    pallas_call x0 -> x9, Pallas kernels: none -> 70.1 us  [the longest x8 61.1 us: call(): pl.pallas_call(kernel, in_specs=specs, out_specs=[VMEM] * len(outs), out_...]
    ppermute x0 -> x34, waiting for transfers between devices: none -> 53.8 us  [the longest x12 21.5 us: cross(): return lax.ppermute(array, 'tok', [(i, i ^ 2 * k) for i in range(n_tok)])]
    all_to_all x1 -> x0, waiting for transfers between devices: 48.1 us -> none  [on_device(): lax.all_to_all(blocks, 'tok', split_axis=0, concat_axis=0, tiled=True)]
    dot_general x16 -> x0, matrix products: 45.6 us -> none  [the longest x4 19.1 us: tdot(): lax.dot_general(left, right, (((0,), (0,)), ((), ())), preferred_element_...]
    ppermute x0 -> x34, starting transfers between devices: none -> 42.3 us  [the longest x12 19.7 us: cross(): return lax.ppermute(array, 'tok', [(i, i ^ 2 * k) for i in range(n_tok)])]
    reduce_sum x4 -> x0, other arithmetic: 19.2 us -> none  [the longest x1 9.11 us: on_device(): product = jnp.mean(xfull * scaled, axis=-1)]
  transfers between devices with their start and end apart: 7 -> 34, of which waited for: 6 -> 11; matrix products, arithmetic and copies ran while one was open for 10% -> 7% of each run, Pallas kernels for 0% -> 38%
where the time goes in v2:
time: 185 us; the launch traced here: 184 us
  Pallas kernels  70.1 us (38%)
  waiting for transfers between devices  53.8 us (29%)
  starting transfers between devices  42.3 us (23%)
  other arithmetic  10.5 us (6%)
  local copies, waits for them, and re-layouts  6.03 us (3%)
    pallas_call x8, Pallas kernels, call(): pl.pallas_call(kernel, in_specs=specs, out_specs=[VMEM] * len(outs), out_...  61.1 us
    ppermute x12, waiting for transfers between devices, cross(): return lax.ppermute(array, 'tok', [(i, i ^ 2 * k) for i in range(n_tok)])  21.5 us
    ppermute x12, starting transfers between devices, cross(): return lax.ppermute(array, 'tok', [(i, i ^ 2 * k) for i in range(n_tok)])  19.7 us
    ppermute x17, waiting for transfers between devices, flip(): return lax.ppermute(array, 'mdl', [(i, i ^ bit) for i in range(4)])  18.2 us
    ppermute x17, starting transfers between devices, flip(): return lax.ppermute(array, 'mdl', [(i, i ^ bit) for i in range(4)])  16.6 us
    ppermute x4, waiting for transfers between devices, swap(): return lax.ppermute(array, 'tok', [(i, i ^ 1) for i in range(n_tok)])  14.1 us
    pallas_call x1, Pallas kernels, normalize(): pl.pallas_call(norm_kernel, grid_spec=pltpu.PrefetchScalarGridSpec(num_sc...  9.02 us
    ppermute x4, starting transfers between devices, swap(): return lax.ppermute(array, 'tok', [(i, i ^ 1) for i in range(n_tok)])  5.27 us
  transfers between devices with their start and end apart: 34, of which 11 were waited for; matrix products, arithmetic and copies ran while one was open for 7% of the time, Pallas kernels for 38%

profile of v2, /device:TPU:0, one launch (start us, length us, event | category | flops | bytes accessed | tf_op | source)
XLA Modules:
  0.0 183.9 jit_solution(12016008830495732322)
XLA Ops:
  1.1 2.6 %collective-permute-start.1 = (bf16[1024,512]{1,0:T(8,128)(2,1)}, bf16[1024,512]{1,0:T(8,128)(2,1)S(1)}, u32[]{:S(2)}, u32[]{:S(2)}) collective-permute-start(bf16[1024,512]{1,0:T(8,128)(2,1)} %bitcast.33), channel_id=1, source_target_pairs={{0,2},{1,3},{2,0},{3,1},{4,6},{5,7},{6,4},{7,5},{8,10},{9,11},{10,... | collective-permute-start | bytes 3145736 | tf_op jit(solution)/shard_map/ppermute | solution.py:366
  3.7 1.7 copy.21.refs_1_
  5.5 0.7 pad_add_fusion.idx.refs_0_
  6.1 4.7 %shard_map.139 = bf16[512,512]{1,0:T(8,128)(2,1)} custom-call(s32[4]{0:T(128)} %pad_add_fusion.idx.refs_0_, s32[1024,1]{1,0:T(8,128)} %copy.21.refs_1_, s32[1,2048]{1,0:T(1,128)} %bitcast.41, bf16[2048,512]{1,0:T(8,128)(2,1)} %refs_3_.5), custom_call_target="tpu_custom_call" | custom-call | flops 4600000000 | tf_op jit(solution)/shard_map/pallas_call | solution.py:67
  10.8 1.6 collective-permute-start.3
  13.0 4.9 %shard_map.138 = f32[512,512]{1,0:T(8,128)} custom-call(s32[4]{0:T(128)} %pad_add_fusion.idx.refs_0_, s32[1024,1]{1,0:T(8,128)} %copy.21.refs_1_, s32[1,2048]{1,0:T(1,128)} %bitcast.42, bf16[2048,512]{1,0:T(8,128)(2,1)} %refs_3_.5), custom_call_target="tpu_custom_call" | custom-call | flops 4600000000 | tf_op jit(solution)/shard_map/pallas_call | solution.py:67
  17.9 9.9 %collective-permute-done.1.x2 = bf16[1024,512]{1,0:T(8,128)(2,1)S(1)} collective-permute-done((bf16[1024,512]{1,0:T(8,128)(2,1)}, bf16[1024,512]{1,0:T(8,128)(2,1)S(1)}, u32[]{:S(2)}, u32[]{:S(2)}) %collective-permute-start.1) | collective-permute-done | bytes 1048608 | tf_op jit(solution)/shard_map/ppermute | solution.py:366
  27.7 1.8 fusion.9
  29.6 3.9 %collective-permute-start.6 = (bf16[128,512]{1,0:T(8,128)(2,1)S(1)}, bf16[128,512]{1,0:T(8,128)(2,1)S(1)}, u32[]{:S(2)}, u32[]{:S(2)}) collective-permute-start(bf16[128,512]{1,0:T(8,128)(2,1)S(1)} %get-tuple-element.64), channel_id=1, source_target_pairs={{0,24},{4,28},{8,16},{12,20},{16,8},{20,12},{24,0},{28,4},{1,25},{... | collective-permute-start | bytes 393224 | tf_op jit(solution)/shard_map/ppermute | solution.py:372
  34.7 3.1 %collective-permute-done.6 = bf16[128,512]{1,0:T(8,128)(2,1)S(1)} collective-permute-done((bf16[128,512]{1,0:T(8,128)(2,1)S(1)}, bf16[128,512]{1,0:T(8,128)(2,1)S(1)}, u32[]{:S(2)}, u32[]{:S(2)}) %collective-permute-start.6) | collective-permute-done | bytes 131104 | tf_op jit(solution)/shard_map/ppermute | solution.py:372
  37.9 7.0 %collective-permute-done.5 = bf16[128,512]{1,0:T(8,128)(2,1)S(1)} collective-permute-done((bf16[128,512]{1,0:T(8,128)(2,1)S(1)}, bf16[128,512]{1,0:T(8,128)(2,1)S(1)}, u32[]{:S(2)}, u32[]{:S(2)}) %collective-permute-start.5) | collective-permute-done | bytes 131104 | tf_op jit(solution)/shard_map/ppermute | solution.py:372
  44.9 1.6 collective-permute-start.8
  46.5 0.7 collective-permute-start.29
  47.2 1.3 collective-permute-start.7
  48.5 1.5 collective-permute-done.8.refs_8_
  50.0 1.8 collective-permute-start.30
  51.8 1.0 copy-done.12
  53.1 9.0 %shard_map.137 = (bf16[1024,2048]{1,0:T(8,128)(2,1)}, f32[1024,1]{1,0:T(8,128)}, bf16[256,512]{1,0:T(8,128)(2,1)}, bf16[256,512]{1,0:T(8,128)(2,1)}, bf16[256,512]{1,0:T(8,128)(2,1)}, /*index=5*/bf16[256,512]{1,0:T(8,128)(2,1)}) custom-call(s32[4]{0:T(128)} %pad_add_fusion.idx.refs_0_, bf16[1024,512]{1,0:T(8,128)(2,1)} %bitcast.34, ...), custom_call_target="tpu_custom_call" | custom-call | flops 5750000128 | tf_op jit(solution)/shard_map/pallas_call | solution.py:115
  62.2 6.6 %collective-permute-start.17 = (bf16[256,512]{1,0:T(8,128)(2,1)}, bf16[256,512]{1,0:T(8,128)(2,1)S(1)}, u32[]{:S(2)}, u32[]{:S(2)}) collective-permute-start(bf16[256,512]{1,0:T(8,128)(2,1)} %get-tuple-element.49), channel_id=1, source_target_pairs={{0,24},{4,28},{8,16},{12,20},{16,8},{20,12},{24,0},{28,4},{1,25},{... | collective-permute-start | bytes 786440 | tf_op jit(solution)/shard_map/ppermute | solution.py:372
  68.8 11.2 %shard_map.140 = (bf16[128,1152]{1,0:T(8,128)(2,1)}, f32[4,128,256]{2,1,0:T(8,128)}, f32[4,128,256]{2,1,0:T(8,128)}, bf16[4,128,2048]{2,1,0:T(8,128)(2,1)}) custom-call(s32[4]{0:T(128)} %pad_add_fusion.idx.refs_0_, bf16[1024,2048]{1,0:T(8,128)(2,1)} %get-tuple-element.32.refs_1_, bf16[2048,512]{1,0:T(8,128)(2,1)} %refs_1_.1, bf16[2048,512]{1,0:T(8,128)(2,1)} %refs_2_.3, ...), custom_call_target="tpu_custom_call" | custom-call | flops 12650000384 | tf_op jit(solution)/shard_map/pallas_call | solution.py:67
  80.0 0.7 collective-permute-start.15
  80.7 2.4 %collective-permute-start.22 = (bf16[128,1152]{1,0:T(8,128)(2,1)}, bf16[128,1152]{1,0:T(8,128)(2,1)S(1)}, u32[]{:S(2)}, u32[]{:S(2)}) collective-permute-start(bf16[128,1152]{1,0:T(8,128)(2,1)} %get-tuple-element.33.refs_10_.refs_5_), channel_id=1, source_target_pairs={{0,16},{4,20},{8,24},{12,28},{16,0},{20,4},{24,8},{28,12},{1,17},{... | collective-permute-start | bytes 884744 | tf_op jit(solution)/shard_map/ppermute | solution.py:372
  83.1 11.6 %shard_map.141 = (bf16[128,1152]{1,0:T(8,128)(2,1)}, f32[4,256]{1,0:T(4,128)}, bf16[4,128,2048]{2,1,0:T(8,128)(2,1)}, bf16[4,128,256]{2,1,0:T(8,128)(2,1)}, bf16[4,128,256]{2,1,0:T(8,128)(2,1)}) custom-call(s32[4]{0:T(128)} %pad_add_fusion.idx.refs_0_, bf16[1024,2048]{1,0:T(8,128)(2,1)} %get-tuple-element.32.refs_1_, bf16[2048,512]{1,0:T(8,128)(2,1)} %refs_2_.3, ...), custom_call_target="tpu_custom_call" | custom-call | flops 11500000256 | tf_op jit(solution)/shard_map/pallas_call | solution.py:67
  94.8 1.5 collective-permute-start.31
  97.0 1.1 pad_maximum_fusion.refs_1_
  98.1 3.3 %collective-permute-start.19 = (bf16[4,256,512]{2,1,0:T(8,128)(2,1)}, bf16[4,256,512]{2,1,0:T(8,128)(2,1)}, u32[]{:S(2)}, u32[]{:S(2)}) collective-permute-start(bf16[4,256,512]{2,1,0:T(8,128)(2,1)} %pad_maximum_fusion.refs_1_), channel_id=1, source_target_pairs={{0,2},{1,3},{2,0},{3,1},{4,6},{5,7},{6,4},{7,5},{8,10},{9,11},{10,... | collective-permute-start | bytes 3145736 | tf_op jit(solution)/shard_map/ppermute | solution.py:366
  101.5 1.6 collective-permute-done.22.refs_7_
  103.4 8.3 %shard_map.142 = (bf16[1024,512]{1,0:T(8,128)(2,1)}, bf16[1024,512]{1,0:T(8,128)(2,1)}, bf16[1024,512]{1,0:T(8,128)(2,1)}, bf16[1024,512]{1,0:T(8,128)(2,1)}) custom-call(s32[4]{0:T(128)} %pad_add_fusion.idx.refs_0_, bf16[2048,512]{1,0:T(8,128)(2,1)} %refs_1_.1, f32[4,1,256]{2,1,0:T(1,128)} %get-tuple-element.67.refs_6_.refs_5_.refs_2_, ...), custom_call_target="tpu_custom_call" | custom-call | flops 9200000000 | tf_op jit(solution)/shard_map/pallas_call | solution.py:67
  112.3 1.3 dynamic_slice.3
  114.1 2.9 %collective-permute-start.25 = (bf16[128,1152]{1,0:T(8,128)(2,1)S(1)}, bf16[128,1152]{1,0:T(8,128)(2,1)}, u32[]{:S(2)}, u32[]{:S(2)}) collective-permute-start(bf16[128,1152]{1,0:T(8,128)(2,1)S(1)} %copy-done.17), channel_id=1, source_target_pairs={{0,16},{4,20},{8,24},{12,28},{16,0},{20,4},{24,8},{28,12},{1,17},{... | collective-permute-start | bytes 884744 | tf_op jit(solution)/shard_map/ppermute | solution.py:372
  117.0 1.7 collective-permute-start.14
  118.8 6.8 %collective-permute-done.19.refs_3_ = bf16[4,256,512]{2,1,0:T(8,128)(2,1)} collective-permute-done((bf16[4,256,512]{2,1,0:T(8,128)(2,1)}, bf16[4,256,512]{2,1,0:T(8,128)(2,1)}, u32[]{:S(2)}, u32[]{:S(2)}) %collective-permute-start.19) | collective-permute-done | bytes 1048608 | tf_op jit(solution)/shard_map/ppermute | solution.py:366
  125.7 4.0 %shard_map.145 = (f32[512,256]{1,0:T(8,128)}, bf16[512,256]{1,0:T(8,128)(2,1)}) custom-call(s32[4]{0:T(128)} %pad_add_fusion.idx.refs_0_, bf16[128,512]{1,0:T(8,128)(2,1)} %copy-done.23, bf16[128,512]{1,0:T(8,128)(2,1)} %copy-done.24, bf16[128,512]{1,0:T(8,128)(2,1)} %copy-done.25, bf16[128,512]{1,0:T(8,128)(2,1)} %collective-permute-done.32.refs_4_, ...), custom_call_target="tpu_custom_call" | custom-call | flops 3449999872 | tf_op jit(solution)/shard_map/pallas_call | solution.py:67
  129.7 1.6 collective-permute-start.33
  131.4 7.3 %collective-permute-done.33 = bf16[512,256]{1,0:T(8,128)(2,1)S(1)} collective-permute-done((bf16[512,256]{1,0:T(8,128)(2,1)}, bf16[512,256]{1,0:T(8,128)(2,1)S(1)}, u32[]{:S(2)}, u32[]{:S(2)}) %collective-permute-start.33) | collective-permute-done | bytes 262176 | tf_op jit(solution)/shard_map/ppermute | solution.py:369
  138.7 2.0 %collective-permute-start.24 = (bf16[128,1152]{1,0:T(8,128)(2,1)S(1)}, bf16[128,1152]{1,0:T(8,128)(2,1)S(1)}, u32[]{:S(2)}, u32[]{:S(2)}) collective-permute-start(bf16[128,1152]{1,0:T(8,128)(2,1)S(1)} %copy-done.17), channel_id=1, source_target_pairs={{0,8},{4,12},{8,0},{12,4},{16,24},{20,28},{24,16},{28,20},{1,9},{5... | collective-permute-start | bytes 884744 | tf_op jit(solution)/shard_map/ppermute | solution.py:372
  140.6 1.9 %convert_add_fusion.3 = f32[512,256]{1,0:T(8,128)} fusion(f32[512,256]{1,0:T(8,128)} %get-tuple-element.55, bf16[512,256]{1,0:T(8,128)(2,1)S(1)} %collective-permute-done.33), kind=kLoop, calls=%fused_computation.10 | loop fusion | flops 262144 | bytes 1310720 | tf_op jit(solution)/shard_map/add | solution.py:467
  142.9 5.6 %collective-permute-done.24.refs_10_ = bf16[128,1152]{1,0:T(8,128)(2,1)S(1)} collective-permute-done((bf16[128,1152]{1,0:T(8,128)(2,1)S(1)}, bf16[128,1152]{1,0:T(8,128)(2,1)S(1)}, u32[]{:S(2)}, u32[]{:S(2)}) %collective-permute-start.24) | collective-permute-done | bytes 294944 | tf_op jit(solution)/shard_map/ppermute | solution.py:372
  148.5 1.7 collective-permute-start.12
  150.3 3.5 %collective-permute-done.26.refs_12_ = bf16[128,1152]{1,0:T(8,128)(2,1)S(1)} collective-permute-done((bf16[128,1152]{1,0:T(8,128)(2,1)}, bf16[128,1152]{1,0:T(8,128)(2,1)S(1)}, u32[]{:S(2)}, u32[]{:S(2)}) %collective-permute-start.26) | collective-permute-done | bytes 294944 | tf_op jit(solution)/shard_map/ppermute | solution.py:372
  153.8 0.7 copy-done.21
  154.6 8.5 %shard_map.143 = (f32[256,512]{1,0:T(8,128)}, f32[256,512]{1,0:T(8,128)}, bf16[2,256,512]{2,1,0:T(8,128)(2,1)}) custom-call(s32[4]{0:T(128)} %pad_add_fusion.idx.refs_0_, bf16[4,256,512]{2,1,0:T(8,128)(2,1)} %pad_maximum_fusion.refs_1_, bf16[4,256,512]{2,1,0:T(8,128)(2,1)} %collective-permute-done.18.refs_2_, ...), custom_call_target="tpu_custom_call" | custom-call | flops 6899999744 | tf_op jit(solution)/shard_map/pallas_call | solution.py:67
  163.1 1.5 collective-permute-start.27
  164.6 8.0 %shard_map.144 = (f32[256,512]{1,0:T(8,128)}, bf16[256,512]{1,0:T(8,128)(2,1)}) custom-call(s32[4]{0:T(128)} %pad_add_fusion.idx.refs_0_, bf16[4,256,512]{2,1,0:T(8,128)(2,1)} %pad_maximum_fusion.refs_1_, bf16[4,256,512]{2,1,0:T(8,128)(2,1)} %collective-permute-done.18.refs_2_, bf16[4,256,512]{2,1,0:T(8,128)(2,1)} %collective-permute-done.19.refs_3_, ...), custom_call_target="tpu_custom_call" | custom-call | flops 5750000128 | tf_op jit(solution)/shard_map/pallas_call | solution.py:67
  173.3 1.8 fusion.3
  175.1 6.8 %collective-permute-done.28 = bf16[256,512]{1,0:T(8,128)(2,1)S(1)} collective-permute-done((bf16[256,512]{1,0:T(8,128)(2,1)}, bf16[256,512]{1,0:T(8,128)(2,1)S(1)}, u32[]{:S(2)}, u32[]{:S(2)}) %collective-permute-start.28) | collective-permute-done | bytes 262176 | tf_op jit(solution)/shard_map/ppermute | solution.py:369
  181.9 0.9 convert_add_fusion.4
  182.7 1.1 convert_add_fusion.1
  (118 shorter events, 6.2 us)
Async XLA Ops:
  0.6 51.2 %collective-permute-start = (bf16[1024,512]{1,0:T(8,128)(2,1)}, bf16[1024,512]{1,0:T(8,128)(2,1)S(1)}, u32[]{:S(2)}, u32[]{:S(2)}) collective-permute-start(bf16[1024,512]{1,0:T(8,128)(2,1)} %bitcast.32), channel_id=1, source_target_pairs={{0,1},{1,0},{2,3},{3,2},{4,5},{5,4},{6,7},{7,6},{8,9},{9,8},{10,11... | collective-permute-start | bytes 3145736 | tf_op jit(solution)/shard_map/ppermute | solution.py:366
  1.1 26.6 %collective-permute-start.1 = (bf16[1024,512]{1,0:T(8,128)(2,1)}, bf16[1024,512]{1,0:T(8,128)(2,1)S(1)}, u32[]{:S(2)}, u32[]{:S(2)}) collective-permute-start(bf16[1024,512]{1,0:T(8,128)(2,1)} %bitcast.33), channel_id=1, source_target_pairs={{0,2},{1,3},{2,0},{3,1},{4,6},{5,7},{6,4},{7,5},{8,10},{9,11},{10,... | collective-permute-start | bytes 3145736 | tf_op jit(solution)/shard_map/ppermute | solution.py:366
  10.8 16.9 %collective-permute-start.3 = (bf16[512,512]{1,0:T(8,128)(2,1)}, bf16[512,512]{1,0:T(8,128)(2,1)S(1)}, u32[]{:S(2)}, u32[]{:S(2)}) collective-permute-start(bf16[512,512]{1,0:T(8,128)(2,1)} %shard_map.139), channel_id=1, source_target_pairs={{0,4},{4,0},{8,12},{12,8},{16,20},{20,16},{24,28},{28,24},{1,5},{5... | collective-permute-start | bytes 1572872 | tf_op jit(solution)/shard_map/ppermute | solution.py:369
  27.7 17.2 %copy-start.13 = (bf16[1024,512]{1,0:T(8,128)(2,1)}, bf16[1024,512]{1,0:T(8,128)(2,1)S(1)}, u32[]{:S(2)}) copy-start(bf16[1024,512]{1,0:T(8,128)(2,1)S(1)} %collective-permute-done.1.x2) | copy-start | bytes 3145732
  27.7 24.1 %collective-permute-start.2 = (bf16[1024,512]{1,0:T(8,128)(2,1)S(1)}, bf16[1024,512]{1,0:T(8,128)(2,1)S(1)}, u32[]{:S(2)}, u32[]{:S(2)}) collective-permute-start(bf16[1024,512]{1,0:T(8,128)(2,1)S(1)} %collective-permute-done.1.x2), channel_id=1, source_target_pairs={{0,1},{1,0},{2,3},{3,2},{4,5},{5,4},{6,7},{7,6},{8,9},{9,8},{10,11... | collective-permute-start | bytes 3145736 | tf_op jit(solution)/shard_map/ppermute | solution.py:366
  29.6 8.3 %collective-permute-start.6 = (bf16[128,512]{1,0:T(8,128)(2,1)S(1)}, bf16[128,512]{1,0:T(8,128)(2,1)S(1)}, u32[]{:S(2)}, u32[]{:S(2)}) collective-permute-start(bf16[128,512]{1,0:T(8,128)(2,1)S(1)} %get-tuple-element.64), channel_id=1, source_target_pairs={{0,24},{4,28},{8,16},{12,20},{16,8},{20,12},{24,0},{28,4},{1,25},{... | collective-permute-start | bytes 393224 | tf_op jit(solution)/shard_map/ppermute | solution.py:372
  33.5 11.4 %collective-permute-start.5 = (bf16[128,512]{1,0:T(8,128)(2,1)S(1)}, bf16[128,512]{1,0:T(8,128)(2,1)S(1)}, u32[]{:S(2)}, u32[]{:S(2)}) collective-permute-start(bf16[128,512]{1,0:T(8,128)(2,1)S(1)} %get-tuple-element.65), channel_id=1, source_target_pairs={{0,16},{4,20},{8,24},{12,28},{16,0},{20,4},{24,8},{28,12},{1,17},{... | collective-permute-start | bytes 393224 | tf_op jit(solution)/shard_map/ppermute | solution.py:372
  33.5 11.4 %collective-permute-start.4 = (bf16[128,512]{1,0:T(8,128)(2,1)S(1)}, bf16[128,512]{1,0:T(8,128)(2,1)S(1)}, u32[]{:S(2)}, u32[]{:S(2)}) collective-permute-start(bf16[128,512]{1,0:T(8,128)(2,1)S(1)} %get-tuple-element.63), channel_id=1, source_target_pairs={{0,8},{4,12},{8,0},{12,4},{16,24},{20,28},{24,16},{28,20},{1,9},{5... | collective-permute-start | bytes 393224 | tf_op jit(solution)/shard_map/ppermute | solution.py:372
  44.9 17.2 %copy-start.8 = (bf16[128,512]{1,0:T(8,128)(2,1)}, bf16[128,512]{1,0:T(8,128)(2,1)S(1)}, u32[]{:S(2)}) copy-start(bf16[128,512]{1,0:T(8,128)(2,1)S(1)} %get-tuple-element.58.refs_6_) | copy-start | bytes 393220
  44.9 5.0 %collective-permute-start.8 = (bf16[128,512]{1,0:T(8,128)(2,1)S(1)}, bf16[128,512]{1,0:T(8,128)(2,1)S(1)}, u32[]{:S(2)}, u32[]{:S(2)}) collective-permute-start(bf16[128,512]{1,0:T(8,128)(2,1)S(1)} %get-tuple-element.58.refs_6_), channel_id=1, source_target_pairs={{0,2},{1,3},{2,0},{3,1},{4,6},{5,7},{6,4},{7,5},{8,10},{9,11},{10,... | collective-permute-start | bytes 393224 | tf_op jit(solution)/shard_map/ppermute | solution.py:366
  46.5 3.5 %collective-permute-start.29 = (bf16[128,512]{1,0:T(8,128)(2,1)S(1)}, bf16[128,512]{1,0:T(8,128)(2,1)S(1)}, u32[]{:S(2)}, u32[]{:S(2)}) collective-permute-start(bf16[128,512]{1,0:T(8,128)(2,1)S(1)} %get-tuple-element.58.refs_6_), channel_id=1, source_target_pairs={{0,0},{1,8},{2,16},{3,24},{4,4},{5,12},{6,20},{7,28},{8,1},{9,9},{... | collective-permute-start | bytes 393224 | tf_op jit(solution)/shard_map/ppermute | solution.py:439
  47.2 32.8 %collective-permute-start.7 = (bf16[128,512]{1,0:T(8,128)(2,1)S(1)}, bf16[128,512]{1,0:T(8,128)(2,1)S(1)}, u32[]{:S(2)}, u32[]{:S(2)}) collective-permute-start(bf16[128,512]{1,0:T(8,128)(2,1)S(1)} %get-tuple-element.58.refs_6_), channel_id=1, source_target_pairs={{0,1},{1,0},{2,3},{3,2},{4,5},{5,4},{6,7},{7,6},{8,9},{9,8},{10,11... | collective-permute-start | bytes 393224 | tf_op jit(solution)/shard_map/ppermute | solution.py:366
  50.0 12.2 %copy-start.26 = (bf16[128,512]{1,0:T(8,128)(2,1)}, bf16[128,512]{1,0:T(8,128)(2,1)S(1)}, u32[]{:S(2)}) copy-start(bf16[128,512]{1,0:T(8,128)(2,1)S(1)} %collective-permute-done.8.refs_8_) | copy-start | bytes 393220
  50.0 30.8 %collective-permute-start.9 = (bf16[128,512]{1,0:T(8,128)(2,1)S(1)}, bf16[128,512]{1,0:T(8,128)(2,1)S(1)}, u32[]{:S(2)}, u32[]{:S(2)}) collective-permute-start(bf16[128,512]{1,0:T(8,128)(2,1)S(1)} %collective-permute-done.8.refs_8_), channel_id=1, source_target_pairs={{0,1},{1,0},{2,3},{3,2},{4,5},{5,4},{6,7},{7,6},{8,9},{9,8},{10,11... | collective-permute-start | bytes 393224 | tf_op jit(solution)/shard_map/ppermute | solution.py:366
  50.0 44.8 %copy-start.23 = (bf16[128,512]{1,0:T(8,128)(2,1)}, bf16[128,512]{1,0:T(8,128)(2,1)S(1)}, u32[]{:S(2)}) copy-start(bf16[128,512]{1,0:T(8,128)(2,1)S(1)} %collective-permute-done.29.refs_1_) | copy-start | bytes 393220
  50.0 48.2 %collective-permute-start.30 = (bf16[128,512]{1,0:T(8,128)(2,1)S(1)}, bf16[128,512]{1,0:T(8,128)(2,1)S(1)}, u32[]{:S(2)}, u32[]{:S(2)}) collective-permute-start(bf16[128,512]{1,0:T(8,128)(2,1)S(1)} %collective-permute-done.29.refs_1_), channel_id=1, source_target_pairs={{0,1},{1,0},{2,3},{3,2},{4,5},{5,4},{6,7},{7,6},{8,9},{9,8},{10,11... | collective-permute-start | bytes 393224 | tf_op jit(solution)/shard_map/ppermute | solution.py:366
  62.2 32.5 %collective-permute-start.17 = (bf16[256,512]{1,0:T(8,128)(2,1)}, bf16[256,512]{1,0:T(8,128)(2,1)S(1)}, u32[]{:S(2)}, u32[]{:S(2)}) collective-permute-start(bf16[256,512]{1,0:T(8,128)(2,1)} %get-tuple-element.49), channel_id=1, source_target_pairs={{0,24},{4,28},{8,16},{12,20},{16,8},{20,12},{24,0},{28,4},{1,25},{... | collective-permute-start | bytes 786440 | tf_op jit(solution)/shard_map/ppermute | solution.py:372
  68.8 28.1 %collective-permute-start.16 = (bf16[256,512]{1,0:T(8,128)(2,1)}, bf16[256,512]{1,0:T(8,128)(2,1)S(1)}, u32[]{:S(2)}, u32[]{:S(2)}) collective-permute-start(bf16[256,512]{1,0:T(8,128)(2,1)} %get-tuple-element.48), channel_id=1, source_target_pairs={{0,16},{4,20},{8,24},{12,28},{16,0},{20,4},{24,8},{28,12},{1,17},{... | collective-permute-start | bytes 786440 | tf_op jit(solution)/shard_map/ppermute | solution.py:372
  68.8 11.2 %copy-start.22 = (bf16[256,512]{1,0:T(8,128)(2,1)S(1)}, bf16[256,512]{1,0:T(8,128)(2,1)}, u32[]{:S(2)}) copy-start(bf16[256,512]{1,0:T(8,128)(2,1)} %get-tuple-element.47) | copy-start | bytes 786436
  80.0 17.0 %collective-permute-start.15 = (bf16[256,512]{1,0:T(8,128)(2,1)S(1)}, bf16[256,512]{1,0:T(8,128)(2,1)S(1)}, u32[]{:S(2)}, u32[]{:S(2)}) collective-permute-start(bf16[256,512]{1,0:T(8,128)(2,1)S(1)} %copy-done.22), channel_id=1, source_target_pairs={{0,8},{4,12},{8,0},{12,4},{16,24},{20,28},{24,16},{28,20},{1,9},{5... | collective-permute-start | bytes 786440 | tf_op jit(solution)/shard_map/ppermute | solution.py:372
  80.7 22.3 %collective-permute-start.22 = (bf16[128,1152]{1,0:T(8,128)(2,1)}, bf16[128,1152]{1,0:T(8,128)(2,1)S(1)}, u32[]{:S(2)}, u32[]{:S(2)}) collective-permute-start(bf16[128,1152]{1,0:T(8,128)(2,1)} %get-tuple-element.33.refs_10_.refs_5_), channel_id=1, source_target_pairs={{0,16},{4,20},{8,24},{12,28},{16,0},{20,4},{24,8},{28,12},{1,17},{... | collective-permute-start | bytes 884744 | tf_op jit(solution)/shard_map/ppermute | solution.py:372
  83.1 13.7 %copy-start.15 = (bf16[128,1152]{1,0:T(8,128)(2,1)S(1)}, bf16[128,1152]{1,0:T(8,128)(2,1)}, u32[]{:S(2)}) copy-start(bf16[128,1152]{1,0:T(8,128)(2,1)} %get-tuple-element.33.refs_10_.refs_5_) | copy-start | bytes 884740
  83.1 13.9 %copy-start.7 = (bf16[256,512]{1,0:T(8,128)(2,1)S(1)}, bf16[256,512]{1,0:T(8,128)(2,1)}, u32[]{:S(2)}) copy-start(bf16[256,512]{1,0:T(8,128)(2,1)} %get-tuple-element.46) | copy-start | bytes 786436
  94.8 17.0 %collective-permute-start.31 = (bf16[128,512]{1,0:T(8,128)(2,1)S(1)}, bf16[128,512]{1,0:T(8,128)(2,1)S(1)}, u32[]{:S(2)}, u32[]{:S(2)}) collective-permute-start(bf16[128,512]{1,0:T(8,128)(2,1)S(1)} %collective-permute-done.29.refs_1_), channel_id=1, source_target_pairs={{0,2},{1,3},{2,0},{3,1},{4,6},{5,7},{6,4},{7,5},{8,10},{9,11},{10,... | collective-permute-start | bytes 393224 | tf_op jit(solution)/shard_map/ppermute | solution.py:366
  96.9 20.2 %collective-permute-start.21 = (bf16[128,1152]{1,0:T(8,128)(2,1)S(1)}, bf16[128,1152]{1,0:T(8,128)(2,1)S(1)}, u32[]{:S(2)}, u32[]{:S(2)}) collective-permute-start(bf16[128,1152]{1,0:T(8,128)(2,1)S(1)} %copy-done.15), channel_id=1, source_target_pairs={{0,8},{4,12},{8,0},{12,4},{16,24},{20,28},{24,16},{28,20},{1,9},{5... | collective-permute-start | bytes 884744 | tf_op jit(solution)/shard_map/ppermute | solution.py:372
  97.0 14.8 %collective-permute-start.13 = (f32[4,256]{1,0:T(4,128)}, f32[4,256]{1,0:T(4,128)S(1)}, u32[]{:S(2)}, u32[]{:S(2)}) collective-permute-start(f32[4,256]{1,0:T(4,128)} %get-tuple-element.45), channel_id=1, source_target_pairs={{0,1},{1,0},{2,3},{3,2},{4,5},{5,4},{6,7},{7,6},{8,9},{9,8},{10,11... | collective-permute-start | bytes 12296 | tf_op jit(solution)/shard_map/ppermute | solution.py:366
  98.1 13.6 %copy-start.24 = (bf16[128,512]{1,0:T(8,128)(2,1)}, bf16[128,512]{1,0:T(8,128)(2,1)S(1)}, u32[]{:S(2)}) copy-start(bf16[128,512]{1,0:T(8,128)(2,1)S(1)} %collective-permute-done.30.refs_2_) | copy-start | bytes 393220
  98.1 27.5 %collective-permute-start.19 = (bf16[4,256,512]{2,1,0:T(8,128)(2,1)}, bf16[4,256,512]{2,1,0:T(8,128)(2,1)}, u32[]{:S(2)}, u32[]{:S(2)}) collective-permute-start(bf16[4,256,512]{2,1,0:T(8,128)(2,1)} %pad_maximum_fusion.refs_1_), channel_id=1, source_target_pairs={{0,2},{1,3},{2,0},{3,1},{4,6},{5,7},{6,4},{7,5},{8,10},{9,11},{10,... | collective-permute-start | bytes 3145736 | tf_op jit(solution)/shard_map/ppermute | solution.py:366
  103.1 15.7 %collective-permute-start.23 = (bf16[128,1152]{1,0:T(8,128)(2,1)S(1)}, bf16[128,1152]{1,0:T(8,128)(2,1)S(1)}, u32[]{:S(2)}, u32[]{:S(2)}) collective-permute-start(bf16[128,1152]{1,0:T(8,128)(2,1)S(1)} %collective-permute-done.22.refs_7_), channel_id=1, source_target_pairs={{0,8},{4,12},{8,0},{12,4},{16,24},{20,28},{24,16},{28,20},{1,9},{5... | collective-permute-start | bytes 884744 | tf_op jit(solution)/shard_map/ppermute | solution.py:372
  103.4 10.3 %copy-start.5 = (f32[1024,1]{1,0:T(8,128)S(1)}, f32[1024,1]{1,0:T(8,128)}, u32[]{:S(2)}) copy-start(f32[1024,1]{1,0:T(8,128)} %get-tuple-element.31) | copy-start | bytes 12292
  103.4 10.6 %copy-start.10 = (f32[4,256]{1,0:T(4,128)S(1)}, f32[4,256]{1,0:T(4,128)}, u32[]{:S(2)}) copy-start(f32[4,256]{1,0:T(4,128)} %get-tuple-element.45) | copy-start | bytes 12292
  103.4 10.7 %copy-start.17 = (bf16[128,1152]{1,0:T(8,128)(2,1)S(1)}, bf16[128,1152]{1,0:T(8,128)(2,1)}, u32[]{:S(2)}) copy-start(bf16[128,1152]{1,0:T(8,128)(2,1)} %get-tuple-element.36.refs_3_.refs_9_) | copy-start | bytes 884740
  111.7 13.9 %copy-start.25 = (bf16[128,512]{1,0:T(8,128)(2,1)}, bf16[128,512]{1,0:T(8,128)(2,1)S(1)}, u32[]{:S(2)}) copy-start(bf16[128,512]{1,0:T(8,128)(2,1)S(1)} %collective-permute-done.31.refs_3_) | copy-start | bytes 393220
  111.8 2.3 %collective-permute-start.32 = (bf16[128,512]{1,0:T(8,128)(2,1)S(1)}, bf16[128,512]{1,0:T(8,128)(2,1)}, u32[]{:S(2)}, u32[]{:S(2)}) collective-permute-start(bf16[128,512]{1,0:T(8,128)(2,1)S(1)} %collective-permute-done.31.refs_3_), channel_id=1, source_target_pairs={{0,1},{1,0},{2,3},{3,2},{4,5},{5,4},{6,7},{7,6},{8,9},{9,8},{10,11... | collective-permute-start | bytes 393224 | tf_op jit(solution)/shard_map/ppermute | solution.py:366
  111.8 30.7 %collective-permute-start.11 = (bf16[1024,512]{1,0:T(8,128)(2,1)}, bf16[1024,512]{1,0:T(8,128)(2,1)S(1)}, u32[]{:S(2)}, u32[]{:S(2)}) collective-permute-start(bf16[1024,512]{1,0:T(8,128)(2,1)} %get-tuple-element.44), channel_id=1, source_target_pairs={{0,1},{1,0},{2,3},{3,2},{4,5},{5,4},{6,7},{7,6},{8,9},{9,8},{10,11... | collective-permute-start | bytes 3145736 | tf_op jit(solution)/shard_map/ppermute | solution.py:366
  114.1 28.4 %collective-permute-start.25 = (bf16[128,1152]{1,0:T(8,128)(2,1)S(1)}, bf16[128,1152]{1,0:T(8,128)(2,1)}, u32[]{:S(2)}, u32[]{:S(2)}) collective-permute-start(bf16[128,1152]{1,0:T(8,128)(2,1)S(1)} %copy-done.17), channel_id=1, source_target_pairs={{0,16},{4,20},{8,24},{12,28},{16,0},{20,4},{24,8},{28,12},{1,17},{... | collective-permute-start | bytes 884744 | tf_op jit(solution)/shard_map/ppermute | solution.py:372
  117.0 12.6 %collective-permute-start.14 = (f32[4,256]{1,0:T(4,128)S(1)}, f32[4,256]{1,0:T(4,128)S(1)}, u32[]{:S(2)}, u32[]{:S(2)}) collective-permute-start(f32[4,256]{1,0:T(4,128)S(1)} %add.65), channel_id=1, source_target_pairs={{0,2},{1,3},{2,0},{3,1},{4,6},{5,7},{6,4},{7,5},{8,10},{9,11},{10,... | collective-permute-start | bytes 12296 | tf_op jit(solution)/shard_map/ppermute | solution.py:366
  118.8 35.0 %collective-permute-start.18 = (bf16[4,256,512]{2,1,0:T(8,128)(2,1)}, bf16[4,256,512]{2,1,0:T(8,128)(2,1)}, u32[]{:S(2)}, u32[]{:S(2)}) collective-permute-start(bf16[4,256,512]{2,1,0:T(8,128)(2,1)} %pad_maximum_fusion.refs_1_), channel_id=1, source_target_pairs={{0,1},{1,0},{2,3},{3,2},{4,5},{5,4},{6,7},{7,6},{8,9},{9,8},{10,11... | collective-permute-start | bytes 3145736 | tf_op jit(solution)/shard_map/ppermute | solution.py:366
  125.6 28.2 %collective-permute-start.20 = (bf16[4,256,512]{2,1,0:T(8,128)(2,1)}, bf16[4,256,512]{2,1,0:T(8,128)(2,1)}, u32[]{:S(2)}, u32[]{:S(2)}) collective-permute-start(bf16[4,256,512]{2,1,0:T(8,128)(2,1)} %collective-permute-done.19.refs_3_), channel_id=1, source_target_pairs={{0,1},{1,0},{2,3},{3,2},{4,5},{5,4},{6,7},{7,6},{8,9},{9,8},{10,11... | collective-permute-start | bytes 3145736 | tf_op jit(solution)/shard_map/ppermute | solution.py:366
  129.7 13.0 %copy-start.2 = (bf16[1024,512]{1,0:T(8,128)(2,1)S(1)}, bf16[1024,512]{1,0:T(8,128)(2,1)}, u32[]{:S(2)}) copy-start(bf16[1024,512]{1,0:T(8,128)(2,1)} %get-tuple-element.43) | copy-start | bytes 3145732
  129.7 9.0 %collective-permute-start.33 = (bf16[512,256]{1,0:T(8,128)(2,1)}, bf16[512,256]{1,0:T(8,128)(2,1)S(1)}, u32[]{:S(2)}, u32[]{:S(2)}) collective-permute-start(bf16[512,256]{1,0:T(8,128)(2,1)} %get-tuple-element.56), channel_id=1, source_target_pairs={{0,4},{4,0},{8,12},{12,8},{16,20},{20,16},{24,28},{28,24},{1,5},{5... | collective-permute-start | bytes 786440 | tf_op jit(solution)/shard_map/ppermute | solution.py:369
  138.7 9.9 %collective-permute-start.24 = (bf16[128,1152]{1,0:T(8,128)(2,1)S(1)}, bf16[128,1152]{1,0:T(8,128)(2,1)S(1)}, u32[]{:S(2)}, u32[]{:S(2)}) collective-permute-start(bf16[128,1152]{1,0:T(8,128)(2,1)S(1)} %copy-done.17), channel_id=1, source_target_pairs={{0,8},{4,12},{8,0},{12,4},{16,24},{20,28},{24,16},{28,20},{1,9},{5... | collective-permute-start | bytes 884744 | tf_op jit(solution)/shard_map/ppermute | solution.py:372
  142.5 30.7 %collective-permute-start.10 = (bf16[1024,512]{1,0:T(8,128)(2,1)}, bf16[1024,512]{1,0:T(8,128)(2,1)S(1)}, u32[]{:S(2)}, u32[]{:S(2)}) collective-permute-start(bf16[1024,512]{1,0:T(8,128)(2,1)} %get-tuple-element.42), channel_id=1, source_target_pairs={{0,1},{1,0},{2,3},{3,2},{4,5},{5,4},{6,7},{7,6},{8,9},{9,8},{10,11... | collective-permute-start | bytes 3145736 | tf_op jit(solution)/shard_map/ppermute | solution.py:366
  142.5 11.3 %collective-permute-start.26 = (bf16[128,1152]{1,0:T(8,128)(2,1)}, bf16[128,1152]{1,0:T(8,128)(2,1)S(1)}, u32[]{:S(2)}, u32[]{:S(2)}) collective-permute-start(bf16[128,1152]{1,0:T(8,128)(2,1)} %collective-permute-done.25.refs_11_), channel_id=1, source_target_pairs={{0,8},{4,12},{8,0},{12,4},{16,24},{20,28},{24,16},{28,20},{1,9},{5... | collective-permute-start | bytes 884744 | tf_op jit(solution)/shard_map/ppermute | solution.py:372
  148.5 24.7 %collective-permute-start.12 = (bf16[1024,512]{1,0:T(8,128)(2,1)S(1)}, bf16[1024,512]{1,0:T(8,128)(2,1)S(1)}, u32[]{:S(2)}, u32[]{:S(2)}) collective-permute-start(bf16[1024,512]{1,0:T(8,128)(2,1)S(1)} %add_convert_fusion), channel_id=1, source_target_pairs={{0,2},{1,3},{2,0},{3,1},{4,6},{5,7},{6,4},{7,5},{8,10},{9,11},{10,... | collective-permute-start | bytes 3145736 | tf_op jit(solution)/shard_map/ppermute | solution.py:366
  163.0 10.2 %copy-start = (bf16[128,8,512]{2,1,0:T(8,128)(2,1)S(1)}, bf16[128,8,512]{2,1,0:T(8,128)(2,1)}, u32[]{:S(2)}) copy-start(bf16[128,8,512]{2,1,0:T(8,128)(2,1)} %param.14) | copy-start | bytes 3145732
  163.1 19.7 %collective-permute-start.27 = (bf16[2,256,512]{2,1,0:T(8,128)(2,1)}, bf16[2,256,512]{2,1,0:T(8,128)(2,1)S(1)}, u32[]{:S(2)}, u32[]{:S(2)}) collective-permute-start(bf16[2,256,512]{2,1,0:T(8,128)(2,1)} %get-tuple-element.51), channel_id=1, source_target_pairs={{0,4},{4,0},{8,12},{12,8},{16,20},{20,16},{24,28},{28,24},{1,5},{5... | collective-permute-start | bytes 1572872 | tf_op jit(solution)/shard_map/ppermute | solution.py:369
  172.6 9.2 %collective-permute-start.28 = (bf16[256,512]{1,0:T(8,128)(2,1)}, bf16[256,512]{1,0:T(8,128)(2,1)S(1)}, u32[]{:S(2)}, u32[]{:S(2)}) collective-permute-start(bf16[256,512]{1,0:T(8,128)(2,1)} %get-tuple-element.54), channel_id=1, source_target_pairs={{0,4},{4,0},{8,12},{12,8},{16,20},{20,16},{24,28},{28,24},{1,5},{5... | collective-permute-start | bytes 786440 | tf_op jit(solution)/shard_map/ppermute | solution.py:369
  (15 other events, 92.1 us)

commit v3 on v2

v3 whole, which is shorter than its diff:
```python
import functools

import jax
import jax.numpy as jnp
from jax import lax
from jax.experimental import pallas as pl
from jax.experimental.pallas import tpu as pltpu
from jax.sharding import PartitionSpec as P

HEAD = 128
BF = jnp.bfloat16
F32 = jnp.float32
VMEM = pl.BlockSpec(memory_space=pltpu.VMEM)
SMEM = pl.BlockSpec(memory_space=pltpu.SMEM)
LIMIT = 56 * 2**20
SCALE = 1.15e9
COSTS = [0.1, 0.1, 0.1, 5, 0.1, 0.1, 5, 0.1, 0.1]
TIES = [1, 2, 1, 0, 2, 1, 0, 0, 1, 1, 1, 1, 0, 0, 1, 1, 0, 0, 0, 0, 1, 1, 1, 0]


def dot(left, right):
    return jnp.dot(left, right, preferred_element_type=F32)


def tdot(left, right):
    return lax.dot_general(left, right, (((0,), (0,)), ((), ())), preferred_element_type=F32)


def rdot(left, right):
    return lax.dot_general(left, right, (((1,), (1,)), ((), ())), preferred_element_type=F32)


def after(array, *others, when=True):
    return lax.optimization_barrier((array, *others))[0] if when else array


class Later:
    def __init__(self, copy, ref):
        self.copy, self.ref = copy, ref

    def get(self):
        if self.copy is not None:
            self.copy.wait()
            self.copy = None
        return self.ref


def get(ref):
    return ref.get() if isinstance(ref, Later) else ref


class Sooner:
    def __init__(self, copy, ref):
        self.copy, self.ref, self.started = copy, ref, False

    def start(self):
        self.copy.start()
        self.started = True


def call(body, ins, outs, micros, scratch=(), later=(), sooner=()):
    n_in, n_out, n_later, n_sooner = len(ins), len(outs), len(later), len(sooner)

    def kernel(*refs):
        given = list(refs[:n_in])
        made = list(refs[n_in:n_in + n_out])
        rest = refs[n_in + n_out:]
        buffers, rest = rest[:n_later + n_sooner], rest[n_later + n_sooner:]
        if buffers:
            sems, rest = rest[0], rest[1:]
        for j, i in enumerate(later):
            copy = pltpu.make_async_copy(given[i], buffers[j], sems.at[j])
            copy.start()
            given[i] = Later(copy, buffers[j])
        for j, i in enumerate(sooner):
            buffer = buffers[n_later + j]
            made[i] = Sooner(pltpu.make_async_copy(buffer, made[i], sems.at[n_later + j]), buffer)
        body(*given, *made, *rest)
        for i in later:
            given[i].get()
        for i in sooner:
            if not made[i].started:
                made[i].start()
        for i in sooner:
            made[i].copy.wait()

    in_specs, out_specs = [VMEM] * n_in, [VMEM] * n_out
    in_specs[0] = SMEM
    for i in later:
        in_specs[i] = pl.BlockSpec(memory_space=pl.ANY)
    for i in sooner:
        out_specs[i] = pl.BlockSpec(memory_space=pl.ANY)
    buffers = [pltpu.VMEM(ins[i].shape, ins[i].dtype) for i in later]
    buffers += [pltpu.VMEM(*outs[i]) for i in sooner]
    if buffers:
        buffers.append(pltpu.SemaphoreType.DMA((n_later + n_sooner,)))
    return pl.pallas_call(
        kernel,
        in_specs=in_specs,
        out_specs=out_specs,
        out_shape=[jax.ShapeDtypeStruct(s, t) for s, t in outs],
        scratch_shapes=[*buffers, *scratch],
        compiler_params=pltpu.CompilerParams(vmem_limit_bytes=LIMIT),
        cost_estimate=pl.CostEstimate(
            flops=int(micros * SCALE), bytes_accessed=0, transcendentals=0
        ),
    )(*ins)


def sums_kernel(n_out, other, idx, owned, occ, grads, out):
    z, x = idx[1], idx[2]
    f_dev = out.shape[0] // n_out
    side = 1 - x if other else x
    at = [pl.ds(pl.multiple_of(((z ^ k) * 2 + side) * f_dev, f_dev), f_dev) for k in range(n_out)]
    owners = jnp.concatenate([owned[a, :] for a in at], axis=0)
    onehot = jnp.where(owners == occ[...], 1.0, 0.0).astype(BF)
    out[...] = dot(onehot, get(grads)[...]).astype(out.dtype)


def norm_rows(m, tile, sources, gain, normed, recip):
    rows, cols = sources[0].shape
    width = 4 * cols

    def step(i, carry):
        at = pl.ds(pl.multiple_of(i * tile, tile), tile)
        total = jnp.zeros((tile, 1), F32)
        for block in sources:
            part = block[at, :].astype(F32)
            total = total + jnp.sum(part * part, axis=1, keepdims=True)
        r = lax.rsqrt(total * (1.0 / width) + 1e-06)
        if recip is not None:
            recip[at, :] = r
        for k, block in enumerate(sources):
            lanes = pl.ds(pl.multiple_of((m ^ k) * cols, cols), cols)
            normed[at, lanes] = (block[at, :].astype(F32) * r * gain[:, lanes]).astype(BF)
        return carry

    lax.fori_loop(0, rows // tile, step, 0, unroll=True)


def quarter_kernel(idx, x0, x1, x2, x3, gain, *refs):
    sends, normed = refs[:-1], refs[-1]
    m, z = idx[0], idx[1]
    cols = x0.shape[1]
    norm_rows(m, 32, (x0, x1, x2, x3), gain, normed, None)
    for k, send in enumerate(sends):
        send[...] = normed[:, pl.ds(pl.multiple_of((z ^ k) * cols, cols), cols)]


def norm_quarter(idx, blocks, gain):
    rows, cols = blocks[0].shape
    width = 4 * cols
    quarter = rows // 4
    return pl.pallas_call(
        quarter_kernel,
        grid_spec=pltpu.PrefetchScalarGridSpec(
            num_scalar_prefetch=1,
            grid=(1,),
            in_specs=[pl.BlockSpec((quarter, cols), lambda i, idx: (idx[0], 0))] * 4
            + [pl.BlockSpec((1, width), lambda i, idx: (0, 0))],
            out_specs=[pl.BlockSpec((quarter, cols), lambda i, idx: (0, 0))] * 4,
            scratch_shapes=[pltpu.VMEM((quarter, width), BF)],
        ),
        out_shape=[jax.ShapeDtypeStruct((quarter, cols), BF)] * 4,
        compiler_params=pltpu.CompilerParams(vmem_limit_bytes=LIMIT),
        cost_estimate=pl.CostEstimate(flops=int(COSTS[1] * SCALE), bytes_accessed=0, transcendentals=0),
    )(idx, *blocks, gain)


def diagonal(f_quarter, flen):
    rows = lax.broadcasted_iota(jnp.int32, (f_quarter, f_quarter * flen), 0)
    lanes = lax.broadcasted_iota(jnp.int32, (f_quarter, f_quarter * flen), 1)
    return rows == lanes // flen


def fold(which, lanes, flen):
    rows = lax.broadcasted_iota(jnp.int32, (lanes, 128), 0)
    to = lax.broadcasted_iota(jnp.int32, (lanes, 128), 1)
    return jnp.where(to == lax.rem(rows, flen) + which * flen, 1.0, 0.0).astype(BF)


def fold_heads(values, heads, fq, flen, shift):
    lanes = lax.broadcasted_iota(jnp.int32, (heads * fq, 128), 1)
    rows = lax.broadcasted_iota(jnp.int32, (heads * fq, 128), 0)
    back = lax.broadcasted_iota(jnp.int32, (fq * flen, 128), 0)
    to = lax.broadcasted_iota(jnp.int32, (fq * flen, 128), 1)
    every = jnp.where(lax.rem(back, flen) == lax.rem(to, flen), 1.0, 0.0).astype(BF)
    wide = jnp.where(lanes // flen == rows // fq + shift, dot(values, every), 0.0)
    total = wide[0:fq]
    for h in range(1, heads):
        total = total + wide[h * fq:(h + 1) * fq]
    return total


def forward_kernel(flen, idx, x0, x1, x2, x3, gain, w_query, w_key, w_value, kmask, lmask,
                   early, probs, raw, upro, normed_out, recip, last, mixed):
    m = idx[0]
    cols = w_query.ref.shape[1]
    heads = cols // HEAD
    normed = normed_out.ref
    rows = normed.shape[0] // 4
    fq = rows // flen
    scale = 1.0 / HEAD**0.5
    diag = diagonal(fq, flen)
    some = [slice(i * fq, (i + 1) * fq) for i in range(4)]

    norm_rows(m, 32, [get(x) for x in (x0, x1, x2, x3)], gain, normed, recip)
    normed_out.start()
    selects = [jnp.where(diag, lmask[i], 0.0).astype(BF) for i in range(4)]
    for i in range(4):
        last[some[i], :] = dot(selects[i], normed[i * rows:(i + 1) * rows, :]).astype(BF)
    query = dot(last[...], get(w_query)[...]).astype(BF)
    early[:, 0:cols] = query
    w_key = get(w_key)
    for h in range(heads):
        at = slice(h * HEAD, (h + 1) * HEAD)
        up = rdot(query[:, at], w_key[:, at]).astype(BF)
        for i in range(4):
            upro.ref[i, some[h], :] = up[some[i], :]
    upro.start()
    for i in range(4):
        part = normed[i * rows:(i + 1) * rows, :]
        score = rdot(upro.ref[i], part)
        mask = jnp.concatenate([jnp.where(diag, kmask[i], 0.0)] * heads, axis=0) > 0.0
        expo = jnp.where(mask, jnp.exp(score * scale), 0.0)
        prob = expo / jnp.sum(expo, axis=1, keepdims=True)
        raw[i] = score
        probs[i] = prob
        prob_b = prob.astype(BF)
        mix = dot(prob_b, part).astype(BF)
        for h in range(heads):
            mixed[h, some[i], :] = mix[some[h], :]
        coef = fold_heads(prob_b, heads, fq, flen, 0) + fold_heads(selects[i], 1, fq, flen, 2 * heads)
        early[some[i], 2 * cols:2 * cols + 128] = coef.astype(BF)
    w_value = get(w_value)
    for h in range(heads):
        at = slice(h * HEAD, (h + 1) * HEAD)
        early[:, cols + h * HEAD:cols + (h + 1) * HEAD] = dot(mixed[h], w_value[:, at]).astype(BF)


def in_turn(m, ref, cols):
    return jnp.concatenate(
        [ref[:, pl.ds(pl.multiple_of((m ^ k) * cols, cols), cols)] for k in range(4)], axis=1
    )


def scores_kernel(flen, idx, normed, w_key, w_value, w_out, lmask, g0, g1, g23, early, probs, raw,
                  late, product, tpro, dscore, probs_b, mixed):
    m = idx[0]
    cols = w_key.ref.shape[1]
    heads = cols // HEAD
    rows = normed.ref.shape[0] // 4
    fq = rows // flen
    scale = 1.0 / HEAD**0.5
    diag = diagonal(fq, flen)
    some = [slice(i * fq, (i + 1) * fq) for i in range(4)]

    grads = jnp.concatenate([g[...] for g in (g0, g1, g23.at[0], g23.at[1])], axis=1)
    d_att = rdot(grads, in_turn(m, get(w_out), cols)).astype(BF)
    late[:, 0:cols] = d_att
    w_value = get(w_value)
    for h in range(heads):
        at = slice(h * HEAD, (h + 1) * HEAD)
        up = rdot(d_att[:, at], w_value[:, at]).astype(BF)
        for i in range(4):
            tpro.ref[i, some[h], :] = up[some[i], :]
    tpro.start()
    prods = []
    normed = get(normed)
    for i in range(4):
        part = normed[i * rows:(i + 1) * rows, :]
        d_prob = rdot(tpro.ref[i], part)
        prob = get(probs)[i]
        d_score = prob * (d_prob - jnp.sum(prob * d_prob, axis=1, keepdims=True)) * scale
        score_b = d_score.astype(BF)
        prob_b = prob.astype(BF)
        dscore[i] = score_b
        probs_b[i] = prob_b
        inner = d_score * get(raw)[i] + prob_b.astype(F32) * d_prob
        prods.append(jnp.sum(inner, axis=0, keepdims=True))
        mix = dot(score_b, part).astype(BF)
        for h in range(heads):
            mixed[h, some[i], :] = mix[some[h], :]
        coef = fold_heads(score_b, heads, fq, flen, heads)
        late[some[i], 2 * cols:2 * cols + 128] = coef.astype(BF)
    parts = []
    w_key = get(w_key)
    for h in range(heads):
        at = slice(h * HEAD, (h + 1) * HEAD)
        parts.append(dot(mixed[h], w_key[:, at]))
    d_query = jnp.concatenate(parts, axis=1).astype(BF)
    late[:, cols:2 * cols] = d_query
    inner = early[:, 0:cols].astype(F32) * d_query.astype(F32)
    inner = jnp.sum(inner, axis=1, keepdims=True)
    for i in range(4):
        select = jnp.where(diag, lmask[i], 0.0)
        product[i:i + 1, :] = prods[i] + jnp.sum(select * inner[some[i], :], axis=0, keepdims=True)


def normed_kernel(flen, idx, w_query, lmask, late, product, upro, tpro, dscore, probs_b, d0, d2, d1, d3, vpro):
    m = idx[0]
    rows = dscore.shape[2]
    fq = rows // flen
    cols = d0.shape[1]
    diag = diagonal(fq, flen)
    vpro[...] = rdot(late[:, cols:2 * cols], get(w_query)[...]).astype(BF)
    upro, tpro = get(upro), get(tpro)
    for i in range(4):
        select = jnp.where(diag, lmask[i], 0.0).astype(BF)
        left = jnp.concatenate([dscore[i], probs_b[i], select], axis=0)
        right = jnp.concatenate(
            [in_turn(m, upro.at[i], cols), in_turn(m, tpro.at[i], cols),
             in_turn(m, vpro.at[pl.ds(i * fq, fq), :], cols)], axis=0
        )
        total = tdot(left, right).astype(BF)
        for k, out in enumerate((d0, d1, d2, d3)):
            out[i * rows:(i + 1) * rows, :] = total[:, k * cols:(k + 1) * cols]
    for out in (d0, d1, d2, d3):
        out[4 * rows:4 * rows + 16, :] = jnp.zeros((16, cols), BF)
    for out in (d2, d3):
        out[4 * rows:4 * rows + 16, 0:rows] = jnp.concatenate(
            [product[...], jnp.zeros((12, rows), F32)], axis=0
        ).astype(BF)


def mix_rows(parts, flen, coefs, normed, z_all):
    fq = z_all.shape[1] // 16
    rows = fq * flen
    diag = jnp.where(diagonal(fq, flen), 1.0, 0.0)
    spread = jnp.concatenate([fold(p, rows, flen).T for p in parts], axis=1)
    for k, block in enumerate(normed):
        block = get(block)
        wide = dot(coefs[k], spread)
        for s in range(4):
            left = jnp.concatenate(
                [(wide[s * fq:(s + 1) * fq, j * rows:(j + 1) * rows] * diag).astype(BF)
                 for j in range(len(parts))], axis=0
            )
            mix = dot(left, block[s * rows:(s + 1) * rows, :]).astype(BF)
            for j in range(len(parts)):
                z_all[j, (k * 4 + s) * fq:(k * 4 + s + 1) * fq, :] = mix[j * fq:(j + 1) * fq, :]


def first_kernel(flen, heads, idx, b0, b1, b2, b3, e0, e1, e2, e3,
                 out_mine, out_other, z_value, z_last, z_all, att, all_grads):
    m, z, x = idx[0], idx[1], idx[2]
    early = (e0, e1, e2, e3)
    cols, half = out_mine.shape
    f_dev = e0.ref.shape[0]
    fq = f_dev // 4
    own = pl.ds(pl.multiple_of(x * half, half), half)
    far = pl.ds(pl.multiple_of((1 - x) * half, half), half)
    at = [pl.ds(pl.multiple_of((m ^ k) * fq, fq), fq) for k in range(4)]
    last = slice(2 * cols, 2 * cols + 128)
    coefs = [jnp.concatenate([get(e)[a, last] for e in early], axis=0) for a in at]
    mix_rows((*range(heads), 2 * heads), flen, coefs, (b0, b1, b2, b3), z_all)
    z_value.ref[...] = z_all[0:heads]
    z_last.ref[...] = z_all[heads]
    z_value.start()
    z_last.start()
    for k, rows in enumerate((b0, b1, b2, b3)):
        to = pl.ds(pl.multiple_of(((z ^ m) ^ k) * f_dev, f_dev), f_dev)
        all_grads[to, :] = get(rows)[4 * fq * flen:4 * fq * flen + f_dev, :]
    for s in range(4):
        att[s * f_dev:(s + 1) * f_dev, :] = get(early[s])[:, cols:2 * cols]
    out_mine[...] = tdot(att[...], all_grads[:, own])
    out_other[...] = tdot(att[...], all_grads[:, far]).astype(BF)


def value_kernel(heads, idx, z_value, z_last, l0, l1, l2, l3, value_mine, query_mine, other, d_all, dq_all):
    m, x = idx[0], idx[2]
    half, cols = value_mine.shape
    fq = l0.shape[0] // 4
    for k in range(4):
        a = pl.ds(pl.multiple_of((m ^ k) * fq, fq), fq)
        for s, late in enumerate((l0, l1, l2, l3)):
            to = slice((k * 4 + s) * fq, (k * 4 + s + 1) * fq)
            d_all[to, :] = late[a, 0:cols]
            dq_all[to, :] = late[a, cols:2 * cols]
    own = pl.ds(pl.multiple_of(x * half, half), half)
    far = pl.ds(pl.multiple_of((1 - x) * half, half), half)
    z_value, z_last = get(z_value), get(z_last)
    for h in range(heads):
        lanes = slice(h * HEAD, (h + 1) * HEAD)
        value_mine[:, lanes] = tdot(z_value[h, :, own], d_all[:, lanes])
        other[0, :, lanes] = tdot(z_value[h, :, far], d_all[:, lanes]).astype(BF)
    query_mine[...] = tdot(z_last[:, own], dq_all[...])
    other[1] = tdot(z_last[:, far], dq_all[...]).astype(BF)


def key_kernel(flen, heads, idx, b0, b1, b2, b3, *refs):
    early, late, refs = refs[:4], refs[4:8], refs[8:]
    mine, other, z_all, q_all = refs
    m, x = idx[0], idx[2]
    half, cols = mine.shape
    fq = late[0].ref.shape[0] // 4
    at = [pl.ds(pl.multiple_of((m ^ k) * fq, fq), fq) for k in range(4)]
    last = slice(2 * cols, 2 * cols + 128)
    coefs = [jnp.concatenate([get(item)[a, last] for item in late], axis=0) for a in at]
    mix_rows(range(heads, 2 * heads), flen, coefs, (b0, b1, b2, b3), z_all)
    for k, a in enumerate(at):
        for s in range(4):
            q_all[(k * 4 + s) * fq:(k * 4 + s + 1) * fq, :] = get(early[s])[a, 0:cols]
    own = pl.ds(pl.multiple_of(x * half, half), half)
    far = pl.ds(pl.multiple_of((1 - x) * half, half), half)
    for h in range(heads):
        lanes = slice(h * HEAD, (h + 1) * HEAD)
        mine[:, lanes] = tdot(z_all[h, :, own], q_all[:, lanes])
        other[:, lanes] = tdot(z_all[h, :, far], q_all[:, lanes]).astype(BF)


def on_device(tok_grad, occurrence, owned, token_ids, embeds, gain, w_query, w_key, w_value, w_out):
    n_tok = lax.axis_size("tok")
    n_out = n_tok // 2
    f_dev, flen = token_ids.shape
    width = gain.shape[0]
    cols = w_key.shape[1]
    rows = f_dev * flen
    feats = width // n_tok
    fq = f_dev // 4
    quarter = fq * flen
    heads = cols // HEAD
    m = lax.axis_index("mdl")
    t = lax.axis_index("tok")
    z, x = t // 2, t % 2
    idx = jnp.stack([m, z, x, t]).astype(jnp.int32)

    def flip(array, bit):
        return lax.ppermute(array, "mdl", [(i, i ^ bit) for i in range(4)])

    def swap(array):
        return lax.ppermute(array, "tok", [(i, i ^ 1) for i in range(n_tok)])

    def cross(array, k):
        return lax.ppermute(array, "tok", [(i, i ^ (2 * k)) for i in range(n_tok)])

    flat = embeds.reshape(rows, cols)
    flat2 = flip(flat, 2)

    owned_col = owned.reshape(-1, 1)
    occ_row = occurrence.reshape(1, -1)

    def sums(other, dtype, owners):
        return call(
            functools.partial(sums_kernel, n_out, other),
            (idx, owners, occ_row, tok_grad),
            [((n_out * f_dev, cols), dtype)],
            COSTS[0],
            later=(3,),
        )[0]

    give = sums(True, BF, owned_col)
    took = swap(give)
    keep = sums(False, F32, owned_col)
    flat2 = after(flat2, keep, when=TIES[11])
    flat1 = flip(flat, 1)
    both = (keep + took.astype(F32)).reshape(n_out, f_dev, cols)
    pieces = [both[k].astype(BF) for k in range(1, n_out)]
    came = [cross(piece, k) for k, piece in enumerate(pieces, 1)]
    flat2 = after(flat2, *pieces, when=TIES[23])
    flat3 = flip(flat2, 1)
    gain_row = gain.reshape(1, width)

    length = jnp.sum((token_ids != 0).astype(jnp.int32), axis=1)
    positions = jnp.arange(flen, dtype=jnp.int32)
    lastmask = (positions[None, :] == (length - 1)[:, None]).astype(F32)
    keymask = (positions[None, :] < length[:, None]).astype(F32)
    lmask = lastmask.reshape(4, 1, quarter)
    kmask = keymask.reshape(4, 1, quarter)

    sends = norm_quarter(idx, (flat, flat1, flat2, flat3), gain_row)
    far_rows = [cross(sends[k], k) for k in range(1, n_out)]

    item = ((f_dev, 2 * cols + 128), BF)
    square = (4, heads * fq, quarter)
    tall = ((4, heads * fq, width), BF)
    def sums_over_tok(*before):
        total = both[0]
        for piece in came:
            total = total + after(piece, *before).astype(F32)
        grad0 = total.astype(BF)
        grad1 = flip(grad0, 1)
        return grad0, grad1, flip(jnp.stack([grad0, grad1]), 2)

    if not TIES[18]:
        grad0, grad1, grad23 = sums_over_tok(sends[0])
    early, probs, raw, upro, normed, recip = call(
        functools.partial(forward_kernel, flen),
        (idx, flat, flat1, flat2, flat3, (after(gain_row, (grad0, grad23)[TIES[1] - 1]) if TIES[1] else gain_row), w_query, w_key, w_value, kmask, lmask),
        [item, (square, F32), (square, F32), tall, ((rows, width), BF), ((rows, 1), F32)],
        COSTS[2],
        [pltpu.VMEM((f_dev, width), BF), pltpu.VMEM((heads, f_dev, width), BF)],
        later=(1, 2, 3, 4, 6, 7, 8),
        sooner=(3, 4),
    )
    if TIES[18]:
        grad0, grad1, grad23 = sums_over_tok(early)
    pairs = []
    for a in range(n_out):
        for b in range(2):
            for c in range(4):
                pairs.append(((a * 2 + b) * 4 + c, (c * 2 + b) * 4 + a))
    turned = lax.ppermute(after(after(grad0, early, when=TIES[16]), grad23, when=TIES[19] > 1), ("tok", "mdl"), pairs)
    far_rows = [after(r, early, when=TIES[2]) for r in far_rows]
    turned = after(turned, early, when=TIES[2])
    sent = after(early, grad23, when=TIES[19])
    early1, early2 = cross(sent, 1), cross(sent, 2)
    gate1 = after(lmask, *far_rows, when=TIES[12])
    if TIES[17]:
        gate1 = after(gate1, early1)

    late, product, tpro, dscore, probs_b = call(
        functools.partial(scores_kernel, flen),
        (idx, normed, w_key, w_value, w_out, gate1, grad0, grad1, grad23, early, probs, raw),
        [item, ((4, quarter), F32), tall, (square, BF), (square, BF)],
        COSTS[4],
        [pltpu.VMEM((heads, f_dev, width), BF)],
        later=(4, 3, 1, 10, 11, 2),
        sooner=(2,),
    )
    if TIES[20]:
        early1, early2 = after(early1, late), after(early2, late)
    early_all = (early, early1, early2, cross(early2, 1) if TIES[10] else cross(early, 3))
    sent = after(late, early1, early2, when=TIES[21])
    late1, late2 = cross(sent, 1), cross(sent, 2)
    gate = after(lmask, late1, when=TIES[4])
    gate = after(gate, late2, when=TIES[4] > 1)
    gate = after(gate, early1, early2, when=TIES[14])
    whole = jnp.concatenate([sends[0]] + far_rows + [turned])
    from2 = flip(after(whole, late, when=TIES[3]), 2)
    gate = after(gate, whole, when=TIES[15])
    d0, d2, d1, d3 = call(
        functools.partial(normed_kernel, flen),
        (idx, w_query, gate, late, product, upro, tpro, dscore, probs_b),
        [((rows + 16, cols), BF)] * 4,
        COSTS[5],
        [pltpu.VMEM((f_dev, width), BF)],
        later=(1, 5, 6),
    )
    beside = (flip(d1, 1), flip(d3, 1))
    from2 = after(from2, d0, when=TIES[6])
    normed_all = (whole, flip(whole, 1), from2, flip(from2, 1))
    across = (d2.astype(F32) + beside[1].astype(F32)).astype(BF)
    own = d0.astype(F32) + beside[0].astype(F32)

    late_all = (late, late1, late2, cross(after(late2, late1, when=TIES[5]), 1))


    f_all = n_out * f_dev
    out_mine, out_other, z_value, z_last = call(
        functools.partial(first_kernel, flen, heads),
        (after(idx, across, when=TIES[7]), *normed_all, *early_all),
        [((cols, feats), F32), ((cols, feats), BF), ((heads, f_all, 2 * feats), BF), ((f_all, 2 * feats), BF)],
        COSTS[6],
        [
            pltpu.VMEM((heads + 1, f_all, 2 * feats), BF),
            pltpu.VMEM((f_all, cols), BF),
            pltpu.VMEM((f_all, 2 * feats), BF),
        ],
        later=(5, 6, 7, 8, 1, 2, 3, 4),
        sooner=(2, 3),
    )
    out_grad = out_mine + swap(out_other).astype(F32)
    value_mine, query_mine, both_other = call(
        functools.partial(value_kernel, heads),
        (after(idx, out_grad, when=TIES[13]), z_value, z_last, *late_all),
        [((feats, cols), F32), ((feats, cols), F32), ((2, feats, cols), BF)],
        COSTS[7],
        [pltpu.VMEM((f_all, cols), BF), pltpu.VMEM((f_all, cols), BF)],
        later=(1, 2),
    )
    key_mine, key_other = call(
        functools.partial(key_kernel, flen, heads),
        (after(idx, both_other), *normed_all, *early_all, *late_all),
        [((feats, cols), F32), ((feats, cols), BF)],
        COSTS[8],
        [pltpu.VMEM((heads, f_all, 2 * feats), BF), pltpu.VMEM((f_all, cols), BF)],
        later=(9, 10, 11, 12, 1, 2, 3, 4, 5, 6, 7, 8),
    )
    came = after(swap(both_other), key_other, when=TIES[8])
    value_grad = value_mine + came[0].astype(F32)
    query_grad = query_mine + came[1].astype(F32)
    key_grad = key_mine + after(swap(key_other), value_grad, query_grad, out_grad, when=TIES[22]).astype(F32)

    crossed_over = after(flip(across, 2), key_other, when=TIES[9]).astype(F32)
    summed = own[0:rows] + crossed_over[0:rows]
    product = (across.astype(F32) + crossed_over)[rows:rows + 4, 0:quarter]
    gain_mine = lax.dynamic_slice_in_dim(gain, m * cols, cols, 0)
    scaled = summed.reshape(f_dev, flen, cols) * gain_mine
    recip = recip.reshape(f_dev, flen, 1)
    weight = recip * recip * (product.reshape(f_dev, flen, 1) * (1.0 / width))
    result = recip * scaled - embeds.astype(F32) * weight
    result = result + jnp.where(lastmask[..., None] > 0, grad0.astype(F32)[:, None, :], 0.0)
    return (result.astype(BF), query_grad, key_grad, value_grad, out_grad)


def general(tok_grad, occurrence, owned, token_ids, embeds, gain, w_query, w_key, w_value, w_out):
    f32 = F32
    bf16 = BF
    n_tok = lax.axis_size("tok")
    fgrams = owned.shape[0]
    f_dev = fgrams // n_tok
    width = gain.shape[0]
    cols = w_key.shape[1]
    local_heads = cols // HEAD
    flen = token_ids.shape[1]
    scale = 1.0 / HEAD**0.5
    onehot = (owned[:, None] == occurrence[None, :]).astype(bf16)
    partial_sum = jnp.dot(onehot, tok_grad, preferred_element_type=f32)
    blocks = partial_sum.reshape(n_tok, f_dev, tok_grad.shape[1])
    arrived = lax.all_to_all(blocks, "tok", split_axis=0, concat_axis=0, tiled=True)
    fgram_sum = jnp.sum(arrived, axis=0)
    fgram_grad = fgram_sum.astype(bf16)
    full_grad = lax.all_gather(fgram_grad, "mdl", axis=1, tiled=True)
    whole_embeds = lax.all_gather(embeds, "mdl", axis=2, tiled=True)
    length = jnp.sum((token_ids != 0).astype(jnp.int32), axis=1)
    positions = jnp.arange(flen, dtype=jnp.int32)
    lastmask = positions[None, :] == (length - 1)[:, None]
    keymask = (positions[None, :] < length[:, None]).astype(f32)
    xfull = whole_embeds.astype(f32)
    recip = lax.rsqrt(jnp.mean(xfull * xfull, axis=-1) + 1e-06)
    normed = (xfull * recip[..., None] * gain).astype(bf16)
    normed_last = jnp.sum(jnp.where(lastmask[..., None], normed.astype(f32), 0.0), axis=1).astype(bf16)
    rows = normed.reshape(f_dev * flen, width)
    keys = dot(rows, w_key).astype(bf16).reshape(f_dev, flen, local_heads, HEAD)
    values = dot(rows, w_value).astype(bf16).reshape(f_dev, flen, local_heads, HEAD)
    query = dot(normed_last, w_query).astype(bf16).reshape(f_dev, local_heads, HEAD)
    keys32 = keys.astype(f32)
    values32 = values.astype(f32)
    query32 = query.astype(f32)
    scores = jnp.einsum("fhd,fjhd->fhj", query, keys, preferred_element_type=f32) * scale
    expo = jnp.exp(scores) * keymask[:, None, :]
    probs = expo / jnp.sum(expo, axis=-1, keepdims=True)
    probs_b = probs.astype(bf16)
    attended = jnp.einsum("fhj,fjhd->fhd", probs_b, values, preferred_element_type=f32)
    attended = attended.astype(bf16).reshape(f_dev, cols)
    d_att = rdot(full_grad, w_out).reshape(f_dev, local_heads, HEAD)
    d_prob = jnp.einsum("fhd,fjhd->fhj", d_att, values32)
    d_score = probs * (d_prob - jnp.sum(probs * d_prob, axis=-1, keepdims=True)) * scale
    d_query = jnp.einsum("fhj,fjhd->fhd", d_score, keys32).astype(bf16).reshape(f_dev, cols)
    d_key = jnp.einsum("fhj,fhd->fjhd", d_score, query32).astype(bf16).reshape(f_dev * flen, cols)
    d_value = jnp.einsum("fhj,fhd->fjhd", probs_b.astype(f32), d_att)
    d_value = d_value.astype(bf16).reshape(f_dev * flen, cols)
    d_normed = (rdot(d_key, w_key) + rdot(d_value, w_value)).reshape(f_dev, flen, width)
    from_query = rdot(d_query, w_query)
    d_normed = d_normed + jnp.where(lastmask[..., None], from_query[:, None, :], 0.0)
    feat_start = lax.axis_index("mdl") * embeds.shape[2]
    summed = lax.psum(d_normed, "mdl")
    scaled = summed * gain
    product = jnp.mean(xfull * scaled, axis=-1)
    result = recip[..., None] * scaled - xfull * (recip**3 * product)[..., None]
    result = lax.dynamic_slice_in_dim(result, feat_start, embeds.shape[2], 2)
    result = result + jnp.where(lastmask[..., None], fgram_grad.astype(f32)[:, None, :], 0.0)
    query_grad, key_grad, value_grad = (
        lax.psum_scatter(part, "tok", scatter_dimension=0, tiled=True)
        for part in (tdot(normed_last, d_query), tdot(rows, d_key), tdot(rows, d_value))
    )
    out_grad = lax.psum_scatter(tdot(attended, full_grad), "tok", scatter_dimension=1, tiled=True)
    return (result.astype(bf16), query_grad, key_grad, value_grad, out_grad)


def chosen(*args):
    fits = lax.axis_size("tok") == 8 and lax.axis_size("mdl") == 4
    return (on_device if fits else general)(*args)


def solution(mesh):
    return jax.shard_map(
        chosen,
        mesh=mesh,
        in_specs=(
            P("tok", "mdl"),
            P("tok"),
            P(),
            P("tok", None),
            P("tok", None, "mdl"),
            P(),
            P(None, "mdl"),
            P(None, "mdl"),
            P(None, "mdl"),
            P("mdl", None),
        ),
        out_specs=(
            P("tok", None, "mdl"),
            P("tok", "mdl"),
            P("tok", "mdl"),
            P("tok", "mdl"),
            P("mdl", "tok"),
        ),
        check_vma=False,
    )
```

time: 185 us -> 172 us (0.930)
  starting transfers between devices: 42.3 us -> 28.9 us
  other arithmetic: 10.5 us -> 19.9 us
  Pallas kernels: 70.1 us -> 63.1 us
  waiting for transfers between devices: 53.8 us -> 48.5 us
  local copies, waits for them, and re-layouts: 6.03 us -> 9.54 us
    ppermute x4, waiting for transfers between devices: 14.1 us -> 0.85 us  [swap(): return lax.ppermute(array, 'tok', [(i, i ^ 1) for i in range(n_tok)])]
    ppermute x17 -> x11, starting transfers between devices: 16.6 us -> 6.41 us  [flip(): return lax.ppermute(array, 'mdl', [(i, i ^ bit) for i in range(4)])]
    ppermute x12, waiting for transfers between devices: 21.5 us -> 30.1 us  [cross(): return lax.ppermute(array, 'tok', [(i, i ^ 2 * k) for i in range(n_tok)])]
    pallas_call x9, Pallas kernels: 70.1 us -> 63.1 us  [the longest x8 59.8 us: call(): pl.pallas_call(kernel, in_specs=in_specs, out_specs=out_specs, out_shape=...]
    convert_element_type x1 -> x2, other arithmetic: 0.29 us -> 4.08 us  [the longest x1 2.56 us: on_device(): across = (d2.astype(F32) + beside[1].astype(F32)).astype(BF)]
    ppermute x12, starting transfers between devices: 19.7 us -> 16.4 us  [cross(): return lax.ppermute(array, 'tok', [(i, i ^ 2 * k) for i in range(n_tok)])]
    unnamed x58 -> x48, local copies, waits for them, and re-layouts: 2.16 us -> 4.89 us
    add x3 -> x2, other arithmetic: 2.02 us -> 4.02 us  [the longest x1 2.21 us: on_device(): value_grad = value_mine + came[0].astype(F32)]
  transfers between devices with their start and end apart: 34 -> 28, of which waited for: 11 -> 10; matrix products, arithmetic and copies ran while one was open for 7% -> 13% of each run, Pallas kernels for 38% -> 37%
where the time goes in v3:
time: 172 us; the launch traced here: 171 us
  Pallas kernels  63.1 us (37%)
  waiting for transfers between devices  48.5 us (28%)
  starting transfers between devices  28.9 us (17%)
  other arithmetic  19.9 us (12%)
  local copies, waits for them, and re-layouts  9.54 us (6%)
    pallas_call x8, Pallas kernels, call(): pl.pallas_call(kernel, in_specs=in_specs, out_specs=out_specs, out_shape=...  59.8 us
    ppermute x12, waiting for transfers between devices, cross(): return lax.ppermute(array, 'tok', [(i, i ^ 2 * k) for i in range(n_tok)])  30.1 us
    ppermute x11, waiting for transfers between devices, flip(): return lax.ppermute(array, 'mdl', [(i, i ^ bit) for i in range(4)])  17.5 us
    ppermute x12, starting transfers between devices, cross(): return lax.ppermute(array, 'tok', [(i, i ^ 2 * k) for i in range(n_tok)])  16.4 us
    ppermute x11, starting transfers between devices, flip(): return lax.ppermute(array, 'mdl', [(i, i ^ bit) for i in range(4)])  6.41 us
    ppermute x4, starting transfers between devices, swap(): return lax.ppermute(array, 'tok', [(i, i ^ 1) for i in range(n_tok)])  5.27 us
    unnamed x48, local copies, waits for them, and re-layouts  4.89 us
  transfers between devices with their start and end apart: 28, of which 10 were waited for; matrix products, arithmetic and copies ran while one was open for 13% of the time, Pallas kernels for 37%

profile of v3, /device:TPU:0, one launch (start us, length us, event | category | flops | bytes accessed | tf_op | source)
XLA Modules:
  0.0 171.1 jit_solution(14145359939013366131)
XLA Ops:
  0.6 3.0 %collective-permute-start.1 = (bf16[1024,512]{1,0:T(8,128)(2,1)}, bf16[1024,512]{1,0:T(8,128)(2,1)S(1)}, u32[]{:S(2)}, u32[]{:S(2)}) collective-permute-start(bf16[1024,512]{1,0:T(8,128)(2,1)} %bitcast.28), channel_id=1, source_target_pairs={{0,2},{1,3},{2,0},{3,1},{4,6},{5,7},{6,4},{7,5},{8,10},{9,11},{10,... | collective-permute-start | bytes 3145736 | tf_op jit(solution)/shard_map/ppermute | solution.py:429
  3.7 1.7 copy.19.refs_1_
  5.9 4.7 %shard_map.138 = bf16[512,512]{1,0:T(8,128)(2,1)} custom-call(s32[4]{0:T(128)} %pad_add_fusion.refs_0_.idx, s32[1024,1]{1,0:T(8,128)} %copy.19.refs_1_, s32[1,2048]{1,0:T(1,128)} %bitcast.36, bf16[2048,512]{1,0:T(8,128)(2,1)} %refs_3_.4), custom_call_target="tpu_custom_call" | custom-call | flops 115000000 | tf_op jit(solution)/shard_map/pallas_call | solution.py:97
  10.6 1.6 collective-permute-start.3
  12.2 4.9 %shard_map.137 = f32[512,512]{1,0:T(8,128)} custom-call(s32[4]{0:T(128)} %pad_add_fusion.refs_0_.idx, s32[1024,1]{1,0:T(8,128)} %copy.19.refs_1_, s32[1,2048]{1,0:T(1,128)} %bitcast.37, bf16[2048,512]{1,0:T(8,128)(2,1)} %refs_3_.4), custom_call_target="tpu_custom_call" | custom-call | flops 115000000 | tf_op jit(solution)/shard_map/pallas_call | solution.py:97
  17.1 10.0 %collective-permute-done.1.x2.refs_3_ = bf16[1024,512]{1,0:T(8,128)(2,1)S(1)} collective-permute-done((bf16[1024,512]{1,0:T(8,128)(2,1)}, bf16[1024,512]{1,0:T(8,128)(2,1)S(1)}, u32[]{:S(2)}, u32[]{:S(2)}) %collective-permute-start.1) | collective-permute-done | bytes 1048608 | tf_op jit(solution)/shard_map/ppermute | solution.py:429
  27.1 2.8 %fusion.12 = (bf16[512,512]{1,0:T(8,128)(2,1)S(1)}, f32[512,512]{1,0:T(8,128)}) fusion(f32[512,512]{1,0:T(8,128)} %shard_map.137, bf16[512,512]{1,0:T(8,128)(2,1)S(1)} %collective-permute-done.3), kind=kLoop, calls=%fused_computation.35 | loop fusion | flops 786432 | bytes 3145728 | tf_op jit(solution)/shard_map/convert.4
  29.9 0.7 fusion.13
  30.6 3.8 %collective-permute-start.6 = (bf16[128,512]{1,0:T(8,128)(2,1)}, bf16[128,512]{1,0:T(8,128)(2,1)}, u32[]{:S(2)}, u32[]{:S(2)}) collective-permute-start(bf16[128,512]{1,0:T(8,128)(2,1)} %get-tuple-element.110), channel_id=1, source_target_pairs={{0,24},{4,28},{8,16},{12,20},{16,8},{20,12},{24,0},{28,4},{1,25},{... | collective-permute-start | bytes 393224 | tf_op jit(solution)/shard_map/ppermute | solution.py:435
  35.4 0.9 copy-done.3
  36.3 3.3 %shard_map.139 = (bf16[256,512]{1,0:T(8,128)(2,1)}, bf16[256,512]{1,0:T(8,128)(2,1)}, bf16[256,512]{1,0:T(8,128)(2,1)}, bf16[256,512]{1,0:T(8,128)(2,1)}) custom-call(s32[4]{0:T(128)} %pad_add_fusion.refs_0_.idx, bf16[1024,512]{1,0:T(8,128)(2,1)} %bitcast.29, bf16[1024,512]{1,0:T(8,128)(2,1)} %copy-done.3, bf16[1024,512]{1,0:T(8,128)(2,1)} %copy-done.2, ...), custom_call_target="tpu_custom_call" | custom-call | flops 115000000 | tf_op jit(solution)/shard_map/pallas_call | solution.py:154
  39.6 6.4 %collective-permute-done.5 = bf16[128,512]{1,0:T(8,128)(2,1)} collective-permute-done((bf16[128,512]{1,0:T(8,128)(2,1)S(1)}, bf16[128,512]{1,0:T(8,128)(2,1)}, u32[]{:S(2)}, u32[]{:S(2)}) %collective-permute-start.5) | collective-permute-done | bytes 131104 | tf_op jit(solution)/shard_map/ppermute | solution.py:435
  46.1 1.2 fusion.10
  47.6 0.8 collective-permute-start.16
  48.4 3.4 %collective-permute-start.13 = (bf16[256,512]{1,0:T(8,128)(2,1)}, bf16[256,512]{1,0:T(8,128)(2,1)S(1)}, u32[]{:S(2)}, u32[]{:S(2)}) collective-permute-start(bf16[256,512]{1,0:T(8,128)(2,1)} %get-tuple-element.72), channel_id=1, source_target_pairs={{0,8},{4,12},{8,0},{12,4},{16,24},{20,28},{24,16},{28,20},{1,9},{5... | collective-permute-start | bytes 786440 | tf_op jit(solution)/shard_map/ppermute | solution.py:435
  51.8 3.3 %collective-permute-start.14 = (bf16[256,512]{1,0:T(8,128)(2,1)}, bf16[256,512]{1,0:T(8,128)(2,1)S(1)}, u32[]{:S(2)}, u32[]{:S(2)}) collective-permute-start(bf16[256,512]{1,0:T(8,128)(2,1)} %get-tuple-element.74), channel_id=1, source_target_pairs={{0,16},{4,20},{8,24},{12,28},{16,0},{20,4},{24,8},{28,12},{1,17},{... | collective-permute-start | bytes 786440 | tf_op jit(solution)/shard_map/ppermute | solution.py:435
  56.3 1.0 constant_dynamic-update-slice_fusion.4
  57.3 6.6 %collective-permute-done.8.refs_8_ = bf16[2,128,512]{2,1,0:T(8,128)(2,1)S(1)} collective-permute-done((bf16[2,128,512]{2,1,0:T(8,128)(2,1)S(1)}, bf16[2,128,512]{2,1,0:T(8,128)(2,1)S(1)}, u32[]{:S(2)}, u32[]{:S(2)}) %collective-permute-start.8) | collective-permute-done | bytes 262176 | tf_op jit(solution)/shard_map/ppermute | solution.py:429
  63.9 13.4 %shard_map.140 = (bf16[128,1152]{1,0:T(8,128)(2,1)}, f32[4,128,256]{2,1,0:T(8,128)}, f32[4,128,256]{2,1,0:T(8,128)}, bf16[4,128,2048]{2,1,0:T(8,128)(2,1)}, bf16...) custom-call(s32[4]{0:T(128)} %pad_add_fusion.refs_0_.idx, bf16[1024,512]{1,0:T(8,128)(2,1)} %bitcast.30, ...), custom_call_target="tpu_custom_call" | custom-call | flops 115000000 | tf_op jit(solution)/shard_map/pallas_call | solution.py:97
  77.5 2.0 %collective-permute-start.21 = (bf16[1152,512]{1,0:T(8,128)(2,1)S(1)}, bf16[1152,512]{1,0:T(8,128)(2,1)S(1)}, u32[]{:S(2)}, u32[]{:S(2)}) collective-permute-start(bf16[1152,512]{1,0:T(8,128)(2,1)S(1)} %constant_dynamic-update-slice_fusion.refs_1_), channel_id=1, source_target_pairs={{0,2},{1,3},{2,0},{3,1},{4,6},{5,7},{6,4},{7,5},{8,10},{9,11},{10,... | collective-permute-start | bytes 3538952 | tf_op jit(solution)/shard_map/ppermute | solution.py:429
  79.5 2.1 %collective-permute-start.10 = (bf16[128,1152]{1,0:T(8,128)(2,1)}, bf16[128,1152]{1,0:T(8,128)(2,1)S(1)}, u32[]{:S(2)}, u32[]{:S(2)}) collective-permute-start(bf16[128,1152]{1,0:T(8,128)(2,1)} %get-tuple-element.62.refs_9_.refs_5_), channel_id=1, source_target_pairs={{0,16},{4,20},{8,24},{12,28},{16,0},{20,4},{24,8},{28,12},{1,17},{... | collective-permute-start | bytes 884744 | tf_op jit(solution)/shard_map/ppermute | solution.py:435
  81.7 11.0 %shard_map.141 = (bf16[128,1152]{1,0:T(8,128)(2,1)}, f32[4,256]{1,0:T(4,128)}, bf16[4,128,2048]{2,1,0:T(8,128)(2,1)}, bf16[4,128,256]{2,1,0:T(8,128)(2,1)}, bf16[4,128,256]{2,1,0:T(8,128)(2,1)}) custom-call(s32[4]{0:T(128)} %pad_add_fusion.refs_0_.idx, bf16[1024,2048]{1,0:T(8,128)(2,1)} %get-tuple-element.61.refs_1_, bf16[2048,512]{1,0:T(8,128)(2,1)} %refs_2_.1, ...), custom_call_target="tpu_custom_call" | custom-call | flops 115000000 | tf_op jit(solution)/shard_map/pallas_call | solution.py:97
  92.7 3.1 %collective-permute-done.10.refs_7_ = bf16[128,1152]{1,0:T(8,128)(2,1)S(1)} collective-permute-done((bf16[128,1152]{1,0:T(8,128)(2,1)}, bf16[128,1152]{1,0:T(8,128)(2,1)S(1)}, u32[]{:S(2)}, u32[]{:S(2)}) %collective-permute-start.10) | collective-permute-done | bytes 294944 | tf_op jit(solution)/shard_map/ppermute | solution.py:435
  96.5 1.1 collective-permute-start.11
  97.6 10.1 %collective-permute-done.11.refs_4_.refs_10_ = bf16[128,1152]{1,0:T(8,128)(2,1)S(1)} collective-permute-done((bf16[128,1152]{1,0:T(8,128)(2,1)}, bf16[128,1152]{1,0:T(8,128)(2,1)S(1)}, u32[]{:S(2)}, u32[]{:S(2)}) %collective-permute-start.11) | collective-permute-done | bytes 294944 | tf_op jit(solution)/shard_map/ppermute | solution.py:435
  107.7 5.6 %collective-permute-done.12.refs_5_.refs_11_ = bf16[128,1152]{1,0:T(8,128)(2,1)S(1)} collective-permute-done((bf16[128,1152]{1,0:T(8,128)(2,1)}, bf16[128,1152]{1,0:T(8,128)(2,1)S(1)}, u32[]{:S(2)}, u32[]{:S(2)}) %collective-permute-start.12) | collective-permute-done | bytes 294944 | tf_op jit(solution)/shard_map/ppermute | solution.py:435
  113.3 8.2 %shard_map.142 = (bf16[1040,512]{1,0:T(8,128)(2,1)}, bf16[1040,512]{1,0:T(8,128)(2,1)}, bf16[1040,512]{1,0:T(8,128)(2,1)}, bf16[1040,512]{1,0:T(8,128)(2,1)}) custom-call(s32[4]{0:T(128)} %pad_add_fusion.refs_0_.idx, bf16[2048,512]{1,0:T(8,128)(2,1)} %refs_1_.1, f32[4,1,256]{2,1,0:T(1,128)} %get-tuple-element.79.refs_10_.refs_5_.refs_2_, ...), custom_call_target="tpu_custom_call" | custom-call | flops 115000000 | tf_op jit(solution)/shard_map/pallas_call | solution.py:97
  122.2 2.0 %collective-permute-start.24 = (bf16[128,1152]{1,0:T(8,128)(2,1)S(1)}, bf16[128,1152]{1,0:T(8,128)(2,1)S(1)}, u32[]{:S(2)}, u32[]{:S(2)}) collective-permute-start(bf16[128,1152]{1,0:T(8,128)(2,1)S(1)} %collective-permute-done.12.refs_5_.refs_11_), channel_id=1, source_target_pairs={{0,8},{4,12},{8,0},{12,4},{16,24},{20,28},{24,16},{28,20},{1,9},{5... | collective-permute-start | bytes 884744 | tf_op jit(solution)/shard_map/ppermute | solution.py:435
  124.2 0.9 collective-permute-done.18
  125.3 2.6 %add_convert_fusion = bf16[1040,512]{1,0:T(8,128)(2,1)} fusion(bf16[1040,512]{1,0:T(8,128)(2,1)S(1)} %collective-permute-done.18, bf16[1040,512]{1,0:T(8,128)(2,1)} %get-tuple-element.87), kind=kLoop, calls=%fused_computation | loop fusion | flops 2129920 | bytes 3194880 | tf_op jit(solution)/shard_map/convert_element_type | solution.py:543
  127.8 4.2 %collective-permute-done.23.refs_8_ = bf16[128,1152]{1,0:T(8,128)(2,1)S(1)} collective-permute-done((bf16[128,1152]{1,0:T(8,128)(2,1)S(1)}, bf16[128,1152]{1,0:T(8,128)(2,1)S(1)}, u32[]{:S(2)}, u32[]{:S(2)}) %collective-permute-start.23) | collective-permute-done | bytes 294944 | tf_op jit(solution)/shard_map/ppermute | solution.py:435
  133.1 1.1 copy-done.11
  134.2 7.0 %shard_map.143 = (f32[512,256]{1,0:T(8,128)}, bf16[512,256]{1,0:T(8,128)(2,1)}, bf16[4,512,512]{2,1,0:T(8,128)(2,1)}, bf16[512,512]{1,0:T(8,128)(2,1)}) custom-call(s32[4]{0:T(128)} %pad_add_fusion.refs_0_.idx, bf16[1152,512]{1,0:T(8,128)(2,1)} %copy-done.4, bf16[1152,512]{1,0:T(8,128)(2,1)} %copy-done.10, bf16[1152,512]{1,0:T(8,128)(2,1)} %copy-done.9, ...), custom_call_target="tpu_custom_call" | custom-call | flops 5750000128 | tf_op jit(solution)/shard_map/pallas_call | solution.py:97
  141.2 1.6 collective-permute-start.27
  142.7 0.8 dynamic_slice.3
  143.6 1.2 reduce
  145.0 0.7 copy-done.8
  145.7 4.8 %shard_map.144 = (f32[256,512]{1,0:T(8,128)}, f32[256,512]{1,0:T(8,128)}, bf16[2,256,512]{2,1,0:T(8,128)(2,1)}) custom-call(s32[4]{0:T(128)} %pad_add_fusion.refs_0_.idx, bf16[4,512,512]{2,1,0:T(8,128)(2,1)} %get-tuple-element.89.refs_1_, bf16[512,512]{1,0:T(8,128)(2,1)} %get-tuple-element.90.refs_2_, bf16[128,1152]{1,0:T(8,128)(2,1)} %get-tuple-element.68.refs_3_.refs_9_, ...), custom_call_target="tpu_custom_call" | custom-call | flops 115000000 | tf_op jit(solution)/shard_map/pallas_call | solution.py:97
  151.2 5.8 %shard_map.145 = (f32[256,512]{1,0:T(8,128)}, bf16[256,512]{1,0:T(8,128)(2,1)}) custom-call(s32[4]{0:T(128)} %pad_add_fusion.refs_0_.idx, bf16[1152,512]{1,0:T(8,128)(2,1)} %copy-done.4, bf16[1152,512]{1,0:T(8,128)(2,1)} %copy-done.10, bf16[1152,512]{1,0:T(8,128)(2,1)} %copy-done.9, bf16[1152,512]{1,0:T(8,128)(2,1)} %copy-done.11, ...), custom_call_target="tpu_custom_call" | custom-call | flops 115000000 | tf_op jit(solution)/shard_map/pallas_call | solution.py:97
  157.0 1.6 collective-permute-start.26
  158.6 0.8 convert_add_fusion.4
  159.4 1.5 convert_element_type.108
  161.6 0.7 mul.68
  162.3 0.8 multiply_multiply_fusion
  163.2 3.0 %fusion.5 = bf16[128,8,512]{2,1,0:T(8,128)(2,1)} fusion(f32[1040,512]{1,0:T(8,128)S(1)} %convert_element_type.108, bf16[128,8,512]{2,1,0:T(8,128)(2,1)S(1)} %copy-done.1, bf16[1040,512]{1,0:T(8,128)(2,1)} %collective-permute-done.17, bf16[1040,512]{1,0:T(8,128)(2,1)} %get-tuple-element.85, f32[128,512]{1,0:T(8,128)S(1)} %get-tuple-element.103, ...), kind=kLoop, calls=%fused_computation.7 | loop fusion | flops 6291456 | bytes 6564864 | tf_op jit(solution)/shard_map/convert_element_type | solution.py:594
  166.2 2.2 %convert_add_fusion.1 = (f32[256,512]{1,0:T(8,128)}, f32[256,512]{1,0:T(8,128)}) fusion(f32[256,512]{1,0:T(8,128)S(1)} %copy-done.13, bf16[2,256,512]{2,1,0:T(8,128)(2,1)} %collective-permute-done.25, f32[256,512]{1,0:T(8,128)S(1)} %copy-done.14), kind=kLoop, calls=%fused_computation.9 | loop fusion | flops 524288 | bytes 2621440 | tf_op jit(solution)/shard_map/add | solution.py:581
  168.4 0.8 collective-permute-done.26
  169.3 1.8 %convert_add_fusion.3 = f32[256,512]{1,0:T(8,128)} fusion(f32[256,512]{1,0:T(8,128)S(1)} %copy-done.15, bf16[256,512]{1,0:T(8,128)(2,1)} %collective-permute-done.26), kind=kLoop, calls=%fused_computation.11 | loop fusion | flops 262144 | bytes 1310720 | tf_op jit(solution)/shard_map/add | solution.py:583
  (97 shorter events, 7.3 us)
Async XLA Ops:
  0.6 11.6 %copy-start = (bf16[128,8,512]{2,1,0:T(8,128)(2,1)S(1)}, bf16[128,8,512]{2,1,0:T(8,128)(2,1)}, u32[]{:S(2)}) copy-start(bf16[128,8,512]{2,1,0:T(8,128)(2,1)} %param.14) | copy-start | bytes 3145732
  0.6 26.4 %collective-permute-start.1 = (bf16[1024,512]{1,0:T(8,128)(2,1)}, bf16[1024,512]{1,0:T(8,128)(2,1)S(1)}, u32[]{:S(2)}, u32[]{:S(2)}) collective-permute-start(bf16[1024,512]{1,0:T(8,128)(2,1)} %bitcast.28), channel_id=1, source_target_pairs={{0,2},{1,3},{2,0},{3,1},{4,6},{5,7},{6,4},{7,5},{8,10},{9,11},{10,... | collective-permute-start | bytes 3145736 | tf_op jit(solution)/shard_map/ppermute | solution.py:429
  10.6 16.4 %collective-permute-start.3 = (bf16[512,512]{1,0:T(8,128)(2,1)}, bf16[512,512]{1,0:T(8,128)(2,1)S(1)}, u32[]{:S(2)}, u32[]{:S(2)}) collective-permute-start(bf16[512,512]{1,0:T(8,128)(2,1)} %shard_map.138), channel_id=1, source_target_pairs={{0,4},{4,0},{8,12},{12,8},{16,20},{20,16},{24,28},{28,24},{1,5},{5... | collective-permute-start | bytes 1572872 | tf_op jit(solution)/shard_map/ppermute | solution.py:432
  12.2 23.1 %collective-permute-start = (bf16[1024,512]{1,0:T(8,128)(2,1)S(1)}, bf16[1024,512]{1,0:T(8,128)(2,1)S(1)}, u32[]{:S(2)}, u32[]{:S(2)}) collective-permute-start(bf16[1024,512]{1,0:T(8,128)(2,1)S(1)} %bitcast.31), channel_id=1, source_target_pairs={{0,1},{1,0},{2,3},{3,2},{4,5},{5,4},{6,7},{7,6},{8,9},{9,8},{10,11... | collective-permute-start | bytes 3145736 | tf_op jit(solution)/shard_map/ppermute | solution.py:429
  17.1 17.9 %copy-start.21 = (s32[128,8]{0,1:T(8,128)S(1)}, s32[128,8]{0,1:T(8,128)}, u32[]{:S(2)}) copy-start(s32[128,8]{0,1:T(8,128)} %param.13) | copy-start | bytes 12292
  27.0 8.3 %copy-start.2 = (bf16[1024,512]{1,0:T(8,128)(2,1)}, bf16[1024,512]{1,0:T(8,128)(2,1)S(1)}, u32[]{:S(2)}) copy-start(bf16[1024,512]{1,0:T(8,128)(2,1)S(1)} %collective-permute-done.1.x2.refs_3_) | copy-start | bytes 3145732
  27.0 8.3 %collective-permute-start.2 = (bf16[1024,512]{1,0:T(8,128)(2,1)S(1)}, bf16[1024,512]{1,0:T(8,128)(2,1)}, u32[]{:S(2)}, u32[]{:S(2)}) collective-permute-start(bf16[1024,512]{1,0:T(8,128)(2,1)S(1)} %collective-permute-done.1.x2.refs_3_), channel_id=1, source_target_pairs={{0,1},{1,0},{2,3},{3,2},{4,5},{5,4},{6,7},{7,6},{8,9},{9,8},{10,11... | collective-permute-start | bytes 3145736 | tf_op jit(solution)/shard_map/ppermute | solution.py:429
  30.6 9.1 %collective-permute-start.6 = (bf16[128,512]{1,0:T(8,128)(2,1)}, bf16[128,512]{1,0:T(8,128)(2,1)}, u32[]{:S(2)}, u32[]{:S(2)}) collective-permute-start(bf16[128,512]{1,0:T(8,128)(2,1)} %get-tuple-element.110), channel_id=1, source_target_pairs={{0,24},{4,28},{8,16},{12,20},{16,8},{20,12},{24,0},{28,4},{1,25},{... | collective-permute-start | bytes 393224 | tf_op jit(solution)/shard_map/ppermute | solution.py:435
  34.4 11.7 %collective-permute-start.5 = (bf16[128,512]{1,0:T(8,128)(2,1)S(1)}, bf16[128,512]{1,0:T(8,128)(2,1)}, u32[]{:S(2)}, u32[]{:S(2)}) collective-permute-start(bf16[128,512]{1,0:T(8,128)(2,1)S(1)} %get-tuple-element.111), channel_id=1, source_target_pairs={{0,16},{4,20},{8,24},{12,28},{16,0},{20,4},{24,8},{28,12},{1,17},{... | collective-permute-start | bytes 393224 | tf_op jit(solution)/shard_map/ppermute | solution.py:435
  34.4 11.7 %collective-permute-start.4 = (bf16[128,512]{1,0:T(8,128)(2,1)S(1)}, bf16[128,512]{1,0:T(8,128)(2,1)}, u32[]{:S(2)}, u32[]{:S(2)}) collective-permute-start(bf16[128,512]{1,0:T(8,128)(2,1)S(1)} %get-tuple-element.109), channel_id=1, source_target_pairs={{0,8},{4,12},{8,0},{12,4},{16,24},{20,28},{24,16},{28,20},{1,9},{5... | collective-permute-start | bytes 393224 | tf_op jit(solution)/shard_map/ppermute | solution.py:435
  35.3 1.0 copy-start.3
  47.3 30.1 %copy-start.5 = (bf16[128,512]{1,0:T(8,128)(2,1)}, bf16[128,512]{1,0:T(8,128)(2,1)S(1)}, u32[]{:S(2)}) copy-start(bf16[128,512]{1,0:T(8,128)(2,1)S(1)} %get-tuple-element.104.refs_6_) | copy-start | bytes 393220
  47.3 7.9 %collective-permute-start.7 = (bf16[128,512]{1,0:T(8,128)(2,1)S(1)}, bf16[128,512]{1,0:T(8,128)(2,1)S(1)}, u32[]{:S(2)}, u32[]{:S(2)}) collective-permute-start(bf16[128,512]{1,0:T(8,128)(2,1)S(1)} %get-tuple-element.104.refs_6_), channel_id=1, source_target_pairs={{0,1},{1,0},{2,3},{3,2},{4,5},{5,4},{6,7},{7,6},{8,9},{9,8},{10,11... | collective-permute-start | bytes 393224 | tf_op jit(solution)/shard_map/ppermute | solution.py:429
  47.6 29.8 %collective-permute-start.16 = (bf16[128,512]{1,0:T(8,128)(2,1)S(1)}, bf16[128,512]{1,0:T(8,128)(2,1)S(1)}, u32[]{:S(2)}, u32[]{:S(2)}) collective-permute-start(bf16[128,512]{1,0:T(8,128)(2,1)S(1)} %get-tuple-element.104.refs_6_), channel_id=1, source_target_pairs={{0,0},{1,8},{2,16},{3,24},{4,4},{5,12},{6,20},{7,28},{8,1},{9,9},{... | collective-permute-start | bytes 393224 | tf_op jit(solution)/shard_map/ppermute | solution.py:503
  48.4 29.0 %collective-permute-start.13 = (bf16[256,512]{1,0:T(8,128)(2,1)}, bf16[256,512]{1,0:T(8,128)(2,1)S(1)}, u32[]{:S(2)}, u32[]{:S(2)}) collective-permute-start(bf16[256,512]{1,0:T(8,128)(2,1)} %get-tuple-element.72), channel_id=1, source_target_pairs={{0,8},{4,12},{8,0},{12,4},{16,24},{20,28},{24,16},{28,20},{1,9},{5... | collective-permute-start | bytes 786440 | tf_op jit(solution)/shard_map/ppermute | solution.py:435
  51.8 25.6 %collective-permute-start.14 = (bf16[256,512]{1,0:T(8,128)(2,1)}, bf16[256,512]{1,0:T(8,128)(2,1)S(1)}, u32[]{:S(2)}, u32[]{:S(2)}) collective-permute-start(bf16[256,512]{1,0:T(8,128)(2,1)} %get-tuple-element.74), channel_id=1, source_target_pairs={{0,16},{4,20},{8,24},{12,28},{16,0},{20,4},{24,8},{28,12},{1,17},{... | collective-permute-start | bytes 786440 | tf_op jit(solution)/shard_map/ppermute | solution.py:435
  55.2 22.2 %collective-permute-start.15 = (bf16[256,512]{1,0:T(8,128)(2,1)}, bf16[256,512]{1,0:T(8,128)(2,1)S(1)}, u32[]{:S(2)}, u32[]{:S(2)}) collective-permute-start(bf16[256,512]{1,0:T(8,128)(2,1)} %get-tuple-element.76), channel_id=1, source_target_pairs={{0,24},{4,28},{8,16},{12,20},{16,8},{20,12},{24,0},{28,4},{1,25},{... | collective-permute-start | bytes 786440 | tf_op jit(solution)/shard_map/ppermute | solution.py:435
  55.2 22.2 %copy-start.12 = (bf16[128,512]{1,0:T(8,128)(2,1)}, bf16[128,512]{1,0:T(8,128)(2,1)S(1)}, u32[]{:S(2)}) copy-start(bf16[128,512]{1,0:T(8,128)(2,1)S(1)} %collective-permute-done.7.refs_7_) | copy-start | bytes 393220
  55.2 8.7 %collective-permute-start.8 = (bf16[2,128,512]{2,1,0:T(8,128)(2,1)S(1)}, bf16[2,128,512]{2,1,0:T(8,128)(2,1)S(1)}, u32[]{:S(2)}, u32[]{:S(2)}) collective-permute-start(bf16[2,128,512]{2,1,0:T(8,128)(2,1)S(1)} %pad_maximum_fusion), channel_id=1, source_target_pairs={{0,2},{1,3},{2,0},{3,1},{4,6},{5,7},{6,4},{7,5},{8,10},{9,11},{10,... | collective-permute-start | bytes 786440 | tf_op jit(solution)/shard_map/ppermute | solution.py:429
  63.9 13.5 %copy-start.20 = (bf16[2,128,512]{2,1,0:T(8,128)(2,1)}, bf16[2,128,512]{2,1,0:T(8,128)(2,1)S(1)}, u32[]{:S(2)}) copy-start(bf16[2,128,512]{2,1,0:T(8,128)(2,1)S(1)} %collective-permute-done.8.refs_8_) | copy-start | bytes 786436
  77.5 44.1 %copy-start.4 = (bf16[1152,512]{1,0:T(8,128)(2,1)}, bf16[1152,512]{1,0:T(8,128)(2,1)S(1)}, u32[]{:S(2)}) copy-start(bf16[1152,512]{1,0:T(8,128)(2,1)S(1)} %constant_dynamic-update-slice_fusion.refs_1_) | copy-start | bytes 3538948
  77.5 44.6 %collective-permute-start.21 = (bf16[1152,512]{1,0:T(8,128)(2,1)S(1)}, bf16[1152,512]{1,0:T(8,128)(2,1)S(1)}, u32[]{:S(2)}, u32[]{:S(2)}) collective-permute-start(bf16[1152,512]{1,0:T(8,128)(2,1)S(1)} %constant_dynamic-update-slice_fusion.refs_1_), channel_id=1, source_target_pairs={{0,2},{1,3},{2,0},{3,1},{4,6},{5,7},{6,4},{7,5},{8,10},{9,11},{10,... | collective-permute-start | bytes 3538952 | tf_op jit(solution)/shard_map/ppermute | solution.py:429
  79.5 16.3 %collective-permute-start.10 = (bf16[128,1152]{1,0:T(8,128)(2,1)}, bf16[128,1152]{1,0:T(8,128)(2,1)S(1)}, u32[]{:S(2)}, u32[]{:S(2)}) collective-permute-start(bf16[128,1152]{1,0:T(8,128)(2,1)} %get-tuple-element.62.refs_9_.refs_5_), channel_id=1, source_target_pairs={{0,16},{4,20},{8,24},{12,28},{16,0},{20,4},{24,8},{28,12},{1,17},{... | collective-permute-start | bytes 884744 | tf_op jit(solution)/shard_map/ppermute | solution.py:435
  81.6 14.9 %collective-permute-start.9 = (bf16[128,1152]{1,0:T(8,128)(2,1)}, bf16[128,1152]{1,0:T(8,128)(2,1)S(1)}, u32[]{:S(2)}, u32[]{:S(2)}) collective-permute-start(bf16[128,1152]{1,0:T(8,128)(2,1)} %get-tuple-element.62.refs_9_.refs_5_), channel_id=1, source_target_pairs={{0,8},{4,12},{8,0},{12,4},{16,24},{20,28},{24,16},{28,20},{1,9},{5... | collective-permute-start | bytes 884744 | tf_op jit(solution)/shard_map/ppermute | solution.py:435
  95.9 26.3 %copy-start.17 = (bf16[128,1152]{1,0:T(8,128)(2,1)}, bf16[128,1152]{1,0:T(8,128)(2,1)S(1)}, u32[]{:S(2)}) copy-start(bf16[128,1152]{1,0:T(8,128)(2,1)S(1)} %collective-permute-done.10.refs_7_) | copy-start | bytes 884740
  96.5 25.0 %copy-start.18 = (bf16[128,1152]{1,0:T(8,128)(2,1)}, bf16[128,1152]{1,0:T(8,128)(2,1)S(1)}, u32[]{:S(2)}) copy-start(bf16[128,1152]{1,0:T(8,128)(2,1)S(1)} %collective-permute-done.9.refs_6_) | copy-start | bytes 884740
  96.5 11.2 %collective-permute-start.11 = (bf16[128,1152]{1,0:T(8,128)(2,1)}, bf16[128,1152]{1,0:T(8,128)(2,1)S(1)}, u32[]{:S(2)}, u32[]{:S(2)}) collective-permute-start(bf16[128,1152]{1,0:T(8,128)(2,1)} %get-tuple-element.68.refs_3_.refs_9_), channel_id=1, source_target_pairs={{0,8},{4,12},{8,0},{12,4},{16,24},{20,28},{24,16},{28,20},{1,9},{5... | collective-permute-start | bytes 884744 | tf_op jit(solution)/shard_map/ppermute | solution.py:435
  97.5 15.7 %collective-permute-start.12 = (bf16[128,1152]{1,0:T(8,128)(2,1)}, bf16[128,1152]{1,0:T(8,128)(2,1)S(1)}, u32[]{:S(2)}, u32[]{:S(2)}) collective-permute-start(bf16[128,1152]{1,0:T(8,128)(2,1)} %get-tuple-element.68.refs_3_.refs_9_), channel_id=1, source_target_pairs={{0,16},{4,20},{8,24},{12,28},{16,0},{20,4},{24,8},{28,12},{1,17},{... | collective-permute-start | bytes 884744 | tf_op jit(solution)/shard_map/ppermute | solution.py:435
  107.7 13.8 %copy-start.6 = (bf16[128,1152]{1,0:T(8,128)(2,1)}, bf16[128,1152]{1,0:T(8,128)(2,1)S(1)}, u32[]{:S(2)}) copy-start(bf16[128,1152]{1,0:T(8,128)(2,1)S(1)} %collective-permute-done.11.refs_4_.refs_10_) | copy-start | bytes 884740
  113.3 8.9 %copy-start.7 = (bf16[128,1152]{1,0:T(8,128)(2,1)}, bf16[128,1152]{1,0:T(8,128)(2,1)S(1)}, u32[]{:S(2)}) copy-start(bf16[128,1152]{1,0:T(8,128)(2,1)S(1)} %collective-permute-done.12.refs_5_.refs_11_) | copy-start | bytes 884740
  121.5 3.6 %collective-permute-start.18 = (bf16[1040,512]{1,0:T(8,128)(2,1)}, bf16[1040,512]{1,0:T(8,128)(2,1)S(1)}, u32[]{:S(2)}, u32[]{:S(2)}) collective-permute-start(bf16[1040,512]{1,0:T(8,128)(2,1)} %get-tuple-element.88), channel_id=1, source_target_pairs={{0,1},{1,0},{2,3},{3,2},{4,5},{5,4},{6,7},{7,6},{8,9},{9,8},{10,11... | collective-permute-start | bytes 3194888 | tf_op jit(solution)/shard_map/ppermute | solution.py:429
  121.6 10.4 %collective-permute-start.20 = (bf16[1152,512]{1,0:T(8,128)(2,1)S(1)}, bf16[1152,512]{1,0:T(8,128)(2,1)S(1)}, u32[]{:S(2)}, u32[]{:S(2)}) collective-permute-start(bf16[1152,512]{1,0:T(8,128)(2,1)S(1)} %constant_dynamic-update-slice_fusion.refs_1_), channel_id=1, source_target_pairs={{0,1},{1,0},{2,3},{3,2},{4,5},{5,4},{6,7},{7,6},{8,9},{9,8},{10,11... | collective-permute-start | bytes 3538952 | tf_op jit(solution)/shard_map/ppermute | solution.py:429
  122.1 9.9 %copy-start.9 = (bf16[1152,512]{1,0:T(8,128)(2,1)}, bf16[1152,512]{1,0:T(8,128)(2,1)S(1)}, u32[]{:S(2)}) copy-start(bf16[1152,512]{1,0:T(8,128)(2,1)S(1)} %collective-permute-done.21.refs_3_) | copy-start | bytes 3538948
  122.1 9.9 %collective-permute-start.22 = (bf16[1152,512]{1,0:T(8,128)(2,1)S(1)}, bf16[1152,512]{1,0:T(8,128)(2,1)S(1)}, u32[]{:S(2)}, u32[]{:S(2)}) collective-permute-start(bf16[1152,512]{1,0:T(8,128)(2,1)S(1)} %collective-permute-done.21.refs_3_), channel_id=1, source_target_pairs={{0,1},{1,0},{2,3},{3,2},{4,5},{5,4},{6,7},{7,6},{8,9},{9,8},{10,11... | collective-permute-start | bytes 3538952 | tf_op jit(solution)/shard_map/ppermute | solution.py:429
  122.2 9.8 %collective-permute-start.23 = (bf16[128,1152]{1,0:T(8,128)(2,1)S(1)}, bf16[128,1152]{1,0:T(8,128)(2,1)S(1)}, u32[]{:S(2)}, u32[]{:S(2)}) collective-permute-start(bf16[128,1152]{1,0:T(8,128)(2,1)S(1)} %collective-permute-done.10.refs_7_), channel_id=1, source_target_pairs={{0,8},{4,12},{8,0},{12,4},{16,24},{20,28},{24,16},{28,20},{1,9},{5... | collective-permute-start | bytes 884744 | tf_op jit(solution)/shard_map/ppermute | solution.py:435
  122.2 22.8 %collective-permute-start.24 = (bf16[128,1152]{1,0:T(8,128)(2,1)S(1)}, bf16[128,1152]{1,0:T(8,128)(2,1)S(1)}, u32[]{:S(2)}, u32[]{:S(2)}) collective-permute-start(bf16[128,1152]{1,0:T(8,128)(2,1)S(1)} %collective-permute-done.12.refs_5_.refs_11_), channel_id=1, source_target_pairs={{0,8},{4,12},{8,0},{12,4},{16,24},{20,28},{24,16},{28,20},{1,9},{5... | collective-permute-start | bytes 884744 | tf_op jit(solution)/shard_map/ppermute | solution.py:435
  125.1 38.1 %collective-permute-start.17 = (bf16[1040,512]{1,0:T(8,128)(2,1)}, bf16[1040,512]{1,0:T(8,128)(2,1)}, u32[]{:S(2)}, u32[]{:S(2)}) collective-permute-start(bf16[1040,512]{1,0:T(8,128)(2,1)} %get-tuple-element.86), channel_id=1, source_target_pairs={{0,1},{1,0},{2,3},{3,2},{4,5},{5,4},{6,7},{7,6},{8,9},{9,8},{10,11... | collective-permute-start | bytes 3194888 | tf_op jit(solution)/shard_map/ppermute | solution.py:429
  132.0 27.4 %collective-permute-start.19 = (bf16[1040,512]{1,0:T(8,128)(2,1)}, bf16[1040,512]{1,0:T(8,128)(2,1)}, u32[]{:S(2)}, u32[]{:S(2)}) collective-permute-start(bf16[1040,512]{1,0:T(8,128)(2,1)} %add_convert_fusion), channel_id=1, source_target_pairs={{0,2},{1,3},{2,0},{3,1},{4,6},{5,7},{6,4},{7,5},{8,10},{9,11},{10,... | collective-permute-start | bytes 3194888 | tf_op jit(solution)/shard_map/ppermute | solution.py:429
  132.0 1.1 copy-start.10
  133.1 1.1 copy-start.11
  141.2 17.4 %collective-permute-start.27 = (bf16[512,256]{1,0:T(8,128)(2,1)}, bf16[512,256]{1,0:T(8,128)(2,1)S(1)}, u32[]{:S(2)}, u32[]{:S(2)}) collective-permute-start(bf16[512,256]{1,0:T(8,128)(2,1)} %get-tuple-element.101), channel_id=1, source_target_pairs={{0,4},{4,0},{8,12},{12,8},{16,20},{20,16},{24,28},{28,24},{1,5},{5... | collective-permute-start | bytes 786440 | tf_op jit(solution)/shard_map/ppermute | solution.py:432
  150.5 8.0 %copy-start.16 = (f32[512,256]{1,0:T(8,128)S(1)}, f32[512,256]{1,0:T(8,128)}, u32[]{:S(2)}) copy-start(f32[512,256]{1,0:T(8,128)} %get-tuple-element.100) | copy-start | bytes 1572868
  150.6 15.7 %collective-permute-start.25 = (bf16[2,256,512]{2,1,0:T(8,128)(2,1)}, bf16[2,256,512]{2,1,0:T(8,128)(2,1)}, u32[]{:S(2)}, u32[]{:S(2)}) collective-permute-start(bf16[2,256,512]{2,1,0:T(8,128)(2,1)} %get-tuple-element.92), channel_id=1, source_target_pairs={{0,4},{4,0},{8,12},{12,8},{16,20},{20,16},{24,28},{28,24},{1,5},{5... | collective-permute-start | bytes 1572872 | tf_op jit(solution)/shard_map/ppermute | solution.py:432
  157.0 12.3 %collective-permute-start.26 = (bf16[256,512]{1,0:T(8,128)(2,1)}, bf16[256,512]{1,0:T(8,128)(2,1)}, u32[]{:S(2)}, u32[]{:S(2)}) collective-permute-start(bf16[256,512]{1,0:T(8,128)(2,1)} %get-tuple-element.94), channel_id=1, source_target_pairs={{0,4},{4,0},{8,12},{12,8},{16,20},{20,16},{24,28},{28,24},{1,5},{5... | collective-permute-start | bytes 786440 | tf_op jit(solution)/shard_map/ppermute | solution.py:432
  158.6 4.6 %copy-start.1 = (bf16[128,8,512]{2,1,0:T(8,128)(2,1)S(1)}, bf16[128,8,512]{2,1,0:T(8,128)(2,1)}, u32[]{:S(2)}) copy-start(bf16[128,8,512]{2,1,0:T(8,128)(2,1)} %param.14) | copy-start | bytes 3145732
  163.2 3.0 %copy-start.13 = (f32[256,512]{1,0:T(8,128)S(1)}, f32[256,512]{1,0:T(8,128)}, u32[]{:S(2)}) copy-start(f32[256,512]{1,0:T(8,128)} %get-tuple-element.99) | copy-start | bytes 1572868
  163.2 3.0 %copy-start.14 = (f32[256,512]{1,0:T(8,128)S(1)}, f32[256,512]{1,0:T(8,128)}, u32[]{:S(2)}) copy-start(f32[256,512]{1,0:T(8,128)} %get-tuple-element.96) | copy-start | bytes 1572868
  166.2 3.1 %copy-start.15 = (f32[256,512]{1,0:T(8,128)S(1)}, f32[256,512]{1,0:T(8,128)}, u32[]{:S(2)}) copy-start(f32[256,512]{1,0:T(8,128)} %get-tuple-element.98) | copy-start | bytes 1572868
  (2 other events, 1.4 us)

commit v4 on v3

--- a/solution.py
+++ b/solution.py
@@ -15,7 +15,7 @@
 LIMIT = 56 * 2**20
 SCALE = 1.15e9
 COSTS = [0.1, 0.1, 0.1, 5, 0.1, 0.1, 5, 0.1, 0.1]
-TIES = [1, 2, 1, 0, 2, 1, 0, 0, 1, 1, 1, 1, 0, 0, 1, 1, 0, 0, 0, 0, 1, 1, 1, 0]
+TIES = [1, 1, 1, 0, 1, 1, 0, 1, 1, 1, 1, 1, 0, 0, 1, 1, 0, 0, 0, 1, 0, 1, 1, 1]
 
 
 def dot(left, right):
@@ -115,6 +115,14 @@
     owners = jnp.concatenate([owned[a, :] for a in at], axis=0)
     onehot = jnp.where(owners == occ[...], 1.0, 0.0).astype(BF)
     out[...] = dot(onehot, get(grads)[...]).astype(out.dtype)
+
+
+def add_kernel(idx, keep, took, own, *pieces):
+    f_dev = own.shape[0]
+    own[...] = keep[0:f_dev, :] + took[0:f_dev, :].astype(F32)
+    for k, piece in enumerate(pieces, 1):
+        at = slice(k * f_dev, (k + 1) * f_dev)
+        piece[...] = (keep[at, :] + took[at, :].astype(F32)).astype(BF)
 
 
 def norm_rows(m, tile, sources, gain, normed, recip):
@@ -454,8 +462,12 @@
     keep = sums(False, F32, owned_col)
     flat2 = after(flat2, keep, when=TIES[11])
     flat1 = flip(flat, 1)
-    both = (keep + took.astype(F32)).reshape(n_out, f_dev, cols)
-    pieces = [both[k].astype(BF) for k in range(1, n_out)]
+    own_sum, *pieces = call(
+        add_kernel,
+        (idx, keep, took),
+        [((f_dev, cols), F32)] + [((f_dev, cols), BF)] * (n_out - 1),
+        0.1,
+    )
     came = [cross(piece, k) for k, piece in enumerate(pieces, 1)]
     flat2 = after(flat2, *pieces, when=TIES[23])
     flat3 = flip(flat2, 1)
@@ -475,7 +487,7 @@
     square = (4, heads * fq, quarter)
     tall = ((4, heads * fq, width), BF)
     def sums_over_tok(*before):
-        total = both[0]
+        total = own_sum
         for piece in came:
             total = total + after(piece, *before).astype(F32)
         grad0 = total.astype(BF)
@@ -522,9 +534,10 @@
         early1, early2 = after(early1, late), after(early2, late)
     early_all = (early, early1, early2, cross(early2, 1) if TIES[10] else cross(early, 3))
     sent = after(late, early1, early2, when=TIES[21])
-    late1, late2 = cross(sent, 1), cross(sent, 2)
-    gate = after(lmask, late1, when=TIES[4])
-    gate = after(gate, late2, when=TIES[4] > 1)
+    late2 = cross(sent, 2)
+    late13 = cross(jnp.stack([sent, late2]), 1)
+    gate = after(lmask, late2, when=TIES[4])
+    gate = after(gate, early_all[3], when=TIES[5])
     gate = after(gate, early1, early2, when=TIES[14])
     whole = jnp.concatenate([sends[0]] + far_rows + [turned])
     from2 = flip(after(whole, late, when=TIES[3]), 2)
@@ -543,7 +556,7 @@
     across = (d2.astype(F32) + beside[1].astype(F32)).astype(BF)
     own = d0.astype(F32) + beside[0].astype(F32)
 
-    late_all = (late, late1, late2, cross(after(late2, late1, when=TIES[5]), 1))
+    late_all = (late, late13[0], late2, late13[1])
 
 
     f_all = n_out * f_dev

time: 172 us -> 163 us (0.948)
  waiting for transfers between devices: 48.5 us -> 40.2 us
  other arithmetic: 19.9 us -> 14.4 us
  starting transfers between devices: 28.9 us -> 34.1 us
  Pallas kernels: 63.1 us -> 65.3 us
  local copies, waits for them, and re-layouts: 9.54 us -> 7.41 us
    ppermute x11, waiting for transfers between devices: 17.5 us -> 3.58 us  [flip(): return lax.ppermute(array, 'mdl', [(i, i ^ bit) for i in range(4)])]
    ppermute x4, waiting for transfers between devices: 0.85 us -> 10.7 us  [swap(): return lax.ppermute(array, 'tok', [(i, i ^ 1) for i in range(n_tok)])]
    ppermute x11, starting transfers between devices: 6.41 us -> 11.4 us  [flip(): return lax.ppermute(array, 'mdl', [(i, i ^ bit) for i in range(4)])]
    ppermute x12 -> x11, waiting for transfers between devices: 30.1 us -> 26 us  [cross(): return lax.ppermute(array, 'tok', [(i, i ^ 2 * k) for i in range(n_tok)])]
    another operation x1, other arithmetic: 2.8 us -> 0.06 us  [on_device(): late13 = cross(jnp.stack([sent, late2]), 1)]
    unnamed x48 -> x52, local copies, waits for them, and re-layouts: 4.89 us -> 2.56 us
    pallas_call x8 -> x9, Pallas kernels: 59.8 us -> 61.9 us  [call(): pl.pallas_call(kernel, in_specs=in_specs, out_specs=out_specs, out_shape=...]
    ppermute x12 -> x11, starting transfers between devices: 16.4 us -> 16.5 us  [cross(): return lax.ppermute(array, 'tok', [(i, i ^ 2 * k) for i in range(n_tok)])]
  transfers between devices with their start and end apart: 28 -> 27, of which waited for: 10 -> 10; matrix products, arithmetic and copies ran while one was open for 13% -> 10% of each run, Pallas kernels for 37% -> 40%
where the time goes in v4:
time: 163 us
  Pallas kernels  65.3 us (40%)
  waiting for transfers between devices  40.2 us (25%)
  starting transfers between devices  34.1 us (21%)
  other arithmetic  14.4 us (9%)
  local copies, waits for them, and re-layouts  7.41 us (5%)
    pallas_call x9, Pallas kernels, call(): pl.pallas_call(kernel, in_specs=in_specs, out_specs=out_specs, out_shape=...  61.9 us
    ppermute x11, waiting for transfers between devices, cross(): return lax.ppermute(array, 'tok', [(i, i ^ 2 * k) for i in range(n_tok)])  26 us
    ppermute x11, starting transfers between devices, cross(): return lax.ppermute(array, 'tok', [(i, i ^ 2 * k) for i in range(n_tok)])  16.5 us
    ppermute x11, starting transfers between devices, flip(): return lax.ppermute(array, 'mdl', [(i, i ^ bit) for i in range(4)])  11.4 us
    ppermute x4, waiting for transfers between devices, swap(): return lax.ppermute(array, 'tok', [(i, i ^ 1) for i in range(n_tok)])  10.7 us
    ppermute x4, starting transfers between devices, swap(): return lax.ppermute(array, 'tok', [(i, i ^ 1) for i in range(n_tok)])  5.28 us
    ppermute x11, waiting for transfers between devices, flip(): return lax.ppermute(array, 'mdl', [(i, i ^ bit) for i in range(4)])  3.58 us
    pallas_call x1, Pallas kernels, norm_quarter(): pl.pallas_call(quarter_kernel, grid_spec=pltpu.PrefetchScalarGridSpec(num...  3.44 us
  transfers between devices with their start and end apart: 27, of which 10 were waited for; matrix products, arithmetic and copies ran while one was open for 10% of the time, Pallas kernels for 40%

profile of v4, /device:TPU:0, one launch (start us, length us, event | category | flops | bytes accessed | tf_op | source)
XLA Modules:
  0.0 162.6 jit_solution(16260518103966113033)
XLA Ops:
  0.6 3.0 %collective-permute-start.1 = (bf16[1024,512]{1,0:T(8,128)(2,1)}, bf16[1024,512]{1,0:T(8,128)(2,1)S(1)}, u32[]{:S(2)}, u32[]{:S(2)}) collective-permute-start(bf16[1024,512]{1,0:T(8,128)(2,1)} %bitcast.34), channel_id=1, source_target_pairs={{0,2},{1,3},{2,0},{3,1},{4,6},{5,7},{6,4},{7,5},{8,10},{9,11},{10,... | collective-permute-start | bytes 3145736 | tf_op jit(solution)/shard_map/ppermute | solution.py:437
  3.7 1.7 %copy.19.refs_1_ = s32[1024,1]{1,0:T(8,128)} copy(s32[1024,1]{0,1:T(1,128)} %bitcast.46) | data formatting | bytes 8192 | tf_op jit(solution)/shard_map/reshape | solution.py:448
  6.0 4.7 %shard_map.138 = bf16[512,512]{1,0:T(8,128)(2,1)} custom-call(s32[4]{0:T(128)} %pad_add_fusion.refs_0_.idx, s32[1024,1]{1,0:T(8,128)} %copy.19.refs_1_, s32[1,2048]{1,0:T(1,128)} %bitcast.44, bf16[2048,512]{1,0:T(8,128)(2,1)} %refs_3_.4), custom_call_target="tpu_custom_call" | custom-call | flops 115000000 | tf_op jit(solution)/shard_map/pallas_call | solution.py:97
  10.7 1.6 collective-permute-start.2
  12.3 4.9 %shard_map.137.refs_1_ = f32[512,512]{1,0:T(8,128)} custom-call(s32[4]{0:T(128)} %pad_add_fusion.refs_0_.idx, s32[1024,1]{1,0:T(8,128)} %copy.19.refs_1_, s32[1,2048]{1,0:T(1,128)} %bitcast.45, bf16[2048,512]{1,0:T(8,128)(2,1)} %refs_3_.4), custom_call_target="tpu_custom_call" | custom-call | flops 115000000 | tf_op jit(solution)/shard_map/pallas_call | solution.py:97
  17.2 7.2 %collective-permute-done.2.refs_2_ = bf16[512,512]{1,0:T(8,128)(2,1)S(1)} collective-permute-done((bf16[512,512]{1,0:T(8,128)(2,1)}, bf16[512,512]{1,0:T(8,128)(2,1)S(1)}, u32[]{:S(2)}, u32[]{:S(2)}) %collective-permute-start.2) | collective-permute-done | bytes 524320 | tf_op jit(solution)/shard_map/ppermute | solution.py:440
  24.4 0.8 copy-done.15
  25.2 2.2 %shard_map.139 = (f32[128,512]{1,0:T(8,128)}, bf16[128,512]{1,0:T(8,128)(2,1)}, bf16[128,512]{1,0:T(8,128)(2,1)}, bf16[128,512]{1,0:T(8,128)(2,1)}) custom-call(s32[4]{0:T(128)} %pad_add_fusion.refs_0_.idx, f32[512,512]{1,0:T(8,128)} %shard_map.137.refs_1_, bf16[512,512]{1,0:T(8,128)(2,1)} %copy-done.15), custom_call_target="tpu_custom_call" | custom-call | flops 115000000 | tf_op jit(solution)/shard_map/pallas_call | solution.py:97
  27.6 1.6 collective-permute-start.4
  29.2 2.6 %collective-permute-start.5 = (bf16[128,512]{1,0:T(8,128)(2,1)}, bf16[128,512]{1,0:T(8,128)(2,1)S(1)}, u32[]{:S(2)}, u32[]{:S(2)}) collective-permute-start(bf16[128,512]{1,0:T(8,128)(2,1)} %get-tuple-element.60), channel_id=1, source_target_pairs={{0,16},{4,20},{8,24},{12,28},{16,0},{20,4},{24,8},{28,12},{1,17},{... | collective-permute-start | bytes 393224 | tf_op jit(solution)/shard_map/ppermute | solution.py:443
  32.5 0.9 copy-done.4
  33.4 3.4 %shard_map.140 = (bf16[256,512]{1,0:T(8,128)(2,1)}, bf16[256,512]{1,0:T(8,128)(2,1)}, bf16[256,512]{1,0:T(8,128)(2,1)}, bf16[256,512]{1,0:T(8,128)(2,1)}) custom-call(s32[4]{0:T(128)} %pad_add_fusion.refs_0_.idx, bf16[1024,512]{1,0:T(8,128)(2,1)} %bitcast.35, bf16[1024,512]{1,0:T(8,128)(2,1)} %copy-done.4, bf16[1024,512]{1,0:T(8,128)(2,1)} %copy-done.3, ...), custom_call_target="tpu_custom_call" | custom-call | flops 115000000 | tf_op jit(solution)/shard_map/pallas_call | solution.py:162
  36.9 5.4 %collective-permute-done.5 = bf16[128,512]{1,0:T(8,128)(2,1)S(1)} collective-permute-done((bf16[128,512]{1,0:T(8,128)(2,1)}, bf16[128,512]{1,0:T(8,128)(2,1)S(1)}, u32[]{:S(2)}, u32[]{:S(2)}) %collective-permute-start.5) | collective-permute-done | bytes 131104 | tf_op jit(solution)/shard_map/ppermute | solution.py:443
  42.9 1.0 fusion.7
  44.0 0.8 collective-permute-start.16
  44.8 3.5 %collective-permute-start.7 = (bf16[128,512]{1,0:T(8,128)(2,1)S(1)}, bf16[128,512]{1,0:T(8,128)(2,1)S(1)}, u32[]{:S(2)}, u32[]{:S(2)}) collective-permute-start(bf16[128,512]{1,0:T(8,128)(2,1)S(1)} %get-tuple-element.112.refs_6_), channel_id=1, source_target_pairs={{0,1},{1,0},{2,3},{3,2},{4,5},{5,4},{6,7},{7,6},{8,9},{9,8},{10,11... | collective-permute-start | bytes 393224 | tf_op jit(solution)/shard_map/ppermute | solution.py:437
  48.4 2.2 %collective-permute-start.14 = (bf16[256,512]{1,0:T(8,128)(2,1)}, bf16[256,512]{1,0:T(8,128)(2,1)S(1)}, u32[]{:S(2)}, u32[]{:S(2)}) collective-permute-start(bf16[256,512]{1,0:T(8,128)(2,1)} %get-tuple-element.82), channel_id=1, source_target_pairs={{0,16},{4,20},{8,24},{12,28},{16,0},{20,4},{24,8},{28,12},{1,17},{... | collective-permute-start | bytes 786440 | tf_op jit(solution)/shard_map/ppermute | solution.py:443
  51.1 1.7 %collective-permute-start.15 = (bf16[256,512]{1,0:T(8,128)(2,1)}, bf16[256,512]{1,0:T(8,128)(2,1)S(1)}, u32[]{:S(2)}, u32[]{:S(2)}) collective-permute-start(bf16[256,512]{1,0:T(8,128)(2,1)} %get-tuple-element.84), channel_id=1, source_target_pairs={{0,24},{4,28},{8,16},{12,20},{16,8},{20,12},{24,0},{28,4},{1,25},{... | collective-permute-start | bytes 786440 | tf_op jit(solution)/shard_map/ppermute | solution.py:443
  53.4 13.4 %shard_map.141 = (bf16[128,1152]{1,0:T(8,128)(2,1)}, f32[4,128,256]{2,1,0:T(8,128)}, f32[4,128,256]{2,1,0:T(8,128)}, bf16[4,128,2048]{2,1,0:T(8,128)(2,1)}, bf16...) custom-call(s32[4]{0:T(128)} %pad_add_fusion.refs_0_.idx, bf16[1024,512]{1,0:T(8,128)(2,1)} %bitcast.36, ...), custom_call_target="tpu_custom_call" | custom-call | flops 115000000 | tf_op jit(solution)/shard_map/pallas_call | solution.py:97
  66.9 2.5 %collective-permute-start.8 = (bf16[2,128,512]{2,1,0:T(8,128)(2,1)S(1)}, bf16[2,128,512]{2,1,0:T(8,128)(2,1)S(1)}, u32[]{:S(2)}, u32[]{:S(2)}) collective-permute-start(bf16[2,128,512]{2,1,0:T(8,128)(2,1)S(1)} %pad_maximum_fusion.1), channel_id=1, source_target_pairs={{0,2},{1,3},{2,0},{3,1},{4,6},{5,7},{6,4},{7,5},{8,10},{9,11},{10,... | collective-permute-start | bytes 786440 | tf_op jit(solution)/shard_map/ppermute | solution.py:437
  69.4 3.0 %collective-permute-done.14 = bf16[256,512]{1,0:T(8,128)(2,1)S(1)} collective-permute-done((bf16[256,512]{1,0:T(8,128)(2,1)}, bf16[256,512]{1,0:T(8,128)(2,1)S(1)}, u32[]{:S(2)}, u32[]{:S(2)}) %collective-permute-start.14) | collective-permute-done | bytes 262176 | tf_op jit(solution)/shard_map/ppermute | solution.py:443
  72.6 3.6 %collective-permute-done.8.refs_8_ = bf16[2,128,512]{2,1,0:T(8,128)(2,1)S(1)} collective-permute-done((bf16[2,128,512]{2,1,0:T(8,128)(2,1)S(1)}, bf16[2,128,512]{2,1,0:T(8,128)(2,1)S(1)}, u32[]{:S(2)}, u32[]{:S(2)}) %collective-permute-start.8) | collective-permute-done | bytes 262176 | tf_op jit(solution)/shard_map/ppermute | solution.py:437
  76.2 3.8 %collective-permute-start.10 = (bf16[128,1152]{1,0:T(8,128)(2,1)S(1)}, bf16[128,1152]{1,0:T(8,128)(2,1)S(1)}, u32[]{:S(2)}, u32[]{:S(2)}) collective-permute-start(bf16[128,1152]{1,0:T(8,128)(2,1)S(1)} %copy-done.7), channel_id=1, source_target_pairs={{0,16},{4,20},{8,24},{12,28},{16,0},{20,4},{24,8},{28,12},{1,17},{... | collective-permute-start | bytes 884744 | tf_op jit(solution)/shard_map/ppermute | solution.py:443
  79.9 11.0 %shard_map.142 = (bf16[128,1152]{1,0:T(8,128)(2,1)}, f32[4,256]{1,0:T(4,128)}, bf16[4,128,2048]{2,1,0:T(8,128)(2,1)}, bf16[4,128,256]{2,1,0:T(8,128)(2,1)}, bf16[4,128,256]{2,1,0:T(8,128)(2,1)}) custom-call(s32[4]{0:T(128)} %pad_add_fusion.refs_0_.idx, bf16[1024,2048]{1,0:T(8,128)(2,1)} %get-tuple-element.70.refs_1_, bf16[2048,512]{1,0:T(8,128)(2,1)} %refs_2_.1, ...), custom_call_target="tpu_custom_call" | custom-call | flops 115000000 | tf_op jit(solution)/shard_map/pallas_call | solution.py:97
  91.0 1.7 %collective-permute-done.10.refs_7_ = bf16[128,1152]{1,0:T(8,128)(2,1)S(1)} collective-permute-done((bf16[128,1152]{1,0:T(8,128)(2,1)S(1)}, bf16[128,1152]{1,0:T(8,128)(2,1)S(1)}, u32[]{:S(2)}, u32[]{:S(2)}) %collective-permute-start.10) | collective-permute-done | bytes 294944 | tf_op jit(solution)/shard_map/ppermute | solution.py:443
  92.7 2.5 %collective-permute-start.11 = (bf16[128,1152]{1,0:T(8,128)(2,1)}, bf16[128,1152]{1,0:T(8,128)(2,1)S(1)}, u32[]{:S(2)}, u32[]{:S(2)}) collective-permute-start(bf16[128,1152]{1,0:T(8,128)(2,1)} %get-tuple-element.76.refs_3_.refs_9_), channel_id=1, source_target_pairs={{0,16},{4,20},{8,24},{12,28},{16,0},{20,4},{24,8},{28,12},{1,17},{... | collective-permute-start | bytes 884744 | tf_op jit(solution)/shard_map/ppermute | solution.py:443
  95.5 12.8 %collective-permute-done.11.refs_5_.refs_11_ = bf16[128,1152]{1,0:T(8,128)(2,1)S(1)} collective-permute-done((bf16[128,1152]{1,0:T(8,128)(2,1)}, bf16[128,1152]{1,0:T(8,128)(2,1)S(1)}, u32[]{:S(2)}, u32[]{:S(2)}) %collective-permute-start.11) | collective-permute-done | bytes 294944 | tf_op jit(solution)/shard_map/ppermute | solution.py:443
  108.8 8.1 %shard_map.143 = (bf16[1040,512]{1,0:T(8,128)(2,1)}, bf16[1040,512]{1,0:T(8,128)(2,1)}, bf16[1040,512]{1,0:T(8,128)(2,1)}, bf16[1040,512]{1,0:T(8,128)(2,1)}) custom-call(s32[4]{0:T(128)} %pad_add_fusion.refs_0_.idx, bf16[2048,512]{1,0:T(8,128)(2,1)} %refs_1_.1, f32[4,1,256]{2,1,0:T(1,128)} %get-tuple-element.87.refs_10_.refs_5_.refs_2_, ...), custom_call_target="tpu_custom_call" | custom-call | flops 115000000 | tf_op jit(solution)/shard_map/pallas_call | solution.py:97
  117.6 0.8 dynamic_slice.3
  118.5 1.2 reduce
  120.0 1.2 collective-permute-start.23
  121.3 1.8 %add_convert_fusion = bf16[1040,512]{1,0:T(8,128)(2,1)S(1)} fusion(bf16[1040,512]{1,0:T(8,128)(2,1)} %collective-permute-done.18, bf16[1040,512]{1,0:T(8,128)(2,1)} %get-tuple-element.95), kind=kLoop, calls=%fused_computation | loop fusion | flops 2129920 | bytes 3194880 | tf_op jit(solution)/shard_map/convert_element_type | solution.py:556
  123.1 1.5 collective-permute-start.19
  124.6 7.0 %shard_map.144 = (f32[512,256]{1,0:T(8,128)}, bf16[512,256]{1,0:T(8,128)(2,1)}, bf16[4,512,512]{2,1,0:T(8,128)(2,1)}, bf16[512,512]{1,0:T(8,128)(2,1)}) custom-call(s32[4]{0:T(128)} %pad_add_fusion.refs_0_.idx, bf16[1152,512]{1,0:T(8,128)(2,1)} %copy-done.6, bf16[1152,512]{1,0:T(8,128)(2,1)} %collective-permute-done.20.refs_2_, bf16[1152,512]{1,0:T(8,128)(2,1)} %copy-done.9, ...), custom_call_target="tpu_custom_call" | custom-call | flops 5750000128 | tf_op jit(solution)/shard_map/pallas_call | solution.py:97
  131.6 1.6 collective-permute-start.26
  133.2 2.5 %collective-permute-done.23 = bf16[2,128,1152]{2,1,0:T(8,128)(2,1)S(1)} collective-permute-done((bf16[2,128,1152]{2,1,0:T(8,128)(2,1)S(1)}, bf16[2,128,1152]{2,1,0:T(8,128)(2,1)S(1)}, u32[]{:S(2)}, u32[]{:S(2)}) %collective-permute-start.23) | collective-permute-done | bytes 589856 | tf_op jit(solution)/shard_map/ppermute | solution.py:443
  135.7 0.9 slice_bitcast_fusion
  136.5 4.8 %shard_map.145 = (f32[256,512]{1,0:T(8,128)}, f32[256,512]{1,0:T(8,128)}, bf16[2,256,512]{2,1,0:T(8,128)(2,1)}) custom-call(s32[4]{0:T(128)} %pad_add_fusion.refs_0_.idx, bf16[4,512,512]{2,1,0:T(8,128)(2,1)} %get-tuple-element.98.refs_1_, bf16[512,512]{1,0:T(8,128)(2,1)} %get-tuple-element.99.refs_2_, bf16[128,1152]{1,0:T(8,128)(2,1)} %get-tuple-element.76.refs_3_.refs_9_, ...), custom_call_target="tpu_custom_call" | custom-call | flops 115000000 | tf_op jit(solution)/shard_map/pallas_call | solution.py:97
  141.4 1.5 collective-permute-start.24
  142.9 5.8 %shard_map.146 = (f32[256,512]{1,0:T(8,128)}, bf16[256,512]{1,0:T(8,128)(2,1)}) custom-call(s32[4]{0:T(128)} %pad_add_fusion.refs_0_.idx, bf16[1152,512]{1,0:T(8,128)(2,1)} %copy-done.6, bf16[1152,512]{1,0:T(8,128)(2,1)} %collective-permute-done.20.refs_2_, bf16[1152,512]{1,0:T(8,128)(2,1)} %copy-done.9, bf16[1152,512]{1,0:T(8,128)(2,1)} %collective-permute-done.22.refs_4_, ...), custom_call_target="tpu_custom_call" | custom-call | flops 115000000 | tf_op jit(solution)/shard_map/pallas_call | solution.py:97
  149.4 0.8 convert_add_fusion.3
  150.5 0.7 mul.68
  151.2 0.8 multiply_multiply_fusion
  152.1 3.0 %fusion.5 = bf16[128,8,512]{2,1,0:T(8,128)(2,1)} fusion(f32[1040,512]{1,0:T(8,128)S(1)} %convert_element_type.101, bf16[128,8,512]{2,1,0:T(8,128)(2,1)S(1)} %copy-done.1, bf16[1040,512]{1,0:T(8,128)(2,1)} %collective-permute-done.17, bf16[1040,512]{1,0:T(8,128)(2,1)} %get-tuple-element.93, f32[128,512]{1,0:T(8,128)S(1)} %get-tuple-element.111, ...), kind=kLoop, calls=%fused_computation.7 | loop fusion | flops 6291456 | bytes 6564864 | tf_op jit(solution)/shard_map/convert_element_type | solution.py:607
  155.1 1.5 collective-permute-done.24
  156.6 2.1 %convert_add_fusion = (f32[256,512]{1,0:T(8,128)}, f32[256,512]{1,0:T(8,128)}) fusion(f32[256,512]{1,0:T(8,128)S(1)} %copy-done.11, bf16[2,256,512]{2,1,0:T(8,128)(2,1)} %collective-permute-done.24, f32[256,512]{1,0:T(8,128)S(1)} %copy-done.12), kind=kLoop, calls=%fused_computation.9 | loop fusion | flops 524288 | bytes 2621440 | tf_op jit(solution)/shard_map/add | solution.py:594
  158.8 2.0 %collective-permute-done.25 = bf16[256,512]{1,0:T(8,128)(2,1)} collective-permute-done((bf16[256,512]{1,0:T(8,128)(2,1)}, bf16[256,512]{1,0:T(8,128)(2,1)}, u32[]{:S(2)}, u32[]{:S(2)}) %collective-permute-start.25) | collective-permute-done | bytes 262176 | tf_op jit(solution)/shard_map/ppermute | solution.py:440
  160.8 1.8 %convert_add_fusion.2 = f32[256,512]{1,0:T(8,128)} fusion(f32[256,512]{1,0:T(8,128)S(1)} %copy-done.13, bf16[256,512]{1,0:T(8,128)(2,1)} %collective-permute-done.25), kind=kLoop, calls=%fused_computation.11 | loop fusion | flops 262144 | bytes 1310720 | tf_op jit(solution)/shard_map/add | solution.py:596
  (100 shorter events, 6.4 us)
Async XLA Ops:
  0.6 11.7 %copy-start = (bf16[128,8,512]{2,1,0:T(8,128)(2,1)S(1)}, bf16[128,8,512]{2,1,0:T(8,128)(2,1)}, u32[]{:S(2)}) copy-start(bf16[128,8,512]{2,1,0:T(8,128)(2,1)} %param.14) | copy-start | bytes 3145732
  0.6 26.8 %collective-permute-start.1 = (bf16[1024,512]{1,0:T(8,128)(2,1)}, bf16[1024,512]{1,0:T(8,128)(2,1)S(1)}, u32[]{:S(2)}, u32[]{:S(2)}) collective-permute-start(bf16[1024,512]{1,0:T(8,128)(2,1)} %bitcast.34), channel_id=1, source_target_pairs={{0,2},{1,3},{2,0},{3,1},{4,6},{5,7},{6,4},{7,5},{8,10},{9,11},{10,... | collective-permute-start | bytes 3145736 | tf_op jit(solution)/shard_map/ppermute | solution.py:437
  10.7 16.8 %copy-start.23 = (s32[128,8]{0,1:T(8,128)S(1)}, s32[128,8]{0,1:T(8,128)}, u32[]{:S(2)}) copy-start(s32[128,8]{0,1:T(8,128)} %param.13) | copy-start | bytes 12292
  10.7 13.7 %collective-permute-start.2 = (bf16[512,512]{1,0:T(8,128)(2,1)}, bf16[512,512]{1,0:T(8,128)(2,1)S(1)}, u32[]{:S(2)}, u32[]{:S(2)}) collective-permute-start(bf16[512,512]{1,0:T(8,128)(2,1)} %shard_map.138), channel_id=1, source_target_pairs={{0,4},{4,0},{8,12},{12,8},{16,20},{20,16},{24,28},{28,24},{1,5},{5... | collective-permute-start | bytes 1572872 | tf_op jit(solution)/shard_map/ppermute | solution.py:440
  12.3 20.2 %collective-permute-start = (bf16[1024,512]{1,0:T(8,128)(2,1)S(1)}, bf16[1024,512]{1,0:T(8,128)(2,1)S(1)}, u32[]{:S(2)}, u32[]{:S(2)}) collective-permute-start(bf16[1024,512]{1,0:T(8,128)(2,1)S(1)} %bitcast.37), channel_id=1, source_target_pairs={{0,1},{1,0},{2,3},{3,2},{4,5},{5,4},{6,7},{7,6},{8,9},{9,8},{10,11... | collective-permute-start | bytes 3145736 | tf_op jit(solution)/shard_map/ppermute | solution.py:437
  27.4 5.1 %copy-start.3 = (bf16[1024,512]{1,0:T(8,128)(2,1)}, bf16[1024,512]{1,0:T(8,128)(2,1)S(1)}, u32[]{:S(2)}) copy-start(bf16[1024,512]{1,0:T(8,128)(2,1)S(1)} %collective-permute-done.1.x2.refs_3_) | copy-start | bytes 3145732
  27.4 5.1 %collective-permute-start.3 = (bf16[1024,512]{1,0:T(8,128)(2,1)S(1)}, bf16[1024,512]{1,0:T(8,128)(2,1)}, u32[]{:S(2)}, u32[]{:S(2)}) collective-permute-start(bf16[1024,512]{1,0:T(8,128)(2,1)S(1)} %collective-permute-done.1.x2.refs_3_), channel_id=1, source_target_pairs={{0,1},{1,0},{2,3},{3,2},{4,5},{5,4},{6,7},{7,6},{8,9},{9,8},{10,11... | collective-permute-start | bytes 3145736 | tf_op jit(solution)/shard_map/ppermute | solution.py:437
  27.6 9.3 %collective-permute-start.4 = (bf16[128,512]{1,0:T(8,128)(2,1)}, bf16[128,512]{1,0:T(8,128)(2,1)S(1)}, u32[]{:S(2)}, u32[]{:S(2)}) collective-permute-start(bf16[128,512]{1,0:T(8,128)(2,1)} %get-tuple-element.59), channel_id=1, source_target_pairs={{0,8},{4,12},{8,0},{12,4},{16,24},{20,28},{24,16},{28,20},{1,9},{5... | collective-permute-start | bytes 393224 | tf_op jit(solution)/shard_map/ppermute | solution.py:443
  29.2 13.1 %collective-permute-start.5 = (bf16[128,512]{1,0:T(8,128)(2,1)}, bf16[128,512]{1,0:T(8,128)(2,1)S(1)}, u32[]{:S(2)}, u32[]{:S(2)}) collective-permute-start(bf16[128,512]{1,0:T(8,128)(2,1)} %get-tuple-element.60), channel_id=1, source_target_pairs={{0,16},{4,20},{8,24},{12,28},{16,0},{20,4},{24,8},{28,12},{1,17},{... | collective-permute-start | bytes 393224 | tf_op jit(solution)/shard_map/ppermute | solution.py:443
  31.8 10.5 %collective-permute-start.6 = (bf16[128,512]{1,0:T(8,128)(2,1)}, bf16[128,512]{1,0:T(8,128)(2,1)}, u32[]{:S(2)}, u32[]{:S(2)}) collective-permute-start(bf16[128,512]{1,0:T(8,128)(2,1)} %get-tuple-element.61), channel_id=1, source_target_pairs={{0,24},{4,28},{8,16},{12,20},{16,8},{20,12},{24,0},{28,4},{1,25},{... | collective-permute-start | bytes 393224 | tf_op jit(solution)/shard_map/ppermute | solution.py:443
  33.4 9.5 %copy-start.21 = (f32[128,512]{1,0:T(8,128)S(1)}, f32[128,512]{1,0:T(8,128)}, u32[]{:S(2)}) copy-start(f32[128,512]{1,0:T(8,128)} %get-tuple-element.63) | copy-start | bytes 786436
  44.0 22.9 %copy-start.8 = (bf16[128,512]{1,0:T(8,128)(2,1)}, bf16[128,512]{1,0:T(8,128)(2,1)S(1)}, u32[]{:S(2)}) copy-start(bf16[128,512]{1,0:T(8,128)(2,1)S(1)} %get-tuple-element.112.refs_6_) | copy-start | bytes 393220
  44.0 22.9 %collective-permute-start.16 = (bf16[128,512]{1,0:T(8,128)(2,1)S(1)}, bf16[128,512]{1,0:T(8,128)(2,1)S(1)}, u32[]{:S(2)}, u32[]{:S(2)}) collective-permute-start(bf16[128,512]{1,0:T(8,128)(2,1)S(1)} %get-tuple-element.112.refs_6_), channel_id=1, source_target_pairs={{0,0},{1,8},{2,16},{3,24},{4,4},{5,12},{6,20},{7,28},{8,1},{9,9},{... | collective-permute-start | bytes 393224 | tf_op jit(solution)/shard_map/ppermute | solution.py:515
  44.8 22.0 %collective-permute-start.7 = (bf16[128,512]{1,0:T(8,128)(2,1)S(1)}, bf16[128,512]{1,0:T(8,128)(2,1)S(1)}, u32[]{:S(2)}, u32[]{:S(2)}) collective-permute-start(bf16[128,512]{1,0:T(8,128)(2,1)S(1)} %get-tuple-element.112.refs_6_), channel_id=1, source_target_pairs={{0,1},{1,0},{2,3},{3,2},{4,5},{5,4},{6,7},{7,6},{8,9},{9,8},{10,11... | collective-permute-start | bytes 393224 | tf_op jit(solution)/shard_map/ppermute | solution.py:437
  48.4 24.0 %collective-permute-start.14 = (bf16[256,512]{1,0:T(8,128)(2,1)}, bf16[256,512]{1,0:T(8,128)(2,1)S(1)}, u32[]{:S(2)}, u32[]{:S(2)}) collective-permute-start(bf16[256,512]{1,0:T(8,128)(2,1)} %get-tuple-element.82), channel_id=1, source_target_pairs={{0,16},{4,20},{8,24},{12,28},{16,0},{20,4},{24,8},{28,12},{1,17},{... | collective-permute-start | bytes 786440 | tf_op jit(solution)/shard_map/ppermute | solution.py:443
  50.6 21.8 %collective-permute-start.13 = (bf16[256,512]{1,0:T(8,128)(2,1)}, bf16[256,512]{1,0:T(8,128)(2,1)S(1)}, u32[]{:S(2)}, u32[]{:S(2)}) collective-permute-start(bf16[256,512]{1,0:T(8,128)(2,1)} %get-tuple-element.80), channel_id=1, source_target_pairs={{0,8},{4,12},{8,0},{12,4},{16,24},{20,28},{24,16},{28,20},{1,9},{5... | collective-permute-start | bytes 786440 | tf_op jit(solution)/shard_map/ppermute | solution.py:443
  51.1 21.4 %collective-permute-start.15 = (bf16[256,512]{1,0:T(8,128)(2,1)}, bf16[256,512]{1,0:T(8,128)(2,1)S(1)}, u32[]{:S(2)}, u32[]{:S(2)}) collective-permute-start(bf16[256,512]{1,0:T(8,128)(2,1)} %get-tuple-element.84), channel_id=1, source_target_pairs={{0,24},{4,28},{8,16},{12,20},{16,8},{20,12},{24,0},{28,4},{1,25},{... | collective-permute-start | bytes 786440 | tf_op jit(solution)/shard_map/ppermute | solution.py:443
  53.4 13.4 %copy-start.20 = (bf16[256,512]{1,0:T(8,128)(2,1)S(1)}, bf16[256,512]{1,0:T(8,128)(2,1)}, u32[]{:S(2)}) copy-start(bf16[256,512]{1,0:T(8,128)(2,1)} %get-tuple-element.64) | copy-start | bytes 786436
  66.8 9.4 %copy-start.7 = (bf16[128,1152]{1,0:T(8,128)(2,1)S(1)}, bf16[128,1152]{1,0:T(8,128)(2,1)}, u32[]{:S(2)}) copy-start(bf16[128,1152]{1,0:T(8,128)(2,1)} %get-tuple-element.75.refs_9_.refs_5_) | copy-start | bytes 884740
  66.9 13.1 %copy-start.10 = (bf16[128,512]{1,0:T(8,128)(2,1)}, bf16[128,512]{1,0:T(8,128)(2,1)S(1)}, u32[]{:S(2)}) copy-start(bf16[128,512]{1,0:T(8,128)(2,1)S(1)} %collective-permute-done.7.refs_7_) | copy-start | bytes 393220
  66.9 9.2 %collective-permute-start.8 = (bf16[2,128,512]{2,1,0:T(8,128)(2,1)S(1)}, bf16[2,128,512]{2,1,0:T(8,128)(2,1)S(1)}, u32[]{:S(2)}, u32[]{:S(2)}) collective-permute-start(bf16[2,128,512]{2,1,0:T(8,128)(2,1)S(1)} %pad_maximum_fusion.1), channel_id=1, source_target_pairs={{0,2},{1,3},{2,0},{3,1},{4,6},{5,7},{6,4},{7,5},{8,10},{9,11},{10,... | collective-permute-start | bytes 786440 | tf_op jit(solution)/shard_map/ppermute | solution.py:437
  72.5 44.5 %copy-start.6 = (bf16[1152,512]{1,0:T(8,128)(2,1)}, bf16[1152,512]{1,0:T(8,128)(2,1)S(1)}, u32[]{:S(2)}) copy-start(bf16[1152,512]{1,0:T(8,128)(2,1)S(1)} %constant_dynamic-update-slice_fusion.refs_1_) | copy-start | bytes 3538948
  72.5 45.0 %collective-permute-start.21 = (bf16[1152,512]{1,0:T(8,128)(2,1)S(1)}, bf16[1152,512]{1,0:T(8,128)(2,1)S(1)}, u32[]{:S(2)}, u32[]{:S(2)}) collective-permute-start(bf16[1152,512]{1,0:T(8,128)(2,1)S(1)} %constant_dynamic-update-slice_fusion.refs_1_), channel_id=1, source_target_pairs={{0,2},{1,3},{2,0},{3,1},{4,6},{5,7},{6,4},{7,5},{8,10},{9,11},{10,... | collective-permute-start | bytes 3538952 | tf_op jit(solution)/shard_map/ppermute | solution.py:437
  76.2 3.8 %copy-start.19 = (bf16[2,128,512]{2,1,0:T(8,128)(2,1)}, bf16[2,128,512]{2,1,0:T(8,128)(2,1)S(1)}, u32[]{:S(2)}) copy-start(bf16[2,128,512]{2,1,0:T(8,128)(2,1)S(1)} %collective-permute-done.8.refs_8_) | copy-start | bytes 786436
  76.2 16.5 %collective-permute-start.10 = (bf16[128,1152]{1,0:T(8,128)(2,1)S(1)}, bf16[128,1152]{1,0:T(8,128)(2,1)S(1)}, u32[]{:S(2)}, u32[]{:S(2)}) collective-permute-start(bf16[128,1152]{1,0:T(8,128)(2,1)S(1)} %copy-done.7), channel_id=1, source_target_pairs={{0,16},{4,20},{8,24},{12,28},{16,0},{20,4},{24,8},{28,12},{1,17},{... | collective-permute-start | bytes 884744 | tf_op jit(solution)/shard_map/ppermute | solution.py:443
  79.9 12.8 %collective-permute-start.9 = (bf16[128,1152]{1,0:T(8,128)(2,1)S(1)}, bf16[128,1152]{1,0:T(8,128)(2,1)S(1)}, u32[]{:S(2)}, u32[]{:S(2)}) collective-permute-start(bf16[128,1152]{1,0:T(8,128)(2,1)S(1)} %copy-done.7), channel_id=1, source_target_pairs={{0,8},{4,12},{8,0},{12,4},{16,24},{20,28},{24,16},{28,20},{1,9},{5... | collective-permute-start | bytes 884744 | tf_op jit(solution)/shard_map/ppermute | solution.py:443
  92.7 24.2 %copy-start.16 = (bf16[128,1152]{1,0:T(8,128)(2,1)}, bf16[128,1152]{1,0:T(8,128)(2,1)S(1)}, u32[]{:S(2)}) copy-start(bf16[128,1152]{1,0:T(8,128)(2,1)S(1)} %collective-permute-done.10.refs_7_) | copy-start | bytes 884740
  92.7 24.2 %copy-start.17 = (bf16[128,1152]{1,0:T(8,128)(2,1)}, bf16[128,1152]{1,0:T(8,128)(2,1)S(1)}, u32[]{:S(2)}) copy-start(bf16[128,1152]{1,0:T(8,128)(2,1)S(1)} %collective-permute-done.9.refs_6_) | copy-start | bytes 884740
  92.7 15.6 %collective-permute-start.11 = (bf16[128,1152]{1,0:T(8,128)(2,1)}, bf16[128,1152]{1,0:T(8,128)(2,1)S(1)}, u32[]{:S(2)}, u32[]{:S(2)}) collective-permute-start(bf16[128,1152]{1,0:T(8,128)(2,1)} %get-tuple-element.76.refs_3_.refs_9_), channel_id=1, source_target_pairs={{0,16},{4,20},{8,24},{12,28},{16,0},{20,4},{24,8},{28,12},{1,17},{... | collective-permute-start | bytes 884744 | tf_op jit(solution)/shard_map/ppermute | solution.py:443
  95.2 13.6 %collective-permute-start.12 = (bf16[128,1152]{1,0:T(8,128)(2,1)S(1)}, bf16[128,1152]{1,0:T(8,128)(2,1)S(1)}, u32[]{:S(2)}, u32[]{:S(2)}) collective-permute-start(bf16[128,1152]{1,0:T(8,128)(2,1)S(1)} %collective-permute-done.10.refs_7_), channel_id=1, source_target_pairs={{0,8},{4,12},{8,0},{12,4},{16,24},{20,28},{24,16},{28,20},{1,9},{5... | collective-permute-start | bytes 884744 | tf_op jit(solution)/shard_map/ppermute | solution.py:443
  108.3 11.6 %copy-start.5 = (bf16[128,1152]{1,0:T(8,128)(2,1)}, bf16[128,1152]{1,0:T(8,128)(2,1)S(1)}, u32[]{:S(2)}) copy-start(bf16[128,1152]{1,0:T(8,128)(2,1)S(1)} %collective-permute-done.11.refs_5_.refs_11_) | copy-start | bytes 884740
  108.8 8.1 %copy-start.18 = (bf16[128,1152]{1,0:T(8,128)(2,1)}, bf16[128,1152]{1,0:T(8,128)(2,1)S(1)}, u32[]{:S(2)}) copy-start(bf16[128,1152]{1,0:T(8,128)(2,1)S(1)} %collective-permute-done.12.refs_8_) | copy-start | bytes 884740
  108.8 11.1 %copy-start.2 = (bf16[128,1152]{1,0:T(8,128)(2,1)S(1)}, bf16[128,1152]{1,0:T(8,128)(2,1)}, u32[]{:S(2)}) copy-start(bf16[128,1152]{1,0:T(8,128)(2,1)} %get-tuple-element.76.refs_3_.refs_9_) | copy-start | bytes 884740
  116.9 4.4 %collective-permute-start.18 = (bf16[1040,512]{1,0:T(8,128)(2,1)}, bf16[1040,512]{1,0:T(8,128)(2,1)}, u32[]{:S(2)}, u32[]{:S(2)}) collective-permute-start(bf16[1040,512]{1,0:T(8,128)(2,1)} %get-tuple-element.96), channel_id=1, source_target_pairs={{0,1},{1,0},{2,3},{3,2},{4,5},{5,4},{6,7},{7,6},{8,9},{9,8},{10,11... | collective-permute-start | bytes 3194888 | tf_op jit(solution)/shard_map/ppermute | solution.py:437
  117.0 7.6 %collective-permute-start.20 = (bf16[1152,512]{1,0:T(8,128)(2,1)S(1)}, bf16[1152,512]{1,0:T(8,128)(2,1)}, u32[]{:S(2)}, u32[]{:S(2)}) collective-permute-start(bf16[1152,512]{1,0:T(8,128)(2,1)S(1)} %constant_dynamic-update-slice_fusion.refs_1_), channel_id=1, source_target_pairs={{0,1},{1,0},{2,3},{3,2},{4,5},{5,4},{6,7},{7,6},{8,9},{9,8},{10,11... | collective-permute-start | bytes 3538952 | tf_op jit(solution)/shard_map/ppermute | solution.py:437
  117.5 5.6 %copy-start.9 = (bf16[1152,512]{1,0:T(8,128)(2,1)}, bf16[1152,512]{1,0:T(8,128)(2,1)S(1)}, u32[]{:S(2)}) copy-start(bf16[1152,512]{1,0:T(8,128)(2,1)S(1)} %collective-permute-done.21.refs_3_) | copy-start | bytes 3538948
  117.5 7.1 %collective-permute-start.22 = (bf16[1152,512]{1,0:T(8,128)(2,1)S(1)}, bf16[1152,512]{1,0:T(8,128)(2,1)}, u32[]{:S(2)}, u32[]{:S(2)}) collective-permute-start(bf16[1152,512]{1,0:T(8,128)(2,1)S(1)} %collective-permute-done.21.refs_3_), channel_id=1, source_target_pairs={{0,1},{1,0},{2,3},{3,2},{4,5},{5,4},{6,7},{7,6},{8,9},{9,8},{10,11... | collective-permute-start | bytes 3538952 | tf_op jit(solution)/shard_map/ppermute | solution.py:437
  120.0 15.7 %collective-permute-start.23 = (bf16[2,128,1152]{2,1,0:T(8,128)(2,1)S(1)}, bf16[2,128,1152]{2,1,0:T(8,128)(2,1)S(1)}, u32[]{:S(2)}, u32[]{:S(2)}) collective-permute-start(bf16[2,128,1152]{2,1,0:T(8,128)(2,1)S(1)} %pad_maximum_fusion), channel_id=1, source_target_pairs={{0,8},{4,12},{8,0},{12,4},{16,24},{20,28},{24,16},{28,20},{1,9},{5... | collective-permute-start | bytes 1769480 | tf_op jit(solution)/shard_map/ppermute | solution.py:443
  121.2 30.9 %collective-permute-start.17 = (bf16[1040,512]{1,0:T(8,128)(2,1)}, bf16[1040,512]{1,0:T(8,128)(2,1)}, u32[]{:S(2)}, u32[]{:S(2)}) collective-permute-start(bf16[1040,512]{1,0:T(8,128)(2,1)} %get-tuple-element.94), channel_id=1, source_target_pairs={{0,1},{1,0},{2,3},{3,2},{4,5},{5,4},{6,7},{7,6},{8,9},{9,8},{10,11... | collective-permute-start | bytes 3194888 | tf_op jit(solution)/shard_map/ppermute | solution.py:437
  123.1 27.1 %collective-permute-start.19 = (bf16[1040,512]{1,0:T(8,128)(2,1)S(1)}, bf16[1040,512]{1,0:T(8,128)(2,1)S(1)}, u32[]{:S(2)}, u32[]{:S(2)}) collective-permute-start(bf16[1040,512]{1,0:T(8,128)(2,1)S(1)} %add_convert_fusion), channel_id=1, source_target_pairs={{0,2},{1,3},{2,0},{3,1},{4,6},{5,7},{6,4},{7,5},{8,10},{9,11},{10,... | collective-permute-start | bytes 3194888 | tf_op jit(solution)/shard_map/ppermute | solution.py:437
  131.6 17.7 %collective-permute-start.26 = (bf16[512,256]{1,0:T(8,128)(2,1)}, bf16[512,256]{1,0:T(8,128)(2,1)S(1)}, u32[]{:S(2)}, u32[]{:S(2)}) collective-permute-start(bf16[512,256]{1,0:T(8,128)(2,1)} %get-tuple-element.109), channel_id=1, source_target_pairs={{0,4},{4,0},{8,12},{12,8},{16,20},{20,16},{24,28},{28,24},{1,5},{5... | collective-permute-start | bytes 786440 | tf_op jit(solution)/shard_map/ppermute | solution.py:440
  141.4 8.0 %copy-start.14 = (f32[512,256]{1,0:T(8,128)S(1)}, f32[512,256]{1,0:T(8,128)}, u32[]{:S(2)}) copy-start(f32[512,256]{1,0:T(8,128)} %get-tuple-element.108) | copy-start | bytes 1572868
  141.4 15.2 %collective-permute-start.24 = (bf16[2,256,512]{2,1,0:T(8,128)(2,1)}, bf16[2,256,512]{2,1,0:T(8,128)(2,1)}, u32[]{:S(2)}, u32[]{:S(2)}) collective-permute-start(bf16[2,256,512]{2,1,0:T(8,128)(2,1)} %get-tuple-element.100), channel_id=1, source_target_pairs={{0,4},{4,0},{8,12},{12,8},{16,20},{20,16},{24,28},{28,24},{1,5},{5... | collective-permute-start | bytes 1572872 | tf_op jit(solution)/shard_map/ppermute | solution.py:440
  148.7 12.0 %collective-permute-start.25 = (bf16[256,512]{1,0:T(8,128)(2,1)}, bf16[256,512]{1,0:T(8,128)(2,1)}, u32[]{:S(2)}, u32[]{:S(2)}) collective-permute-start(bf16[256,512]{1,0:T(8,128)(2,1)} %get-tuple-element.102), channel_id=1, source_target_pairs={{0,4},{4,0},{8,12},{12,8},{16,20},{20,16},{24,28},{28,24},{1,5},{5... | collective-permute-start | bytes 786440 | tf_op jit(solution)/shard_map/ppermute | solution.py:440
  149.4 2.7 %copy-start.1 = (bf16[128,8,512]{2,1,0:T(8,128)(2,1)S(1)}, bf16[128,8,512]{2,1,0:T(8,128)(2,1)}, u32[]{:S(2)}) copy-start(bf16[128,8,512]{2,1,0:T(8,128)(2,1)} %param.14) | copy-start | bytes 3145732
  152.1 4.5 %copy-start.11 = (f32[256,512]{1,0:T(8,128)S(1)}, f32[256,512]{1,0:T(8,128)}, u32[]{:S(2)}) copy-start(f32[256,512]{1,0:T(8,128)} %get-tuple-element.107) | copy-start | bytes 1572868
  152.1 4.5 %copy-start.12 = (f32[256,512]{1,0:T(8,128)S(1)}, f32[256,512]{1,0:T(8,128)}, u32[]{:S(2)}) copy-start(f32[256,512]{1,0:T(8,128)} %get-tuple-element.104) | copy-start | bytes 1572868
  155.1 5.6 %copy-start.13 = (f32[256,512]{1,0:T(8,128)S(1)}, f32[256,512]{1,0:T(8,128)}, u32[]{:S(2)}) copy-start(f32[256,512]{1,0:T(8,128)} %get-tuple-element.106) | copy-start | bytes 1572868
  (3 other events, 2.4 us)

commit v5 on v4

--- a/solution.py
+++ b/solution.py
@@ -375,8 +375,9 @@
     out_other[...] = tdot(att[...], all_grads[:, far]).astype(BF)
 
 
-def value_kernel(heads, idx, z_value, z_last, l0, l1, l2, l3, value_mine, query_mine, other, d_all, dq_all):
+def value_kernel(heads, idx, z_value, z_last, l0, l2, l13, value_mine, query_mine, other, d_all, dq_all):
     m, x = idx[0], idx[2]
+    l1, l3 = l13.at[0], l13.at[1]
     half, cols = value_mine.shape
     fq = l0.shape[0] // 4
     for k in range(4):
@@ -397,11 +398,12 @@
 
 
 def key_kernel(flen, heads, idx, b0, b1, b2, b3, *refs):
-    early, late, refs = refs[:4], refs[4:8], refs[8:]
+    early, late, refs = refs[:4], [get(r) for r in refs[4:7]], refs[7:]
+    late = [late[0], late[2].at[0], late[1], late[2].at[1]]
     mine, other, z_all, q_all = refs
     m, x = idx[0], idx[2]
     half, cols = mine.shape
-    fq = late[0].ref.shape[0] // 4
+    fq = late[0].shape[0] // 4
     at = [pl.ds(pl.multiple_of((m ^ k) * fq, fq), fq) for k in range(4)]
     last = slice(2 * cols, 2 * cols + 128)
     coefs = [jnp.concatenate([get(item)[a, last] for item in late], axis=0) for a in at]
@@ -556,7 +558,7 @@
     across = (d2.astype(F32) + beside[1].astype(F32)).astype(BF)
     own = d0.astype(F32) + beside[0].astype(F32)
 
-    late_all = (late, late13[0], late2, late13[1])
+    late_all = (late, late2, late13)
 
 
     f_all = n_out * f_dev
@@ -588,7 +590,7 @@
         [((feats, cols), F32), ((feats, cols), BF)],
         COSTS[8],
         [pltpu.VMEM((heads, f_all, 2 * feats), BF), pltpu.VMEM((f_all, cols), BF)],
-        later=(9, 10, 11, 12, 1, 2, 3, 4, 5, 6, 7, 8),
+        later=(9, 10, 11, 1, 2, 3, 4, 5, 6, 7, 8),
     )
     came = after(swap(both_other), key_other, when=TIES[8])
     value_grad = value_mine + came[0].astype(F32)

time: 163 us -> 164 us (level)
  waiting for transfers between devices: 40.2 us -> 37.6 us
  other arithmetic: 14.4 us -> 16.1 us
    ppermute x11, waiting for transfers between devices: 26 us -> 22.7 us  [cross(): return lax.ppermute(array, 'tok', [(i, i ^ 2 * k) for i in range(n_tok)])]
    ppermute x11, waiting for transfers between devices: 3.58 us -> 6.11 us  [flip(): return lax.ppermute(array, 'mdl', [(i, i ^ bit) for i in range(4)])]
    ppermute x4, waiting for transfers between devices: 10.7 us -> 8.76 us  [swap(): return lax.ppermute(array, 'tok', [(i, i ^ 1) for i in range(n_tok)])]
    unnamed x52 -> x58, local copies, waits for them, and re-layouts: 2.56 us -> 4.33 us
  transfers between devices with their start and end apart: 27 -> 27, of which waited for: 10 -> 10; matrix products, arithmetic and copies ran while one was open for 10% -> 11% of each run, Pallas kernels for 40% -> 40%
where the time goes in v5:
time: 164 us; the launch traced here: 163 us
  Pallas kernels  65.5 us (40%)
  waiting for transfers between devices  37.6 us (23%)
  starting transfers between devices  34.9 us (21%)
  other arithmetic  16.1 us (10%)
  local copies, waits for them, and re-layouts  8.28 us (5%)
    pallas_call x9, Pallas kernels, call(): pl.pallas_call(kernel, in_specs=in_specs, out_specs=out_specs, out_shape=...  62.1 us
    ppermute x11, waiting for transfers between devices, cross(): return lax.ppermute(array, 'tok', [(i, i ^ 2 * k) for i in range(n_tok)])  22.7 us
    ppermute x11, starting transfers between devices, cross(): return lax.ppermute(array, 'tok', [(i, i ^ 2 * k) for i in range(n_tok)])  17.2 us
    ppermute x11, starting transfers between devices, flip(): return lax.ppermute(array, 'mdl', [(i, i ^ bit) for i in range(4)])  11.6 us
    ppermute x4, waiting for transfers between devices, swap(): return lax.ppermute(array, 'tok', [(i, i ^ 1) for i in range(n_tok)])  8.76 us
    ppermute x11, waiting for transfers between devices, flip(): return lax.ppermute(array, 'mdl', [(i, i ^ bit) for i in range(4)])  6.11 us
    ppermute x4, starting transfers between devices, swap(): return lax.ppermute(array, 'tok', [(i, i ^ 1) for i in range(n_tok)])  5.28 us
    unnamed x58, local copies, waits for them, and re-layouts  4.33 us
  transfers between devices with their start and end apart: 27, of which 10 were waited for; matrix products, arithmetic and copies ran while one was open for 11% of the time, Pallas kernels for 40%

profile of v5, /device:TPU:0, one launch (start us, length us, event | category | flops | bytes accessed | tf_op | source)
XLA Modules:
  0.0 163.4 jit_solution(6235318711701101534)
XLA Ops:
  0.6 3.0 %collective-permute-start.1 = (bf16[1024,512]{1,0:T(8,128)(2,1)}, bf16[1024,512]{1,0:T(8,128)(2,1)S(1)}, u32[]{:S(2)}, u32[]{:S(2)}) collective-permute-start(bf16[1024,512]{1,0:T(8,128)(2,1)} %bitcast.30), channel_id=1, source_target_pairs={{0,2},{1,3},{2,0},{3,1},{4,6},{5,7},{6,4},{7,5},{8,10},{9,11},{10,... | collective-permute-start | bytes 3145736 | tf_op jit(solution)/shard_map/ppermute | solution.py:439
  3.7 1.7 %copy.19.refs_1_ = s32[1024,1]{1,0:T(8,128)} copy(s32[1024,1]{0,1:T(1,128)} %bitcast.42) | data formatting | bytes 8192 | tf_op jit(solution)/shard_map/reshape | solution.py:450
  6.0 4.7 %shard_map.138 = bf16[512,512]{1,0:T(8,128)(2,1)} custom-call(s32[4]{0:T(128)} %pad_add_fusion.refs_0_.idx, s32[1024,1]{1,0:T(8,128)} %copy.19.refs_1_, s32[1,2048]{1,0:T(1,128)} %bitcast.40, bf16[2048,512]{1,0:T(8,128)(2,1)} %refs_3_.4), custom_call_target="tpu_custom_call" | custom-call | flops 115000000 | tf_op jit(solution)/shard_map/pallas_call | solution.py:97
  10.7 1.6 collective-permute-start.2
  12.3 4.9 %shard_map.137.refs_1_ = f32[512,512]{1,0:T(8,128)} custom-call(s32[4]{0:T(128)} %pad_add_fusion.refs_0_.idx, s32[1024,1]{1,0:T(8,128)} %copy.19.refs_1_, s32[1,2048]{1,0:T(1,128)} %bitcast.41, bf16[2048,512]{1,0:T(8,128)(2,1)} %refs_3_.4), custom_call_target="tpu_custom_call" | custom-call | flops 115000000 | tf_op jit(solution)/shard_map/pallas_call | solution.py:97
  17.2 7.2 %collective-permute-done.2.refs_2_ = bf16[512,512]{1,0:T(8,128)(2,1)S(1)} collective-permute-done((bf16[512,512]{1,0:T(8,128)(2,1)}, bf16[512,512]{1,0:T(8,128)(2,1)S(1)}, u32[]{:S(2)}, u32[]{:S(2)}) %collective-permute-start.2) | collective-permute-done | bytes 524320 | tf_op jit(solution)/shard_map/ppermute | solution.py:442
  24.4 0.8 copy-done.19
  25.2 2.2 %shard_map.139 = (f32[128,512]{1,0:T(8,128)}, bf16[128,512]{1,0:T(8,128)(2,1)}, bf16[128,512]{1,0:T(8,128)(2,1)}, bf16[128,512]{1,0:T(8,128)(2,1)}) custom-call(s32[4]{0:T(128)} %pad_add_fusion.refs_0_.idx, f32[512,512]{1,0:T(8,128)} %shard_map.137.refs_1_, bf16[512,512]{1,0:T(8,128)(2,1)} %copy-done.19), custom_call_target="tpu_custom_call" | custom-call | flops 115000000 | tf_op jit(solution)/shard_map/pallas_call | solution.py:97
  27.6 1.6 collective-permute-start.4
  29.2 2.6 %collective-permute-start.5 = (bf16[128,512]{1,0:T(8,128)(2,1)}, bf16[128,512]{1,0:T(8,128)(2,1)S(1)}, u32[]{:S(2)}, u32[]{:S(2)}) collective-permute-start(bf16[128,512]{1,0:T(8,128)(2,1)} %get-tuple-element.60), channel_id=1, source_target_pairs={{0,16},{4,20},{8,24},{12,28},{16,0},{20,4},{24,8},{28,12},{1,17},{... | collective-permute-start | bytes 393224 | tf_op jit(solution)/shard_map/ppermute | solution.py:445
  32.5 0.9 copy-done.4
  33.5 3.4 %shard_map.140 = (bf16[256,512]{1,0:T(8,128)(2,1)}, bf16[256,512]{1,0:T(8,128)(2,1)}, bf16[256,512]{1,0:T(8,128)(2,1)}, bf16[256,512]{1,0:T(8,128)(2,1)}) custom-call(s32[4]{0:T(128)} %pad_add_fusion.refs_0_.idx, bf16[1024,512]{1,0:T(8,128)(2,1)} %bitcast.31, bf16[1024,512]{1,0:T(8,128)(2,1)} %copy-done.4, bf16[1024,512]{1,0:T(8,128)(2,1)} %copy-done.3, ...), custom_call_target="tpu_custom_call" | custom-call | flops 115000000 | tf_op jit(solution)/shard_map/pallas_call | solution.py:162
  36.9 5.4 %collective-permute-done.5 = bf16[128,512]{1,0:T(8,128)(2,1)S(1)} collective-permute-done((bf16[128,512]{1,0:T(8,128)(2,1)}, bf16[128,512]{1,0:T(8,128)(2,1)S(1)}, u32[]{:S(2)}, u32[]{:S(2)}) %collective-permute-start.5) | collective-permute-done | bytes 131104 | tf_op jit(solution)/shard_map/ppermute | solution.py:445
  42.3 1.0 fusion.7
  43.3 0.8 collective-permute-start.16
  44.1 4.2 %collective-permute-start.7 = (bf16[128,512]{1,0:T(8,128)(2,1)S(1)}, bf16[128,512]{1,0:T(8,128)(2,1)S(1)}, u32[]{:S(2)}, u32[]{:S(2)}) collective-permute-start(bf16[128,512]{1,0:T(8,128)(2,1)S(1)} %get-tuple-element.112.refs_6_), channel_id=1, source_target_pairs={{0,1},{1,0},{2,3},{3,2},{4,5},{5,4},{6,7},{7,6},{8,9},{9,8},{10,11... | collective-permute-start | bytes 393224 | tf_op jit(solution)/shard_map/ppermute | solution.py:439
  48.3 2.2 %collective-permute-start.14 = (bf16[256,512]{1,0:T(8,128)(2,1)}, bf16[256,512]{1,0:T(8,128)(2,1)S(1)}, u32[]{:S(2)}, u32[]{:S(2)}) collective-permute-start(bf16[256,512]{1,0:T(8,128)(2,1)} %get-tuple-element.82), channel_id=1, source_target_pairs={{0,16},{4,20},{8,24},{12,28},{16,0},{20,4},{24,8},{28,12},{1,17},{... | collective-permute-start | bytes 786440 | tf_op jit(solution)/shard_map/ppermute | solution.py:445
  51.0 1.7 %collective-permute-start.15 = (bf16[256,512]{1,0:T(8,128)(2,1)}, bf16[256,512]{1,0:T(8,128)(2,1)S(1)}, u32[]{:S(2)}, u32[]{:S(2)}) collective-permute-start(bf16[256,512]{1,0:T(8,128)(2,1)} %get-tuple-element.84), channel_id=1, source_target_pairs={{0,24},{4,28},{8,16},{12,20},{16,8},{20,12},{24,0},{28,4},{1,25},{... | collective-permute-start | bytes 786440 | tf_op jit(solution)/shard_map/ppermute | solution.py:445
  53.3 13.4 %shard_map.141 = (bf16[128,1152]{1,0:T(8,128)(2,1)}, f32[4,128,256]{2,1,0:T(8,128)}, f32[4,128,256]{2,1,0:T(8,128)}, bf16[4,128,2048]{2,1,0:T(8,128)(2,1)}, bf16...) custom-call(s32[4]{0:T(128)} %pad_add_fusion.refs_0_.idx, bf16[1024,512]{1,0:T(8,128)(2,1)} %bitcast.32, ...), custom_call_target="tpu_custom_call" | custom-call | flops 115000000 | tf_op jit(solution)/shard_map/pallas_call | solution.py:97
  66.8 2.5 %collective-permute-start.8 = (bf16[2,128,512]{2,1,0:T(8,128)(2,1)S(1)}, bf16[2,128,512]{2,1,0:T(8,128)(2,1)S(1)}, u32[]{:S(2)}, u32[]{:S(2)}) collective-permute-start(bf16[2,128,512]{2,1,0:T(8,128)(2,1)S(1)} %pad_maximum_fusion.1), channel_id=1, source_target_pairs={{0,2},{1,3},{2,0},{3,1},{4,6},{5,7},{6,4},{7,5},{8,10},{9,11},{10,... | collective-permute-start | bytes 786440 | tf_op jit(solution)/shard_map/ppermute | solution.py:439
  69.4 2.9 %collective-permute-done.14 = bf16[256,512]{1,0:T(8,128)(2,1)S(1)} collective-permute-done((bf16[256,512]{1,0:T(8,128)(2,1)}, bf16[256,512]{1,0:T(8,128)(2,1)S(1)}, u32[]{:S(2)}, u32[]{:S(2)}) %collective-permute-start.14) | collective-permute-done | bytes 262176 | tf_op jit(solution)/shard_map/ppermute | solution.py:445
  72.5 3.6 %collective-permute-done.8.refs_8_ = bf16[2,128,512]{2,1,0:T(8,128)(2,1)S(1)} collective-permute-done((bf16[2,128,512]{2,1,0:T(8,128)(2,1)S(1)}, bf16[2,128,512]{2,1,0:T(8,128)(2,1)S(1)}, u32[]{:S(2)}, u32[]{:S(2)}) %collective-permute-start.8) | collective-permute-done | bytes 262176 | tf_op jit(solution)/shard_map/ppermute | solution.py:439
  76.1 3.8 %collective-permute-start.10 = (bf16[128,1152]{1,0:T(8,128)(2,1)S(1)}, bf16[128,1152]{1,0:T(8,128)(2,1)S(1)}, u32[]{:S(2)}, u32[]{:S(2)}) collective-permute-start(bf16[128,1152]{1,0:T(8,128)(2,1)S(1)} %copy-done.8), channel_id=1, source_target_pairs={{0,16},{4,20},{8,24},{12,28},{16,0},{20,4},{24,8},{28,12},{1,17},{... | collective-permute-start | bytes 884744 | tf_op jit(solution)/shard_map/ppermute | solution.py:445
  79.9 11.0 %shard_map.142 = (bf16[128,1152]{1,0:T(8,128)(2,1)}, f32[4,256]{1,0:T(4,128)}, bf16[4,128,2048]{2,1,0:T(8,128)(2,1)}, bf16[4,128,256]{2,1,0:T(8,128)(2,1)}, bf16[4,128,256]{2,1,0:T(8,128)(2,1)}) custom-call(s32[4]{0:T(128)} %pad_add_fusion.refs_0_.idx, bf16[1024,2048]{1,0:T(8,128)(2,1)} %get-tuple-element.70.refs_1_, bf16[2048,512]{1,0:T(8,128)(2,1)} %refs_2_.1, ...), custom_call_target="tpu_custom_call" | custom-call | flops 115000000 | tf_op jit(solution)/shard_map/pallas_call | solution.py:97
  90.9 1.0 collective-permute-done.10.refs_7_
  91.9 3.1 %collective-permute-start.11 = (bf16[128,1152]{1,0:T(8,128)(2,1)}, bf16[128,1152]{1,0:T(8,128)(2,1)S(1)}, u32[]{:S(2)}, u32[]{:S(2)}) collective-permute-start(bf16[128,1152]{1,0:T(8,128)(2,1)} %get-tuple-element.76.refs_3_.refs_9_), channel_id=1, source_target_pairs={{0,16},{4,20},{8,24},{12,28},{16,0},{20,4},{24,8},{28,12},{1,17},{... | collective-permute-start | bytes 884744 | tf_op jit(solution)/shard_map/ppermute | solution.py:445
  95.0 0.8 collective-permute-start.12
  95.9 12.3 %collective-permute-done.11.refs_4_.refs_10_ = bf16[128,1152]{1,0:T(8,128)(2,1)S(1)} collective-permute-done((bf16[128,1152]{1,0:T(8,128)(2,1)}, bf16[128,1152]{1,0:T(8,128)(2,1)S(1)}, u32[]{:S(2)}, u32[]{:S(2)}) %collective-permute-start.11) | collective-permute-done | bytes 294944 | tf_op jit(solution)/shard_map/ppermute | solution.py:445
  108.1 1.0 collective-permute-done.12.refs_8_
  109.2 8.2 %shard_map.143 = (bf16[1040,512]{1,0:T(8,128)(2,1)}, bf16[1040,512]{1,0:T(8,128)(2,1)}, bf16[1040,512]{1,0:T(8,128)(2,1)}, bf16[1040,512]{1,0:T(8,128)(2,1)}) custom-call(s32[4]{0:T(128)} %pad_add_fusion.refs_0_.idx, bf16[2048,512]{1,0:T(8,128)(2,1)} %refs_1_.1, f32[4,1,256]{2,1,0:T(1,128)} %get-tuple-element.87.refs_10_.refs_5_.refs_2_, ...), custom_call_target="tpu_custom_call" | custom-call | flops 115000000 | tf_op jit(solution)/shard_map/pallas_call | solution.py:97
  119.0 2.0 %collective-permute-done.18 = bf16[1040,512]{1,0:T(8,128)(2,1)S(1)} collective-permute-done((bf16[1040,512]{1,0:T(8,128)(2,1)}, bf16[1040,512]{1,0:T(8,128)(2,1)S(1)}, u32[]{:S(2)}, u32[]{:S(2)}) %collective-permute-start.18) | collective-permute-done | bytes 1064992 | tf_op jit(solution)/shard_map/ppermute | solution.py:439
  121.0 2.6 %add_convert_fusion = bf16[1040,512]{1,0:T(8,128)(2,1)} fusion(bf16[1040,512]{1,0:T(8,128)(2,1)S(1)} %collective-permute-done.18, bf16[1040,512]{1,0:T(8,128)(2,1)} %get-tuple-element.95), kind=kLoop, calls=%fused_computation | loop fusion | flops 2129920 | bytes 3194880 | tf_op jit(solution)/shard_map/convert_element_type | solution.py:558
  123.6 1.0 collective-permute-start.19
  125.6 1.1 copy-done.12
  126.7 7.0 %shard_map.144 = (f32[512,256]{1,0:T(8,128)}, bf16[512,256]{1,0:T(8,128)(2,1)}, bf16[4,512,512]{2,1,0:T(8,128)(2,1)}, bf16[512,512]{1,0:T(8,128)(2,1)}) custom-call(s32[4]{0:T(128)} %pad_add_fusion.refs_0_.idx, bf16[1152,512]{1,0:T(8,128)(2,1)} %copy-done.7, bf16[1152,512]{1,0:T(8,128)(2,1)} %copy-done.11, bf16[1152,512]{1,0:T(8,128)(2,1)} %copy-done.10, ...), custom_call_target="tpu_custom_call" | custom-call | flops 5750000128 | tf_op jit(solution)/shard_map/pallas_call | solution.py:97
  133.7 1.6 collective-permute-start.26
  135.2 0.8 dynamic_slice.3
  136.5 0.8 copy-done.6
  137.3 4.9 %shard_map.145 = (f32[256,512]{1,0:T(8,128)}, f32[256,512]{1,0:T(8,128)}, bf16[2,256,512]{2,1,0:T(8,128)(2,1)}) custom-call(s32[4]{0:T(128)} %pad_add_fusion.refs_0_.idx, bf16[4,512,512]{2,1,0:T(8,128)(2,1)} %get-tuple-element.98.refs_1_, bf16[512,512]{1,0:T(8,128)(2,1)} %get-tuple-element.99.refs_2_, bf16[128,1152]{1,0:T(8,128)(2,1)} %get-tuple-element.76.refs_3_.refs_9_, ...), custom_call_target="tpu_custom_call" | custom-call | flops 115000000 | tf_op jit(solution)/shard_map/pallas_call | solution.py:97
  142.8 5.8 %shard_map.146 = (f32[256,512]{1,0:T(8,128)}, bf16[256,512]{1,0:T(8,128)(2,1)}) custom-call(s32[4]{0:T(128)} %pad_add_fusion.refs_0_.idx, bf16[1152,512]{1,0:T(8,128)(2,1)} %copy-done.7, bf16[1152,512]{1,0:T(8,128)(2,1)} %copy-done.11, bf16[1152,512]{1,0:T(8,128)(2,1)} %copy-done.10, bf16[1152,512]{1,0:T(8,128)(2,1)} %copy-done.12, ...), custom_call_target="tpu_custom_call" | custom-call | flops 115000000 | tf_op jit(solution)/shard_map/pallas_call | solution.py:97
  148.6 1.6 collective-permute-start.25
  150.1 0.8 convert_add_fusion.3
  151.0 1.5 convert_element_type.101
  153.9 0.8 multiply_multiply_fusion
  154.8 3.0 %fusion.5 = bf16[128,8,512]{2,1,0:T(8,128)(2,1)} fusion(f32[1040,512]{1,0:T(8,128)S(1)} %convert_element_type.101, bf16[128,8,512]{2,1,0:T(8,128)(2,1)S(1)} %copy-done.1, bf16[1040,512]{1,0:T(8,128)(2,1)} %collective-permute-done.17, bf16[1040,512]{1,0:T(8,128)(2,1)} %get-tuple-element.93, f32[128,512]{1,0:T(8,128)S(1)} %get-tuple-element.111, ...), kind=kLoop, calls=%fused_computation.7 | loop fusion | flops 6291456 | bytes 6564864 | tf_op jit(solution)/shard_map/convert_element_type | solution.py:609
  157.8 2.2 %convert_add_fusion = (f32[256,512]{1,0:T(8,128)}, f32[256,512]{1,0:T(8,128)}) fusion(f32[256,512]{1,0:T(8,128)S(1)} %copy-done.14, bf16[2,256,512]{2,1,0:T(8,128)(2,1)} %collective-permute-done.24, f32[256,512]{1,0:T(8,128)S(1)} %copy-done.15), kind=kLoop, calls=%fused_computation.9 | loop fusion | flops 524288 | bytes 2621440 | tf_op jit(solution)/shard_map/add | solution.py:596
  160.0 1.5 collective-permute-done.25
  161.6 1.8 %convert_add_fusion.2 = f32[256,512]{1,0:T(8,128)} fusion(f32[256,512]{1,0:T(8,128)S(1)} %copy-done.18, bf16[256,512]{1,0:T(8,128)(2,1)} %collective-permute-done.25), kind=kLoop, calls=%fused_computation.11 | loop fusion | flops 262144 | bytes 1310720 | tf_op jit(solution)/shard_map/add | solution.py:598
  (105 shorter events, 7.9 us)
Async XLA Ops:
  0.6 11.7 %copy-start = (bf16[128,8,512]{2,1,0:T(8,128)(2,1)S(1)}, bf16[128,8,512]{2,1,0:T(8,128)(2,1)}, u32[]{:S(2)}) copy-start(bf16[128,8,512]{2,1,0:T(8,128)(2,1)} %param.14) | copy-start | bytes 3145732
  0.6 26.8 %collective-permute-start.1 = (bf16[1024,512]{1,0:T(8,128)(2,1)}, bf16[1024,512]{1,0:T(8,128)(2,1)S(1)}, u32[]{:S(2)}, u32[]{:S(2)}) collective-permute-start(bf16[1024,512]{1,0:T(8,128)(2,1)} %bitcast.30), channel_id=1, source_target_pairs={{0,2},{1,3},{2,0},{3,1},{4,6},{5,7},{6,4},{7,5},{8,10},{9,11},{10,... | collective-permute-start | bytes 3145736 | tf_op jit(solution)/shard_map/ppermute | solution.py:439
  10.7 16.8 %copy-start.26 = (s32[128,8]{0,1:T(8,128)S(1)}, s32[128,8]{0,1:T(8,128)}, u32[]{:S(2)}) copy-start(s32[128,8]{0,1:T(8,128)} %param.13) | copy-start | bytes 12292
  10.7 13.7 %collective-permute-start.2 = (bf16[512,512]{1,0:T(8,128)(2,1)}, bf16[512,512]{1,0:T(8,128)(2,1)S(1)}, u32[]{:S(2)}, u32[]{:S(2)}) collective-permute-start(bf16[512,512]{1,0:T(8,128)(2,1)} %shard_map.138), channel_id=1, source_target_pairs={{0,4},{4,0},{8,12},{12,8},{16,20},{20,16},{24,28},{28,24},{1,5},{5... | collective-permute-start | bytes 1572872 | tf_op jit(solution)/shard_map/ppermute | solution.py:442
  12.3 20.2 %collective-permute-start = (bf16[1024,512]{1,0:T(8,128)(2,1)S(1)}, bf16[1024,512]{1,0:T(8,128)(2,1)S(1)}, u32[]{:S(2)}, u32[]{:S(2)}) collective-permute-start(bf16[1024,512]{1,0:T(8,128)(2,1)S(1)} %bitcast.33), channel_id=1, source_target_pairs={{0,1},{1,0},{2,3},{3,2},{4,5},{5,4},{6,7},{7,6},{8,9},{9,8},{10,11... | collective-permute-start | bytes 3145736 | tf_op jit(solution)/shard_map/ppermute | solution.py:439
  27.4 5.1 %copy-start.3 = (bf16[1024,512]{1,0:T(8,128)(2,1)}, bf16[1024,512]{1,0:T(8,128)(2,1)S(1)}, u32[]{:S(2)}) copy-start(bf16[1024,512]{1,0:T(8,128)(2,1)S(1)} %collective-permute-done.1.x2.refs_3_) | copy-start | bytes 3145732
  27.4 5.1 %collective-permute-start.3 = (bf16[1024,512]{1,0:T(8,128)(2,1)S(1)}, bf16[1024,512]{1,0:T(8,128)(2,1)}, u32[]{:S(2)}, u32[]{:S(2)}) collective-permute-start(bf16[1024,512]{1,0:T(8,128)(2,1)S(1)} %collective-permute-done.1.x2.refs_3_), channel_id=1, source_target_pairs={{0,1},{1,0},{2,3},{3,2},{4,5},{5,4},{6,7},{7,6},{8,9},{9,8},{10,11... | collective-permute-start | bytes 3145736 | tf_op jit(solution)/shard_map/ppermute | solution.py:439
  27.6 9.3 %collective-permute-start.4 = (bf16[128,512]{1,0:T(8,128)(2,1)}, bf16[128,512]{1,0:T(8,128)(2,1)S(1)}, u32[]{:S(2)}, u32[]{:S(2)}) collective-permute-start(bf16[128,512]{1,0:T(8,128)(2,1)} %get-tuple-element.59), channel_id=1, source_target_pairs={{0,8},{4,12},{8,0},{12,4},{16,24},{20,28},{24,16},{28,20},{1,9},{5... | collective-permute-start | bytes 393224 | tf_op jit(solution)/shard_map/ppermute | solution.py:445
  29.2 13.1 %collective-permute-start.5 = (bf16[128,512]{1,0:T(8,128)(2,1)}, bf16[128,512]{1,0:T(8,128)(2,1)S(1)}, u32[]{:S(2)}, u32[]{:S(2)}) collective-permute-start(bf16[128,512]{1,0:T(8,128)(2,1)} %get-tuple-element.60), channel_id=1, source_target_pairs={{0,16},{4,20},{8,24},{12,28},{16,0},{20,4},{24,8},{28,12},{1,17},{... | collective-permute-start | bytes 393224 | tf_op jit(solution)/shard_map/ppermute | solution.py:445
  31.8 10.5 %collective-permute-start.6 = (bf16[128,512]{1,0:T(8,128)(2,1)}, bf16[128,512]{1,0:T(8,128)(2,1)}, u32[]{:S(2)}, u32[]{:S(2)}) collective-permute-start(bf16[128,512]{1,0:T(8,128)(2,1)} %get-tuple-element.61), channel_id=1, source_target_pairs={{0,24},{4,28},{8,16},{12,20},{16,8},{20,12},{24,0},{28,4},{1,25},{... | collective-permute-start | bytes 393224 | tf_op jit(solution)/shard_map/ppermute | solution.py:445
  33.4 8.8 %copy-start.25 = (f32[128,512]{1,0:T(8,128)S(1)}, f32[128,512]{1,0:T(8,128)}, u32[]{:S(2)}) copy-start(f32[128,512]{1,0:T(8,128)} %get-tuple-element.63) | copy-start | bytes 786436
  43.3 23.5 %copy-start.9 = (bf16[128,512]{1,0:T(8,128)(2,1)}, bf16[128,512]{1,0:T(8,128)(2,1)S(1)}, u32[]{:S(2)}) copy-start(bf16[128,512]{1,0:T(8,128)(2,1)S(1)} %get-tuple-element.112.refs_6_) | copy-start | bytes 393220
  43.3 23.5 %collective-permute-start.16 = (bf16[128,512]{1,0:T(8,128)(2,1)S(1)}, bf16[128,512]{1,0:T(8,128)(2,1)S(1)}, u32[]{:S(2)}, u32[]{:S(2)}) collective-permute-start(bf16[128,512]{1,0:T(8,128)(2,1)S(1)} %get-tuple-element.112.refs_6_), channel_id=1, source_target_pairs={{0,0},{1,8},{2,16},{3,24},{4,4},{5,12},{6,20},{7,28},{8,1},{9,9},{... | collective-permute-start | bytes 393224 | tf_op jit(solution)/shard_map/ppermute | solution.py:517
  44.1 22.6 %collective-permute-start.7 = (bf16[128,512]{1,0:T(8,128)(2,1)S(1)}, bf16[128,512]{1,0:T(8,128)(2,1)S(1)}, u32[]{:S(2)}, u32[]{:S(2)}) collective-permute-start(bf16[128,512]{1,0:T(8,128)(2,1)S(1)} %get-tuple-element.112.refs_6_), channel_id=1, source_target_pairs={{0,1},{1,0},{2,3},{3,2},{4,5},{5,4},{6,7},{7,6},{8,9},{9,8},{10,11... | collective-permute-start | bytes 393224 | tf_op jit(solution)/shard_map/ppermute | solution.py:439
  48.3 24.0 %collective-permute-start.14 = (bf16[256,512]{1,0:T(8,128)(2,1)}, bf16[256,512]{1,0:T(8,128)(2,1)S(1)}, u32[]{:S(2)}, u32[]{:S(2)}) collective-permute-start(bf16[256,512]{1,0:T(8,128)(2,1)} %get-tuple-element.82), channel_id=1, source_target_pairs={{0,16},{4,20},{8,24},{12,28},{16,0},{20,4},{24,8},{28,12},{1,17},{... | collective-permute-start | bytes 786440 | tf_op jit(solution)/shard_map/ppermute | solution.py:445
  50.5 21.8 %collective-permute-start.13 = (bf16[256,512]{1,0:T(8,128)(2,1)}, bf16[256,512]{1,0:T(8,128)(2,1)S(1)}, u32[]{:S(2)}, u32[]{:S(2)}) collective-permute-start(bf16[256,512]{1,0:T(8,128)(2,1)} %get-tuple-element.80), channel_id=1, source_target_pairs={{0,8},{4,12},{8,0},{12,4},{16,24},{20,28},{24,16},{28,20},{1,9},{5... | collective-permute-start | bytes 786440 | tf_op jit(solution)/shard_map/ppermute | solution.py:445
  51.0 21.3 %collective-permute-start.15 = (bf16[256,512]{1,0:T(8,128)(2,1)}, bf16[256,512]{1,0:T(8,128)(2,1)S(1)}, u32[]{:S(2)}, u32[]{:S(2)}) collective-permute-start(bf16[256,512]{1,0:T(8,128)(2,1)} %get-tuple-element.84), channel_id=1, source_target_pairs={{0,24},{4,28},{8,16},{12,20},{16,8},{20,12},{24,0},{28,4},{1,25},{... | collective-permute-start | bytes 786440 | tf_op jit(solution)/shard_map/ppermute | solution.py:445
  53.3 13.4 %copy-start.24 = (bf16[256,512]{1,0:T(8,128)(2,1)S(1)}, bf16[256,512]{1,0:T(8,128)(2,1)}, u32[]{:S(2)}) copy-start(bf16[256,512]{1,0:T(8,128)(2,1)} %get-tuple-element.64) | copy-start | bytes 786436
  66.7 9.4 %copy-start.8 = (bf16[128,1152]{1,0:T(8,128)(2,1)S(1)}, bf16[128,1152]{1,0:T(8,128)(2,1)}, u32[]{:S(2)}) copy-start(bf16[128,1152]{1,0:T(8,128)(2,1)} %get-tuple-element.75.refs_9_.refs_5_) | copy-start | bytes 884740
  66.8 13.1 %copy-start.13 = (bf16[128,512]{1,0:T(8,128)(2,1)}, bf16[128,512]{1,0:T(8,128)(2,1)S(1)}, u32[]{:S(2)}) copy-start(bf16[128,512]{1,0:T(8,128)(2,1)S(1)} %collective-permute-done.7.refs_7_) | copy-start | bytes 393220
  66.8 9.3 %collective-permute-start.8 = (bf16[2,128,512]{2,1,0:T(8,128)(2,1)S(1)}, bf16[2,128,512]{2,1,0:T(8,128)(2,1)S(1)}, u32[]{:S(2)}, u32[]{:S(2)}) collective-permute-start(bf16[2,128,512]{2,1,0:T(8,128)(2,1)S(1)} %pad_maximum_fusion.1), channel_id=1, source_target_pairs={{0,2},{1,3},{2,0},{3,1},{4,6},{5,7},{6,4},{7,5},{8,10},{9,11},{10,... | collective-permute-start | bytes 786440 | tf_op jit(solution)/shard_map/ppermute | solution.py:439
  72.4 45.1 %copy-start.7 = (bf16[1152,512]{1,0:T(8,128)(2,1)}, bf16[1152,512]{1,0:T(8,128)(2,1)S(1)}, u32[]{:S(2)}) copy-start(bf16[1152,512]{1,0:T(8,128)(2,1)S(1)} %constant_dynamic-update-slice_fusion.refs_1_) | copy-start | bytes 3538948
  72.4 45.6 %collective-permute-start.21 = (bf16[1152,512]{1,0:T(8,128)(2,1)S(1)}, bf16[1152,512]{1,0:T(8,128)(2,1)S(1)}, u32[]{:S(2)}, u32[]{:S(2)}) collective-permute-start(bf16[1152,512]{1,0:T(8,128)(2,1)S(1)} %constant_dynamic-update-slice_fusion.refs_1_), channel_id=1, source_target_pairs={{0,2},{1,3},{2,0},{3,1},{4,6},{5,7},{6,4},{7,5},{8,10},{9,11},{10,... | collective-permute-start | bytes 3538952 | tf_op jit(solution)/shard_map/ppermute | solution.py:439
  76.1 3.8 %copy-start.23 = (bf16[2,128,512]{2,1,0:T(8,128)(2,1)}, bf16[2,128,512]{2,1,0:T(8,128)(2,1)S(1)}, u32[]{:S(2)}) copy-start(bf16[2,128,512]{2,1,0:T(8,128)(2,1)S(1)} %collective-permute-done.8.refs_8_) | copy-start | bytes 786436
  76.1 15.8 %collective-permute-start.10 = (bf16[128,1152]{1,0:T(8,128)(2,1)S(1)}, bf16[128,1152]{1,0:T(8,128)(2,1)S(1)}, u32[]{:S(2)}, u32[]{:S(2)}) collective-permute-start(bf16[128,1152]{1,0:T(8,128)(2,1)S(1)} %copy-done.8), channel_id=1, source_target_pairs={{0,16},{4,20},{8,24},{12,28},{16,0},{20,4},{24,8},{28,12},{1,17},{... | collective-permute-start | bytes 884744 | tf_op jit(solution)/shard_map/ppermute | solution.py:445
  79.9 12.1 %collective-permute-start.9 = (bf16[128,1152]{1,0:T(8,128)(2,1)S(1)}, bf16[128,1152]{1,0:T(8,128)(2,1)S(1)}, u32[]{:S(2)}, u32[]{:S(2)}) collective-permute-start(bf16[128,1152]{1,0:T(8,128)(2,1)S(1)} %copy-done.8), channel_id=1, source_target_pairs={{0,8},{4,12},{8,0},{12,4},{16,24},{20,28},{24,16},{28,20},{1,9},{5... | collective-permute-start | bytes 884744 | tf_op jit(solution)/shard_map/ppermute | solution.py:445
  91.9 25.5 %copy-start.20 = (bf16[128,1152]{1,0:T(8,128)(2,1)}, bf16[128,1152]{1,0:T(8,128)(2,1)S(1)}, u32[]{:S(2)}) copy-start(bf16[128,1152]{1,0:T(8,128)(2,1)S(1)} %collective-permute-done.10.refs_7_) | copy-start | bytes 884740
  91.9 25.5 %copy-start.21 = (bf16[128,1152]{1,0:T(8,128)(2,1)}, bf16[128,1152]{1,0:T(8,128)(2,1)S(1)}, u32[]{:S(2)}) copy-start(bf16[128,1152]{1,0:T(8,128)(2,1)S(1)} %collective-permute-done.9.refs_6_) | copy-start | bytes 884740
  91.9 16.2 %collective-permute-start.11 = (bf16[128,1152]{1,0:T(8,128)(2,1)}, bf16[128,1152]{1,0:T(8,128)(2,1)S(1)}, u32[]{:S(2)}, u32[]{:S(2)}) collective-permute-start(bf16[128,1152]{1,0:T(8,128)(2,1)} %get-tuple-element.76.refs_3_.refs_9_), channel_id=1, source_target_pairs={{0,16},{4,20},{8,24},{12,28},{16,0},{20,4},{24,8},{28,12},{1,17},{... | collective-permute-start | bytes 884744 | tf_op jit(solution)/shard_map/ppermute | solution.py:445
  95.0 14.1 %collective-permute-start.12 = (bf16[128,1152]{1,0:T(8,128)(2,1)S(1)}, bf16[128,1152]{1,0:T(8,128)(2,1)S(1)}, u32[]{:S(2)}, u32[]{:S(2)}) collective-permute-start(bf16[128,1152]{1,0:T(8,128)(2,1)S(1)} %collective-permute-done.10.refs_7_), channel_id=1, source_target_pairs={{0,8},{4,12},{8,0},{12,4},{16,24},{20,28},{24,16},{28,20},{1,9},{5... | collective-permute-start | bytes 884744 | tf_op jit(solution)/shard_map/ppermute | solution.py:445
  108.1 10.0 %copy-start.5 = (bf16[128,1152]{1,0:T(8,128)(2,1)}, bf16[128,1152]{1,0:T(8,128)(2,1)S(1)}, u32[]{:S(2)}) copy-start(bf16[128,1152]{1,0:T(8,128)(2,1)S(1)} %collective-permute-done.11.refs_4_.refs_10_) | copy-start | bytes 884740
  109.2 8.3 %copy-start.22 = (bf16[128,1152]{1,0:T(8,128)(2,1)}, bf16[128,1152]{1,0:T(8,128)(2,1)S(1)}, u32[]{:S(2)}) copy-start(bf16[128,1152]{1,0:T(8,128)(2,1)S(1)} %collective-permute-done.12.refs_8_) | copy-start | bytes 884740
  109.2 8.9 %copy-start.2 = (bf16[128,1152]{1,0:T(8,128)(2,1)S(1)}, bf16[128,1152]{1,0:T(8,128)(2,1)}, u32[]{:S(2)}) copy-start(bf16[128,1152]{1,0:T(8,128)(2,1)} %get-tuple-element.76.refs_3_.refs_9_) | copy-start | bytes 884740
  117.4 3.6 %collective-permute-start.18 = (bf16[1040,512]{1,0:T(8,128)(2,1)}, bf16[1040,512]{1,0:T(8,128)(2,1)S(1)}, u32[]{:S(2)}, u32[]{:S(2)}) collective-permute-start(bf16[1040,512]{1,0:T(8,128)(2,1)} %get-tuple-element.96), channel_id=1, source_target_pairs={{0,1},{1,0},{2,3},{3,2},{4,5},{5,4},{6,7},{7,6},{8,9},{9,8},{10,11... | collective-permute-start | bytes 3194888 | tf_op jit(solution)/shard_map/ppermute | solution.py:439
  117.5 7.1 %collective-permute-start.20 = (bf16[1152,512]{1,0:T(8,128)(2,1)S(1)}, bf16[1152,512]{1,0:T(8,128)(2,1)S(1)}, u32[]{:S(2)}, u32[]{:S(2)}) collective-permute-start(bf16[1152,512]{1,0:T(8,128)(2,1)S(1)} %constant_dynamic-update-slice_fusion.refs_1_), channel_id=1, source_target_pairs={{0,1},{1,0},{2,3},{3,2},{4,5},{5,4},{6,7},{7,6},{8,9},{9,8},{10,11... | collective-permute-start | bytes 3538952 | tf_op jit(solution)/shard_map/ppermute | solution.py:439
  118.0 5.6 %copy-start.10 = (bf16[1152,512]{1,0:T(8,128)(2,1)}, bf16[1152,512]{1,0:T(8,128)(2,1)S(1)}, u32[]{:S(2)}) copy-start(bf16[1152,512]{1,0:T(8,128)(2,1)S(1)} %collective-permute-done.21.refs_3_) | copy-start | bytes 3538948
  118.0 7.1 %collective-permute-start.22 = (bf16[1152,512]{1,0:T(8,128)(2,1)S(1)}, bf16[1152,512]{1,0:T(8,128)(2,1)S(1)}, u32[]{:S(2)}, u32[]{:S(2)}) collective-permute-start(bf16[1152,512]{1,0:T(8,128)(2,1)S(1)} %collective-permute-done.21.refs_3_), channel_id=1, source_target_pairs={{0,1},{1,0},{2,3},{3,2},{4,5},{5,4},{6,7},{7,6},{8,9},{9,8},{10,11... | collective-permute-start | bytes 3538952 | tf_op jit(solution)/shard_map/ppermute | solution.py:439
  118.2 18.3 %collective-permute-start.23 = (bf16[2,128,1152]{2,1,0:T(8,128)(2,1)S(1)}, bf16[2,128,1152]{2,1,0:T(8,128)(2,1)S(1)}, u32[]{:S(2)}, u32[]{:S(2)}) collective-permute-start(bf16[2,128,1152]{2,1,0:T(8,128)(2,1)S(1)} %pad_maximum_fusion), channel_id=1, source_target_pairs={{0,8},{4,12},{8,0},{12,4},{16,24},{20,28},{24,16},{28,20},{1,9},{5... | collective-permute-start | bytes 1769480 | tf_op jit(solution)/shard_map/ppermute | solution.py:445
  118.9 35.9 %collective-permute-start.17 = (bf16[1040,512]{1,0:T(8,128)(2,1)}, bf16[1040,512]{1,0:T(8,128)(2,1)}, u32[]{:S(2)}, u32[]{:S(2)}) collective-permute-start(bf16[1040,512]{1,0:T(8,128)(2,1)} %get-tuple-element.94), channel_id=1, source_target_pairs={{0,1},{1,0},{2,3},{3,2},{4,5},{5,4},{6,7},{7,6},{8,9},{9,8},{10,11... | collective-permute-start | bytes 3194888 | tf_op jit(solution)/shard_map/ppermute | solution.py:439
  123.6 12.5 %copy-start.16 = (f32[1024,1]{1,0:T(8,128)S(1)}, f32[1024,1]{1,0:T(8,128)}, u32[]{:S(2)}) copy-start(f32[1024,1]{1,0:T(8,128)} %get-tuple-element.69) | copy-start | bytes 12292
  123.6 27.3 %collective-permute-start.19 = (bf16[1040,512]{1,0:T(8,128)(2,1)}, bf16[1040,512]{1,0:T(8,128)(2,1)}, u32[]{:S(2)}, u32[]{:S(2)}) collective-permute-start(bf16[1040,512]{1,0:T(8,128)(2,1)} %add_convert_fusion), channel_id=1, source_target_pairs={{0,2},{1,3},{2,0},{3,1},{4,6},{5,7},{6,4},{7,5},{8,10},{9,11},{10,... | collective-permute-start | bytes 3194888 | tf_op jit(solution)/shard_map/ppermute | solution.py:439
  133.7 16.5 %collective-permute-start.26 = (bf16[512,256]{1,0:T(8,128)(2,1)}, bf16[512,256]{1,0:T(8,128)(2,1)S(1)}, u32[]{:S(2)}, u32[]{:S(2)}) collective-permute-start(bf16[512,256]{1,0:T(8,128)(2,1)} %get-tuple-element.109), channel_id=1, source_target_pairs={{0,4},{4,0},{8,12},{12,8},{16,20},{20,16},{24,28},{28,24},{1,5},{5... | collective-permute-start | bytes 786440 | tf_op jit(solution)/shard_map/ppermute | solution.py:442
  142.2 8.0 %copy-start.17 = (f32[512,256]{1,0:T(8,128)S(1)}, f32[512,256]{1,0:T(8,128)}, u32[]{:S(2)}) copy-start(f32[512,256]{1,0:T(8,128)} %get-tuple-element.108) | copy-start | bytes 1572868
  142.2 15.6 %collective-permute-start.24 = (bf16[2,256,512]{2,1,0:T(8,128)(2,1)}, bf16[2,256,512]{2,1,0:T(8,128)(2,1)}, u32[]{:S(2)}, u32[]{:S(2)}) collective-permute-start(bf16[2,256,512]{2,1,0:T(8,128)(2,1)} %get-tuple-element.100), channel_id=1, source_target_pairs={{0,4},{4,0},{8,12},{12,8},{16,20},{20,16},{24,28},{28,24},{1,5},{5... | collective-permute-start | bytes 1572872 | tf_op jit(solution)/shard_map/ppermute | solution.py:442
  148.6 13.0 %collective-permute-start.25 = (bf16[256,512]{1,0:T(8,128)(2,1)}, bf16[256,512]{1,0:T(8,128)(2,1)}, u32[]{:S(2)}, u32[]{:S(2)}) collective-permute-start(bf16[256,512]{1,0:T(8,128)(2,1)} %get-tuple-element.102), channel_id=1, source_target_pairs={{0,4},{4,0},{8,12},{12,8},{16,20},{20,16},{24,28},{28,24},{1,5},{5... | collective-permute-start | bytes 786440 | tf_op jit(solution)/shard_map/ppermute | solution.py:442
  150.1 4.6 %copy-start.1 = (bf16[128,8,512]{2,1,0:T(8,128)(2,1)S(1)}, bf16[128,8,512]{2,1,0:T(8,128)(2,1)}, u32[]{:S(2)}) copy-start(bf16[128,8,512]{2,1,0:T(8,128)(2,1)} %param.14) | copy-start | bytes 3145732
  154.8 3.0 %copy-start.14 = (f32[256,512]{1,0:T(8,128)S(1)}, f32[256,512]{1,0:T(8,128)}, u32[]{:S(2)}) copy-start(f32[256,512]{1,0:T(8,128)} %get-tuple-element.107) | copy-start | bytes 1572868
  157.8 3.8 %copy-start.18 = (f32[256,512]{1,0:T(8,128)S(1)}, f32[256,512]{1,0:T(8,128)}, u32[]{:S(2)}) copy-start(f32[256,512]{1,0:T(8,128)} %get-tuple-element.106) | copy-start | bytes 1572868
  (6 other events, 7.7 us)
